TPU v7x, 32 devices: a whole 2x2x4 slice. The times are simulated.
32 devices in a mesh: lon: 8 (over z, y), lat: 4 (over x, core).
Axes of the slice: x: 2, y: 2, z: 4, core: 2. Of those that a mesh axis runs over, the one named last changes fastest.
Arguments:
- inverse: float32 [16, 8, 128, 128], P('lon', 'lat'), may hold values from -0.1 to 0.2
- vert_diag: float32 [16, 8, 128], P('lon', 'lat'), may hold values from 0.1 to 1
- vert_coup: float32 [16, 8, 128], P('lon', 'lat'), may hold values from 0.5 to 4
- face_east: float32 [16, 8, 128], P('lon', 'lat'), may hold values from 0.3 to 3
- face_north: float32 [16, 8, 128], P('lon', 'lat'), may hold values from 0.3 to 3
- land_mask: int32 [16, 8], P('lon', 'lat'), may hold values 0 or 1
- aggregate: int32 [16, 8], P('lon', 'lat'), may hold values from -1 to 31, as said below
Outputs:
- coarse: float32 [8, 4, 13, 128, 128], P('lon', 'lat')
Inputs may be any that keep to these rules, and one draw needn't show every extreme that they name: `aggregate`: each entry is -1 (the column belongs to no coarse column) or the index I * 4 + J of the coarse column (I, J) = (i // 2, j // 2) of its own 2 x 2 block; -1 may occur anywhere and is more frequent in the two fine latitudes nearest each end of the latitude range.
All inputs are finite; a program needn't handle non-finite values. No bound on the sum of `land_mask` on one device may be relied on, other than what follows from the above.
Results may differ from a plain program's by a relative error of at most 0.0002.
Values sent between devices are 32-bit elements; how exact they have to be, the bound alone decides.
No kernel may reach another device: no remote copies, remote signals or barrier semaphores. Data moves between devices by JAX's collectives and lax.ppermute only.
A program may use at most 64 MiB of HBM per device.

v0:
```python
import functools

import jax
import jax.numpy as jnp
from jax import lax
from jax.experimental import pallas as pl
from jax.experimental.pallas import tpu as pltpu
from jax.sharding import PartitionSpec as P

relax_weight = 0.6
stencil_offsets = [
    (-2, 0),
    (-1, -1),
    (-1, 0),
    (-1, 1),
    (0, -2),
    (0, -1),
    (0, 0),
    (0, 1),
    (0, 2),
    (1, -1),
    (1, 0),
    (1, 1),
    (2, 0),
]
DIAG, UP, DOWN, EAST, NORTH, OPEN, WEIGHT = range(7)
COEF_ROWS = 8


def pair_near(axis):
    count = lax.axis_size(axis)
    return [(i, i ^ 1) for i in range(count) if i ^ 1 < count]


def pair_far(axis, closed):
    count = lax.axis_size(axis)
    pairs = [(i, i - 1 if i % 2 == 0 else i + 1) for i in range(count)]
    if closed:
        return [(i, j % count) for i, j in pairs]
    return [(i, j) for i, j in pairs if 0 <= j < count]


def second(axis, outward):
    count = lax.axis_size(axis)
    return [(i, (i + (2 if (i % 2 == 0) == outward else -2)) % count) for i in range(count)]


def pack_kernel(inverse, vert_diag, vert_coup, face_east, face_north, land, aggregate, payload, coefs):
    levels = inverse.shape[-1]
    lane = lax.broadcasted_iota(jnp.int32, (1, levels), 1)
    live = [
        jnp.where(jnp.full((1, levels), aggregate[q // 2, q % 2]) >= 0, 1.0, 0.0) for q in range(4)
    ]
    count = live[0] + live[1] + live[2] + live[3]
    scale = jnp.sqrt(jnp.maximum(count, 1.0))
    for q in range(4):
        x, y = q // 2, q % 2
        payload[q * levels : (q + 1) * levels, :] = inverse[x, y]
        coupling = vert_coup[x, y : y + 1, :]
        up = jnp.where(lane < levels - 1, coupling, 0.0)
        down = jnp.where(lane > 0, pltpu.roll(coupling, 1, axis=1), 0.0)
        is_open = jnp.full((1, levels), land[x, y]).astype(jnp.float32)
        rows = [
            vert_diag[x, y : y + 1, :] + coupling + down,
            up,
            down,
            face_east[x, y : y + 1, :] * is_open,
            face_north[x, y : y + 1, :] * is_open,
            is_open,
            live[q] / scale,
            jnp.zeros((1, levels), jnp.float32),
        ]
        block = jnp.concatenate(rows, axis=0)
        base = 4 * levels + q * COEF_ROWS
        payload[base : base + COEF_ROWS, :] = block
        coefs[q * COEF_ROWS : (q + 1) * COEF_ROWS, :] = block


def parities():
    even_lon = lax.rem(lax.axis_index("lon"), 2) == 0
    even_lat = lax.rem(lax.axis_index("lat"), 2) == 0
    return even_lon, even_lat


def corner_kernel(lon_near, lon_far, lat_near, lat_far, to_near, to_far):
    even_lon, even_lat = parities()
    rows = lon_near.shape[0]
    levels = lon_near.shape[1]
    coef = slice(4 * levels, rows)
    west = lambda q: jnp.where(
        even_lon,
        lon_far[q * levels : (q + 1) * levels, :],
        lon_near[q * levels : (q + 1) * levels, :],
    )
    east = lambda q: jnp.where(
        even_lon,
        lon_near[q * levels : (q + 1) * levels, :],
        lon_far[q * levels : (q + 1) * levels, :],
    )
    west_low, west_high, east_low, east_high = west(2), west(3), east(0), east(1)
    west_coef = jnp.where(even_lon, lon_far[coef, :], lon_near[coef, :])
    east_coef = jnp.where(even_lon, lon_near[coef, :], lon_far[coef, :])
    size = rows - 4 * levels
    base = 2 * levels
    for out, low, other in ((to_near, jnp.logical_not(even_lat), lat_far), (to_far, even_lat, lat_near)):
        out[:levels, :] = jnp.where(low, west_low, west_high)
        out[levels:base, :] = jnp.where(low, east_low, east_high)
        out[base : base + size, :] = west_coef
        out[base + size : base + 2 * size, :] = east_coef
        out[base + 2 * size : base + 3 * size, :] = other[coef, :]


def split(values):
    high = values.astype(jnp.bfloat16)
    return high, (values - high.astype(jnp.float32)).astype(jnp.bfloat16)


def product(left, right):
    left_high, left_low = split(left)
    right_high, right_low = split(right)
    return jnp.dot(
        jnp.concatenate([left_high, left_high, left_low], axis=1),
        jnp.concatenate([right_high, right_low, right_high], axis=0),
        preferred_element_type=jnp.float32,
    )


def coarse_kernel(own, lon_near, lon_far, lat_near, lat_far, corner_near, corner_far, ring_near, ring_far, out):
    even_lon, even_lat = parities()
    levels = own.shape[1]
    size = 4 * COEF_ROWS
    full = 4 * levels
    half = 2 * levels
    sources = {
        (0, 0): (None, own, own, full),
        (1, 0): (even_lon, lon_near, lon_far, full),
        (-1, 0): (even_lon, lon_far, lon_near, full),
        (0, 1): (even_lat, lat_near, lat_far, full),
        (0, -1): (even_lat, lat_far, lat_near, full),
        (-1, 1): (even_lat, corner_near, corner_far, half),
        (-1, -1): (even_lat, corner_far, corner_near, half),
        (1, 1): (even_lat, corner_near, corner_far, half + size),
        (1, -1): (even_lat, corner_far, corner_near, half + size),
        (0, 2): (even_lat, corner_near, corner_far, half + 2 * size),
        (0, -2): (even_lat, corner_far, corner_near, half + 2 * size),
        (2, 0): (even_lon, ring_near, ring_far, 0),
        (-2, 0): (even_lon, ring_far, ring_near, 0),
    }

    def fetch(device, start, count):
        flag, first, other, _ = sources[device]
        if flag is None:
            return first[start : start + count, :]
        return jnp.where(flag, first[start : start + count, :], other[start : start + count, :])

    coefs = {}
    for device in sources:
        base = sources[device][3]
        coefs[device] = fetch(device, base, size)

    def coef(x, y, row):
        at = (2 * (x % 2) + y % 2) * COEF_ROWS + row
        return coefs[x // 2, y // 2][at : at + 1, :]

    @functools.cache
    def east(x, y):
        return coef(x, y, EAST) * coef(x + 1, y, OPEN)

    @functools.cache
    def north(x, y):
        return coef(x, y, NORTH) * coef(x, y + 1, OPEN)

    @functools.cache
    def main(x, y):
        return coef(x, y, DIAG) + east(x, y) + east(x - 1, y) + north(x, y) + north(x, y - 1)

    def lon_faces(x, y):
        right = east(x, y) * coef(x + 1, y, WEIGHT)
        left = east(x - 1, y) * coef(x - 1, y, WEIGHT)
        return (right, left) if x % 2 == 0 else (left, right)

    def lat_faces(x, y):
        above = north(x, y) * coef(x, y + 1, WEIGHT)
        below = north(x, y - 1) * coef(x, y - 1, WEIGHT)
        return (above, below) if y % 2 == 0 else (below, above)

    def inverse(x, y):
        device = (x // 2, y // 2)
        if device[0] != 0 and device[1] != 0:
            start = 0 if device[0] < 0 else levels
        else:
            start = (2 * (x % 2) + y % 2) * levels
        return fetch(device, start, levels)

    row = lax.broadcasted_iota(jnp.int32, (levels, levels), 0)
    lane = lax.broadcasted_iota(jnp.int32, (levels, levels), 1)

    def own_diag(x, y):
        return coef(x, y, WEIGHT) * main(x, y) - lon_faces(x, y)[0] - lat_faces(x, y)[0]

    def left(values):
        return pltpu.roll(values, 1, axis=1)

    def right(values):
        return pltpu.roll(values, levels - 1, axis=1)

    own_cells = [(x, y) for x in (0, 1) for y in (0, 1)]
    lon_cells = [(x, y) for x in (-1, 2) for y in (0, 1)]
    lat_cells = [(x, y) for x in (0, 1) for y in (-1, 2)]
    rows_t = {}
    for x, y in own_cells:
        block = inverse(x, y)
        weight = coef(x, y, WEIGHT)
        smoothed = (
            block * own_diag(x, y)
            - left(block * (weight * coef(x, y, UP)))
            - right(block * (weight * coef(x, y, DOWN)))
        )
        rows_t[x, y] = (jnp.where(row == lane, weight, 0.0) - relax_weight * smoothed).T
    for x, y in lon_cells:
        rows_t[x, y] = (inverse(x, y) * (relax_weight * lon_faces(x, y)[1])).T
    for x, y in lat_cells:
        rows_t[x, y] = (inverse(x, y) * (relax_weight * lat_faces(x, y)[1])).T

    def residual(x, y):
        total = None
        if (x, y) in rows_t:
            block = rows_t[x, y]
            total = block * main(x, y) - left(block * coef(x, y, UP)) - right(block * coef(x, y, DOWN))
        for near, face in (
            ((x + 1, y), east(x, y)),
            ((x - 1, y), east(x - 1, y)),
            ((x, y + 1), north(x, y)),
            ((x, y - 1), north(x, y - 1)),
        ):
            if near in rows_t:
                term = rows_t[near] * face
                total = -term if total is None else total - term
        return total

    slot_of = {offset: place for place, offset in enumerate(stencil_offsets)}
    started = set()

    def add(target, term):
        place = slot_of[target]
        if target in started:
            out[place] += term
        else:
            out[place] = term
            started.add(target)

    groups = [
        ((0, 0), own_cells),
        ((0, 1), [(x, y) for x in (0, 1) for y in (2, 3)]),
        ((0, -1), [(x, y) for x in (0, 1) for y in (-1, -2)]),
        ((1, 0), [(x, y) for x in (2, 3) for y in (0, 1)]),
        ((-1, 0), [(x, y) for x in (-1, -2) for y in (0, 1)]),
        ((1, 1), [(2, 2)]),
        ((1, -1), [(2, -1)]),
        ((-1, 1), [(-1, 2)]),
        ((-1, -1), [(-1, -1)]),
    ]
    for device, cells in groups:
        straight = down = up = None
        for x, y in cells:
            rest = residual(x, y)
            weight = coef(x, y, WEIGHT)
            smooth = product(rest, inverse(x, y)) * relax_weight
            terms = (
                rest * weight - smooth * own_diag(x, y),
                smooth * (weight * coef(x, y, UP)),
                smooth * (weight * coef(x, y, DOWN)),
            )
            if straight is None:
                straight, up, down = terms
            else:
                straight, up, down = straight + terms[0], up + terms[1], down + terms[2]
            lon_target = (device[0] + (-1 if x % 2 == 0 else 1), device[1])
            lat_target = (device[0], device[1] + (-1 if y % 2 == 0 else 1))
            add(lon_target, smooth * lon_faces(x, y)[1])
            add(lat_target, smooth * lat_faces(x, y)[1])
        add(device, straight + left(up) + right(down))


def local(inverse, vert_diag, vert_coup, face_east, face_north, land_mask, aggregate):
    levels = inverse.shape[-1]
    rows = 4 * (levels + COEF_ROWS)
    vmem = pl.BlockSpec(memory_space=pltpu.VMEM)
    smem = pl.BlockSpec(memory_space=pltpu.SMEM)
    array = lambda count: jax.ShapeDtypeStruct((count, levels), jnp.float32)
    payload, coefs = pl.pallas_call(
        pack_kernel,
        out_shape=(array(rows), array(4 * COEF_ROWS)),
        in_specs=[vmem] * 5 + [smem] * 2,
        out_specs=(vmem, vmem),
    )(inverse, vert_diag, vert_coup, face_east, face_north, land_mask, aggregate)
    lon_near = lax.ppermute(payload, "lon", pair_near("lon"))
    lon_far = lax.ppermute(payload, "lon", pair_far("lon", True))
    lat_near = lax.ppermute(payload, "lat", pair_near("lat"))
    lat_far = lax.ppermute(payload, "lat", pair_far("lat", False))
    ring_near = lax.ppermute(coefs, "lon", second("lon", False))
    ring_far = lax.ppermute(coefs, "lon", second("lon", True))
    corner_rows = 2 * levels + 3 * 4 * COEF_ROWS
    to_near, to_far = pl.pallas_call(
        corner_kernel,
        out_shape=(array(corner_rows), array(corner_rows)),
        in_specs=[vmem] * 4,
        out_specs=(vmem, vmem),
    )(lon_near, lon_far, lat_near, lat_far)
    corner_near = lax.ppermute(to_near, "lat", pair_near("lat"))
    corner_far = lax.ppermute(to_far, "lat", pair_far("lat", False))
    out = pl.pallas_call(
        coarse_kernel,
        out_shape=jax.ShapeDtypeStruct((len(stencil_offsets), levels, levels), jnp.float32),
        in_specs=[vmem] * 9,
        out_specs=vmem,
        compiler_params=pltpu.CompilerParams(vmem_limit_bytes=32 * 1024 * 1024),
    )(payload, lon_near, lon_far, lat_near, lat_far, corner_near, corner_far, ring_near, ring_far)
    return out[None, None]


def solution(mesh):
    return jax.shard_map(
        local,
        mesh=mesh,
        in_specs=(
            P("lon", "lat", None, None),
            P("lon", "lat", None),
            P("lon", "lat", None),
            P("lon", "lat", None),
            P("lon", "lat", None),
            P("lon", "lat"),
            P("lon", "lat"),
        ),
        out_specs=P("lon", "lat", None, None, None),
        check_vma=False,
    )
```

profile of v0, /device:TPU:6, one launch (start us, length us, event | category | flops | bytes accessed | tf_op | source)
XLA Modules:
  0.0 41.9 jit_solution(1748029803417357111)
XLA Ops:
  0.0 1.8 %shard_map.73 = (f32[544,128]{1,0:T(8,128)}, f32[32,128]{1,0:T(8,128)}) custom-call(f32[2,2,128,128]{3,2,1,0:T(8,128)} %inverse.1, f32[2,2,128]{2,1,0:T(2,128)} %vert_diag.1, f32[2,2,128]{2,1,0:T(2,128)} %vert_coup.1, f32[2,2,128]{2,1,0:T(2,128)} %face_east.1, f32[2,2,128]{2,1,0:T(2,128)} %face_north.1, s32[2,2]{1,0:T(2,128)} %land.1, s32[2,2]{1,0:T(2,128)} %aggregate.1), custom_call_target="tpu_custom_call" | custom-call | tf_op jit(solution)/shard_map/pallas_call | solution.py:291
  1.8 0.0 copy-start.9
  1.8 0.0 copy-start.8
  1.8 2.1 %collective-permute-start.3 = (f32[544,128]{1,0:T(8,128)}, f32[544,128]{1,0:T(8,128)S(1)}, u32[]{:S(2)}, u32[]{:S(2)}) collective-permute-start(f32[544,128]{1,0:T(8,128)} %get-tuple-element.9.own), channel_id=1, source_target_pairs={{1,2},{2,1},{5,6},{6,5},{9,10},{10,9},{13,14},{14,13},{17,18},{18,... | collective-permute-start | bytes 835592 | tf_op jit(solution)/shard_map/ppermute | solution.py:300
  3.9 0.1 collective-permute-start.2
  3.9 1.6 %collective-permute-start.1 = (f32[544,128]{1,0:T(8,128)}, f32[544,128]{1,0:T(8,128)S(1)}, u32[]{:S(2)}, u32[]{:S(2)}) collective-permute-start(f32[544,128]{1,0:T(8,128)} %get-tuple-element.9.own), channel_id=1, source_target_pairs={{0,28},{4,8},{8,4},{12,16},{16,12},{20,24},{24,20},{28,0},{1,29},{... | collective-permute-start | bytes 835592 | tf_op jit(solution)/shard_map/ppermute | solution.py:298
  5.5 3.5 %collective-permute-start = (f32[544,128]{1,0:T(8,128)}, f32[544,128]{1,0:T(8,128)S(1)}, u32[]{:S(2)}, u32[]{:S(2)}) collective-permute-start(f32[544,128]{1,0:T(8,128)} %get-tuple-element.9.own), channel_id=1, source_target_pairs={{0,4},{4,0},{8,12},{12,8},{16,20},{20,16},{24,28},{28,24},{1,5},{5... | collective-permute-start | bytes 835592 | tf_op jit(solution)/shard_map/ppermute | solution.py:297
  9.1 0.9 %collective-permute-done.3.lat_far = f32[544,128]{1,0:T(8,128)S(1)} collective-permute-done((f32[544,128]{1,0:T(8,128)}, f32[544,128]{1,0:T(8,128)S(1)}, u32[]{:S(2)}, u32[]{:S(2)}) %collective-permute-start.3) | collective-permute-done | bytes 278560 | tf_op jit(solution)/shard_map/ppermute | solution.py:300
  10.0 0.0 collective-permute-done.2.lat_near
  10.0 4.2 %collective-permute-done.1.lon_far = f32[544,128]{1,0:T(8,128)S(1)} collective-permute-done((f32[544,128]{1,0:T(8,128)}, f32[544,128]{1,0:T(8,128)S(1)}, u32[]{:S(2)}, u32[]{:S(2)}) %collective-permute-start.1) | collective-permute-done | bytes 278560 | tf_op jit(solution)/shard_map/ppermute | solution.py:298
  14.2 5.9 %collective-permute-done.lon_near = f32[544,128]{1,0:T(8,128)S(1)} collective-permute-done((f32[544,128]{1,0:T(8,128)}, f32[544,128]{1,0:T(8,128)S(1)}, u32[]{:S(2)}, u32[]{:S(2)}) %collective-permute-start) | collective-permute-done | bytes 278560 | tf_op jit(solution)/shard_map/ppermute | solution.py:297
  20.1 0.0 copy-done
  20.1 0.0 copy-done.2
  20.1 0.0 copy-done.4
  20.1 0.7 %copy-done.6 = f32[544,128]{1,0:T(8,128)} copy-done((f32[544,128]{1,0:T(8,128)}, f32[544,128]{1,0:T(8,128)S(1)}, u32[]{:S(2)}) %copy-start.6) | copy-done | bytes 278552
  20.8 2.0 %shard_map.74 = (f32[352,128]{1,0:T(8,128)}, f32[352,128]{1,0:T(8,128)}) custom-call(f32[544,128]{1,0:T(8,128)} %copy-done.6, f32[544,128]{1,0:T(8,128)} %copy-done.4, f32[544,128]{1,0:T(8,128)} %copy-done.2, f32[544,128]{1,0:T(8,128)} %copy-done), custom_call_target="tpu_custom_call" | custom-call | tf_op jit(solution)/shard_map/pallas_call | solution.py:304
  22.8 0.0 collective-permute-start.4
  22.9 3.7 %collective-permute-start.5 = (f32[352,128]{1,0:T(8,128)}, f32[352,128]{1,0:T(8,128)S(1)}, u32[]{:S(2)}, u32[]{:S(2)}) collective-permute-start(f32[352,128]{1,0:T(8,128)} %get-tuple-element.11), channel_id=1, source_target_pairs={{1,2},{2,1},{5,6},{6,5},{9,10},{10,9},{13,14},{14,13},{17,18},{18,... | collective-permute-start | bytes 540680 | tf_op jit(solution)/shard_map/ppermute | solution.py:311
  26.5 0.0 copy-done.9
  26.6 2.8 %collective-permute-start.7 = (f32[32,128]{1,0:T(8,128)S(1)}, f32[32,128]{1,0:T(8,128)S(1)}, u32[]{:S(2)}, u32[]{:S(2)}) collective-permute-start(f32[32,128]{1,0:T(8,128)S(1)} %copy-done.9), channel_id=1, source_target_pairs={{0,8},{4,28},{8,16},{12,4},{16,24},{20,12},{24,0},{28,20},{1,9},{5... | collective-permute-start | bytes 49160 | tf_op jit(solution)/shard_map/ppermute | solution.py:302
  29.3 0.0 collective-permute-start.6
  29.3 1.4 %collective-permute-done.7.ring_far = f32[32,128]{1,0:T(8,128)S(1)} collective-permute-done((f32[32,128]{1,0:T(8,128)S(1)}, f32[32,128]{1,0:T(8,128)S(1)}, u32[]{:S(2)}, u32[]{:S(2)}) %collective-permute-start.7) | collective-permute-done | bytes 16416 | tf_op jit(solution)/shard_map/ppermute | solution.py:302
  30.8 4.1 %collective-permute-done.6.ring_near = f32[32,128]{1,0:T(8,128)S(1)} collective-permute-done((f32[32,128]{1,0:T(8,128)S(1)}, f32[32,128]{1,0:T(8,128)S(1)}, u32[]{:S(2)}, u32[]{:S(2)}) %collective-permute-start.6) | collective-permute-done | bytes 16416 | tf_op jit(solution)/shard_map/ppermute | solution.py:301
  34.9 0.0 collective-permute-done.4.corner_near
  34.9 0.0 collective-permute-done.5.corner_far
  34.9 0.0 copy-done.8
  34.9 0.0 copy-start.1
  34.9 0.9 %copy-done.1 = f32[544,128]{1,0:T(8,128)S(1)} copy-done((f32[544,128]{1,0:T(8,128)S(1)}, f32[544,128]{1,0:T(8,128)}, u32[]{:S(2)}) %copy-start.1) | copy-done | bytes 278552
  35.8 1.0 %copy-done.3 = f32[544,128]{1,0:T(8,128)S(1)} copy-done((f32[544,128]{1,0:T(8,128)S(1)}, f32[544,128]{1,0:T(8,128)}, u32[]{:S(2)}) %copy-start.3) | copy-done | bytes 278552
  36.8 1.0 %copy-done.5 = f32[544,128]{1,0:T(8,128)S(1)} copy-done((f32[544,128]{1,0:T(8,128)S(1)}, f32[544,128]{1,0:T(8,128)}, u32[]{:S(2)}) %copy-start.5) | copy-done | bytes 278552
  37.8 1.0 %copy-done.7 = f32[544,128]{1,0:T(8,128)S(1)} copy-done((f32[544,128]{1,0:T(8,128)S(1)}, f32[544,128]{1,0:T(8,128)}, u32[]{:S(2)}) %copy-start.7) | copy-done | bytes 278552
  38.7 3.2 %shard_map.75 = f32[13,128,128]{2,1,0:T(8,128)} custom-call(f32[544,128]{1,0:T(8,128)S(1)} %copy-done.8, f32[544,128]{1,0:T(8,128)S(1)} %copy-done.7, f32[544,128]{1,0:T(8,128)S(1)} %copy-done.5, f32[544,128]{1,0:T(8,128)S(1)} %copy-done.3, f32[544,128]{1,0:T(8,128)S(1)} %copy-done.1, f32[352,128]{1,0:T(8,128)S(1)} %collective-permute-done.4.corner_near, ...), custom_call_target="tpu_custom_call" | custom-call | tf_op jit(solution)/shard_map/pallas_call | solution.py:312
  (7 shorter events, 0.0 us)
Async XLA Ops:
  1.8 24.8 %copy-start.9 = (f32[32,128]{1,0:T(8,128)S(1)}, f32[32,128]{1,0:T(8,128)}, u32[]{:S(2)}) copy-start(f32[32,128]{1,0:T(8,128)} %get-tuple-element.12) | copy-start | bytes 49156
  1.8 33.1 %copy-start.8 = (f32[544,128]{1,0:T(8,128)S(1)}, f32[544,128]{1,0:T(8,128)}, u32[]{:S(2)}) copy-start(f32[544,128]{1,0:T(8,128)} %get-tuple-element.9.own) | copy-start | bytes 835588
  1.8 8.2 %collective-permute-start.3 = (f32[544,128]{1,0:T(8,128)}, f32[544,128]{1,0:T(8,128)S(1)}, u32[]{:S(2)}, u32[]{:S(2)}) collective-permute-start(f32[544,128]{1,0:T(8,128)} %get-tuple-element.9.own), channel_id=1, source_target_pairs={{1,2},{2,1},{5,6},{6,5},{9,10},{10,9},{13,14},{14,13},{17,18},{18,... | collective-permute-start | bytes 835592 | tf_op jit(solution)/shard_map/ppermute | solution.py:300
  3.9 6.2 %collective-permute-start.2 = (f32[544,128]{1,0:T(8,128)}, f32[544,128]{1,0:T(8,128)S(1)}, u32[]{:S(2)}, u32[]{:S(2)}) collective-permute-start(f32[544,128]{1,0:T(8,128)} %get-tuple-element.9.own), channel_id=1, source_target_pairs={{0,1},{1,0},{2,3},{3,2},{4,5},{5,4},{6,7},{7,6},{8,9},{9,8},{10,11... | collective-permute-start | bytes 835592 | tf_op jit(solution)/shard_map/ppermute | solution.py:299
  3.9 10.3 %collective-permute-start.1 = (f32[544,128]{1,0:T(8,128)}, f32[544,128]{1,0:T(8,128)S(1)}, u32[]{:S(2)}, u32[]{:S(2)}) collective-permute-start(f32[544,128]{1,0:T(8,128)} %get-tuple-element.9.own), channel_id=1, source_target_pairs={{0,28},{4,8},{8,4},{12,16},{16,12},{20,24},{24,20},{28,0},{1,29},{... | collective-permute-start | bytes 835592 | tf_op jit(solution)/shard_map/ppermute | solution.py:298
  5.5 14.6 %collective-permute-start = (f32[544,128]{1,0:T(8,128)}, f32[544,128]{1,0:T(8,128)S(1)}, u32[]{:S(2)}, u32[]{:S(2)}) collective-permute-start(f32[544,128]{1,0:T(8,128)} %get-tuple-element.9.own), channel_id=1, source_target_pairs={{0,4},{4,0},{8,12},{12,8},{16,20},{20,16},{24,28},{28,24},{1,5},{5... | collective-permute-start | bytes 835592 | tf_op jit(solution)/shard_map/ppermute | solution.py:297
  10.0 10.1 %copy-start = (f32[544,128]{1,0:T(8,128)}, f32[544,128]{1,0:T(8,128)S(1)}, u32[]{:S(2)}) copy-start(f32[544,128]{1,0:T(8,128)S(1)} %collective-permute-done.3.lat_far) | copy-start | bytes 835588
  10.0 10.1 %copy-start.2 = (f32[544,128]{1,0:T(8,128)}, f32[544,128]{1,0:T(8,128)S(1)}, u32[]{:S(2)}) copy-start(f32[544,128]{1,0:T(8,128)S(1)} %collective-permute-done.2.lat_near) | copy-start | bytes 835588
  14.2 5.9 %copy-start.4 = (f32[544,128]{1,0:T(8,128)}, f32[544,128]{1,0:T(8,128)S(1)}, u32[]{:S(2)}) copy-start(f32[544,128]{1,0:T(8,128)S(1)} %collective-permute-done.1.lon_far) | copy-start | bytes 835588
  20.1 0.7 %copy-start.6 = (f32[544,128]{1,0:T(8,128)}, f32[544,128]{1,0:T(8,128)S(1)}, u32[]{:S(2)}) copy-start(f32[544,128]{1,0:T(8,128)S(1)} %collective-permute-done.lon_near) | copy-start | bytes 835588
  22.8 12.1 %collective-permute-start.4 = (f32[352,128]{1,0:T(8,128)}, f32[352,128]{1,0:T(8,128)S(1)}, u32[]{:S(2)}, u32[]{:S(2)}) collective-permute-start(f32[352,128]{1,0:T(8,128)} %get-tuple-element.10), channel_id=1, source_target_pairs={{0,1},{1,0},{2,3},{3,2},{4,5},{5,4},{6,7},{7,6},{8,9},{9,8},{10,11... | collective-permute-start | bytes 540680 | tf_op jit(solution)/shard_map/ppermute | solution.py:310
  22.9 12.0 %collective-permute-start.5 = (f32[352,128]{1,0:T(8,128)}, f32[352,128]{1,0:T(8,128)S(1)}, u32[]{:S(2)}, u32[]{:S(2)}) collective-permute-start(f32[352,128]{1,0:T(8,128)} %get-tuple-element.11), channel_id=1, source_target_pairs={{1,2},{2,1},{5,6},{6,5},{9,10},{10,9},{13,14},{14,13},{17,18},{18,... | collective-permute-start | bytes 540680 | tf_op jit(solution)/shard_map/ppermute | solution.py:311
  26.6 4.2 %collective-permute-start.7 = (f32[32,128]{1,0:T(8,128)S(1)}, f32[32,128]{1,0:T(8,128)S(1)}, u32[]{:S(2)}, u32[]{:S(2)}) collective-permute-start(f32[32,128]{1,0:T(8,128)S(1)} %copy-done.9), channel_id=1, source_target_pairs={{0,8},{4,28},{8,16},{12,4},{16,24},{20,12},{24,0},{28,20},{1,9},{5... | collective-permute-start | bytes 49160 | tf_op jit(solution)/shard_map/ppermute | solution.py:302
  29.3 5.5 %collective-permute-start.6 = (f32[32,128]{1,0:T(8,128)S(1)}, f32[32,128]{1,0:T(8,128)S(1)}, u32[]{:S(2)}, u32[]{:S(2)}) collective-permute-start(f32[32,128]{1,0:T(8,128)S(1)} %copy-done.9), channel_id=1, source_target_pairs={{0,24},{4,12},{8,0},{12,20},{16,8},{20,28},{24,16},{28,4},{1,25},{... | collective-permute-start | bytes 49160 | tf_op jit(solution)/shard_map/ppermute | solution.py:301
  34.9 1.0 %copy-start.1 = (f32[544,128]{1,0:T(8,128)S(1)}, f32[544,128]{1,0:T(8,128)}, u32[]{:S(2)}) copy-start(f32[544,128]{1,0:T(8,128)} %copy-done) | copy-start | bytes 835588
  35.8 1.0 %copy-start.3 = (f32[544,128]{1,0:T(8,128)S(1)}, f32[544,128]{1,0:T(8,128)}, u32[]{:S(2)}) copy-start(f32[544,128]{1,0:T(8,128)} %copy-done.2) | copy-start | bytes 835588
  36.8 1.0 %copy-start.5 = (f32[544,128]{1,0:T(8,128)S(1)}, f32[544,128]{1,0:T(8,128)}, u32[]{:S(2)}) copy-start(f32[544,128]{1,0:T(8,128)} %copy-done.4) | copy-start | bytes 835588
  37.8 1.0 %copy-start.7 = (f32[544,128]{1,0:T(8,128)S(1)}, f32[544,128]{1,0:T(8,128)}, u32[]{:S(2)}) copy-start(f32[544,128]{1,0:T(8,128)} %copy-done.6) | copy-start | bytes 835588
where the time goes:
time: 42.2 us; the launch traced here: 41.9 us
  waiting for transfers between devices  16.6 us (39%)
  starting transfers between devices  13.7 us (32%)
  Pallas kernels  6.99 us (17%)
  local copies, waits for them, and re-layouts  4.54 us (11%)
    ppermute x1, waiting for transfers between devices, local(): lon_near = lax.ppermute(payload, 'lon', pair_near('lon'))  5.89 us
    unnamed x20, local copies, waits for them, and re-layouts  4.54 us
    ppermute x1, waiting for transfers between devices, local(): lon_far = lax.ppermute(payload, 'lon', pair_far('lon', True))  4.21 us
    ppermute x1, waiting for transfers between devices, local(): ring_near = lax.ppermute(coefs, 'lon', second('lon', False))  4.09 us
    ppermute x1, starting transfers between devices, local(): corner_far = lax.ppermute(to_far, 'lat', pair_far('lat', False))  3.67 us
    ppermute x1, starting transfers between devices, local(): lon_near = lax.ppermute(payload, 'lon', pair_near('lon'))  3.54 us
    pallas_call x1, Pallas kernels, local(): pl.pallas_call(coarse_kernel, out_shape=jax.ShapeDtypeStruct((len(stencil...  3.21 us
    ppermute x1, starting transfers between devices, local(): ring_far = lax.ppermute(coefs, 'lon', second('lon', True))  2.79 us
  transfers between devices with their start and end apart: 8, of which 5 were waited for; matrix products, arithmetic and copies ran while one was open for 0% of the time, Pallas kernels for 0%

commit v1 on v0

v1 whole, which is shorter than its diff:
```python
import functools

import jax
import jax.numpy as jnp
from jax import lax
from jax.experimental import pallas as pl
from jax.experimental.pallas import tpu as pltpu
from jax.sharding import PartitionSpec as P

relax_weight = 0.6
stencil_offsets = [
    (-2, 0),
    (-1, -1),
    (-1, 0),
    (-1, 1),
    (0, -2),
    (0, -1),
    (0, 0),
    (0, 1),
    (0, 2),
    (1, -1),
    (1, 0),
    (1, 1),
    (2, 0),
]
DIAG, UP, DOWN, EAST, NORTH, OPEN, WEIGHT = range(7)
COEF_ROWS = 8


def pair_near(axis):
    count = lax.axis_size(axis)
    return [(i, i ^ 1) for i in range(count) if i ^ 1 < count]


def pair_far(axis, closed):
    count = lax.axis_size(axis)
    pairs = [(i, i - 1 if i % 2 == 0 else i + 1) for i in range(count)]
    if closed:
        return [(i, j % count) for i, j in pairs]
    return [(i, j) for i, j in pairs if 0 <= j < count]


def second(axis, outward):
    count = lax.axis_size(axis)
    return [(i, (i + (2 if (i % 2 == 0) == outward else -2)) % count) for i in range(count)]


def pack_kernel(
    inverse_hbm,
    diag_hbm,
    coup_hbm,
    east_hbm,
    north_hbm,
    land_hbm,
    aggregate_hbm,
    both,
    to_near,
    to_far,
    inverse,
    vert_diag,
    vert_coup,
    face_east,
    face_north,
    land,
    aggregate,
    block,
    small_sems,
    sems,
):
    lon = lax.rem(lax.axis_index("lon"), 2)
    levels = inverse.shape[-1]
    whole = pltpu.make_async_copy(inverse_hbm, inverse, small_sems.at[6])
    whole.start()
    small = [
        pltpu.make_async_copy(source, target, small_sems.at[place])
        for place, (source, target) in enumerate(
            (
                (land_hbm, land),
                (aggregate_hbm, aggregate),
                (coup_hbm, vert_coup),
                (diag_hbm, vert_diag),
                (east_hbm, face_east),
                (north_hbm, face_north),
            )
        )
    ]
    for copy in small:
        copy.start()
    copies = []
    for y in range(2):
        rows = pl.ds(y * levels, levels)
        copies.append((inverse.at[1 - lon, y], to_near.at[rows]))
        copies.append((inverse.at[lon, y], to_far.at[rows]))
        for x in range(2):
            copies.append((inverse.at[x, y], both.at[pl.ds((2 * x + y) * levels, levels)]))
    copies = [
        pltpu.make_async_copy(source, target, sems.at[place])
        for place, (source, target) in enumerate(copies)
    ]
    whole.wait()
    for copy in copies:
        copy.start()
    for copy in small:
        copy.wait()
    lane = lax.broadcasted_iota(jnp.int32, (1, levels), 1)
    live = [
        jnp.where(jnp.full((1, levels), aggregate[q // 2, q % 2]) >= 0, 1.0, 0.0) for q in range(4)
    ]
    count = live[0] + live[1] + live[2] + live[3]
    scale = jnp.sqrt(jnp.maximum(count, 1.0))
    for q in range(4):
        x, y = q // 2, q % 2
        coupling = vert_coup[x, y : y + 1, :]
        up = jnp.where(lane < levels - 1, coupling, 0.0)
        down = jnp.where(lane > 0, pltpu.roll(coupling, 1, axis=1), 0.0)
        is_open = jnp.full((1, levels), land[x, y]).astype(jnp.float32)
        rows = [
            vert_diag[x, y : y + 1, :] + coupling + down,
            up,
            down,
            face_east[x, y : y + 1, :] * is_open,
            face_north[x, y : y + 1, :] * is_open,
            is_open,
            live[q] / scale,
            jnp.zeros((1, levels), jnp.float32),
        ]
        block[q * COEF_ROWS : (q + 1) * COEF_ROWS, :] = jnp.concatenate(rows, axis=0)
    size = 4 * COEF_ROWS
    last = [
        pltpu.make_async_copy(block, target.at[pl.ds(base, size)], small_sems.at[place])
        for place, (target, base) in enumerate(
            ((to_near, 2 * levels), (to_far, 2 * levels), (both, 4 * levels))
        )
    ]
    for copy in last:
        copy.start()
    for copy in copies + last:
        copy.wait()


def parities():
    even_lon = lax.rem(lax.axis_index("lon"), 2) == 0
    even_lat = lax.rem(lax.axis_index("lat"), 2) == 0
    return even_lon, even_lat


def wide_kernel(block, ring, wide):
    levels = block.shape[1]
    wide[: 2 * levels, :] = block[: 2 * levels, :]
    wide[2 * levels : block.shape[0], :] = ring[2 * levels :, :]


def corner_kernel(lon_near, lon_far, lat_near, lat_far, to_near, to_far):
    even_lon, even_lat = parities()
    levels = lon_near.shape[1]
    size = 4 * COEF_ROWS
    lon = slice(2 * levels, 2 * levels + size)
    lat = slice(4 * levels, 4 * levels + size)

    def west(rows):
        return jnp.where(even_lon, lon_far[rows, :], lon_near[rows, :])

    def east(rows):
        return jnp.where(even_lon, lon_near[rows, :], lon_far[rows, :])

    low, high = slice(0, levels), slice(levels, 2 * levels)
    base = 2 * levels
    for out, lower, other in ((to_near, jnp.logical_not(even_lat), lat_far), (to_far, even_lat, lat_near)):
        out[:levels, :] = jnp.where(lower, west(low), west(high))
        out[levels:base, :] = jnp.where(lower, east(low), east(high))
        out[base : base + size, :] = west(lon)
        out[base + size : base + 2 * size, :] = east(lon)
        out[base + 2 * size : base + 3 * size, :] = other[lat, :]


def split(values):
    high = values.astype(jnp.bfloat16)
    return high, (values - high.astype(jnp.float32)).astype(jnp.bfloat16)


def product(left, right):
    left_high, left_low = split(left)
    right_high, right_low = split(right)
    return jnp.dot(
        jnp.concatenate([left_high, left_high, left_low], axis=1),
        jnp.concatenate([right_high, right_low, right_high], axis=0),
        preferred_element_type=jnp.float32,
    )


def left(values):
    return pltpu.roll(values, 1, axis=1)


def right(values):
    return pltpu.roll(values, values.shape[1] - 1, axis=1)


class Stencil:
    def __init__(self, own, lon_near, lon_far, wide_near, wide_far, lat_near, lat_far, corner_near=None, corner_far=None):
        even_lon, even_lat = parities()
        levels = own.shape[1]
        size = 4 * COEF_ROWS
        full = 4 * levels
        half = 2 * levels
        self.levels = levels
        self.wide = {3: (even_lon, wide_near, wide_far), -2: (even_lon, wide_far, wide_near)}
        sources = {
            (0, 0): (None, own, own, full),
            (1, 0): (even_lon, lon_near, lon_far, half),
            (-1, 0): (even_lon, lon_far, lon_near, half),
            (0, 1): (even_lat, lat_near, lat_far, full),
            (0, -1): (even_lat, lat_far, lat_near, full),
            (2, 0): (even_lon, wide_near, wide_far, half),
            (-2, 0): (even_lon, wide_far, wide_near, half),
        }
        if corner_near is not None:
            sources |= {
                (-1, 1): (even_lat, corner_near, corner_far, half),
                (-1, -1): (even_lat, corner_far, corner_near, half),
                (1, 1): (even_lat, corner_near, corner_far, half + size),
                (1, -1): (even_lat, corner_far, corner_near, half + size),
                (0, 2): (even_lat, corner_near, corner_far, half + 2 * size),
                (0, -2): (even_lat, corner_far, corner_near, half + 2 * size),
            }
        self.sources = sources
        self.coefs = {place: self.fetch(*source, size) for place, source in sources.items()}
        self.east = functools.cache(self.east)
        self.north = functools.cache(self.north)
        self.main = functools.cache(self.main)

    def fetch(self, flag, first, other, start, count):
        if flag is None:
            return first[start : start + count, :]
        return jnp.where(flag, first[start : start + count, :], other[start : start + count, :])

    def coef(self, x, y, row):
        at = (2 * (x % 2) + y % 2) * COEF_ROWS + row
        return self.coefs[x // 2, y // 2][at : at + 1, :]

    def weight(self, x, y):
        return self.coef(x, y, WEIGHT)

    def east(self, x, y):
        return self.coef(x, y, EAST) * self.coef(x + 1, y, OPEN)

    def north(self, x, y):
        return self.coef(x, y, NORTH) * self.coef(x, y + 1, OPEN)

    def main(self, x, y):
        lon = self.east(x, y) + self.east(x - 1, y)
        return self.coef(x, y, DIAG) + lon + self.north(x, y) + self.north(x, y - 1)

    def lon_faces(self, x, y):
        above = self.east(x, y) * self.weight(x + 1, y)
        below = self.east(x - 1, y) * self.weight(x - 1, y)
        return (above, below) if x % 2 == 0 else (below, above)

    def lat_faces(self, x, y):
        above = self.north(x, y) * self.weight(x, y + 1)
        below = self.north(x, y - 1) * self.weight(x, y - 1)
        return (above, below) if y % 2 == 0 else (below, above)

    def own_diag(self, x, y):
        return (
            self.weight(x, y) * self.main(x, y) - self.lon_faces(x, y)[0] - self.lat_faces(x, y)[0]
        )

    def inverse(self, x, y):
        lon, lat = x // 2, y // 2
        levels = self.levels
        if x in self.wide:
            return self.fetch(*self.wide[x], y % 2 * levels, levels)
        if lon != 0 and lat != 0:
            start = 0 if lon < 0 else levels
        elif lon != 0:
            start = y % 2 * levels
        else:
            start = (2 * (x % 2) + y % 2) * levels
        return self.fetch(*self.sources[lon, lat][:3], start, levels)

    def residual(self, rows_t, x, y):
        total = None
        if (x, y) in rows_t:
            block = rows_t[x, y]
            total = (
                block * self.main(x, y)
                - left(block * self.coef(x, y, UP))
                - right(block * self.coef(x, y, DOWN))
            )
        for near, face in (
            ((x + 1, y), lambda: self.east(x, y)),
            ((x - 1, y), lambda: self.east(x - 1, y)),
            ((x, y + 1), lambda: self.north(x, y)),
            ((x, y - 1), lambda: self.north(x, y - 1)),
        ):
            if near in rows_t:
                term = rows_t[near] * face()
                total = -term if total is None else total - term
        return total


own_cells = [(x, y) for x in (0, 1) for y in (0, 1)]
lon_cells = [(x, y) for x in (-1, 2) for y in (0, 1)]
lat_cells = [(x, y) for x in (0, 1) for y in (-1, 2)]
reach_cells = own_cells + lon_cells + lat_cells
far_cells = [(x, y) for x in (-2, 3) for y in (0, 1)] + [(x, y) for x in (0, 1) for y in (-2, 3)]
groups = {}
for cell in lon_cells + lat_cells + far_cells + [(2, 2), (2, -1), (-1, 2), (-1, -1)]:
    groups.setdefault((cell[0] // 2, cell[1] // 2), []).append(cell)
first_targets = [(0, 0), (1, 0), (-1, 0), (0, 1), (0, -1)]


class Sums:
    def __init__(self, out, targets, started=()):
        self.out = out
        self.slots = {target: place for place, target in enumerate(targets)}
        self.started = set(started)

    def add(self, target, term):
        place = self.slots[target]
        if target in self.started:
            self.out[place] += term
        else:
            self.out[place] = term
            self.started.add(target)


def lateral_targets(x, y):
    lon, lat = x // 2, y // 2
    return (lon + (-1 if x % 2 == 0 else 1), lat), (lon, lat + (-1 if y % 2 == 0 else 1))


def apply_columns(cells, sums, x, y, smooth):
    lon_target, lat_target = lateral_targets(x, y)
    sums.add(lon_target, smooth * cells.lon_faces(x, y)[1])
    sums.add(lat_target, smooth * cells.lat_faces(x, y)[1])
    weight = cells.weight(x, y)
    return (
        smooth * cells.own_diag(x, y),
        smooth * (weight * cells.coef(x, y, UP)),
        smooth * (weight * cells.coef(x, y, DOWN)),
    )


def plus(parts, more):
    return more if parts is None else tuple(a + b for a, b in zip(parts, more))


def close_kernel(*refs):
    cells = Stencil(*refs[:7])
    rows_out, smooth_out, partial = refs[7:]
    levels = cells.levels
    row = lax.broadcasted_iota(jnp.int32, (levels, levels), 0)
    lane = lax.broadcasted_iota(jnp.int32, (levels, levels), 1)
    rows_t = {}
    for x, y in own_cells:
        block = cells.inverse(x, y)
        weight = cells.weight(x, y)
        smoothed = (
            block * cells.own_diag(x, y)
            - left(block * (weight * cells.coef(x, y, UP)))
            - right(block * (weight * cells.coef(x, y, DOWN)))
        )
        rows_t[x, y] = (jnp.where(row == lane, weight, 0.0) - relax_weight * smoothed).T
    for x, y in lon_cells:
        rows_t[x, y] = (cells.inverse(x, y) * (relax_weight * cells.lon_faces(x, y)[1])).T
    for x, y in lat_cells:
        rows_t[x, y] = (cells.inverse(x, y) * (relax_weight * cells.lat_faces(x, y)[1])).T
    for place, cell in enumerate(reach_cells):
        rows_out[place] = rows_t[cell]
    sums = Sums(partial, first_targets)
    parts = None
    for x, y in own_cells:
        rest = cells.residual(rows_t, x, y)
        smooth = product(rest, cells.inverse(x, y)) * relax_weight
        terms = apply_columns(cells, sums, x, y, smooth)
        parts = plus(parts, (rest * cells.weight(x, y) - terms[0],) + terms[1:])
    sums.add((0, 0), parts[0] + left(parts[1]) + right(parts[2]))
    for place, (x, y) in enumerate(far_cells):
        rest = cells.residual(rows_t, x, y)
        smooth_out[place] = product(rest, cells.inverse(x, y)) * relax_weight
        sums.add((x // 2, y // 2), rest * cells.weight(x, y))


def coarse_kernel(*refs):
    cells = Stencil(*refs[:9])
    rows_in, smooth_in, partial, out = refs[9:]
    rows_t = {cell: rows_in[place] for place, cell in enumerate(reach_cells)}
    sums = Sums(out, stencil_offsets)
    for place, target in enumerate(first_targets):
        sums.add(target, partial[place])
    for device, members in groups.items():
        straight = parts = None
        for x, y in members:
            if (x, y) in far_cells:
                smooth = smooth_in[far_cells.index((x, y))]
            else:
                rest = cells.residual(rows_t, x, y)
                smooth = product(rest, cells.inverse(x, y)) * relax_weight
                term = rest * cells.weight(x, y)
                straight = term if straight is None else straight + term
            parts = plus(parts, apply_columns(cells, sums, x, y, smooth))
        sums.add(device, straight - parts[0] + left(parts[1]) + right(parts[2]))


def local(inverse, vert_diag, vert_coup, face_east, face_north, land_mask, aggregate):
    levels = inverse.shape[-1]
    size = 4 * COEF_ROWS
    args = (inverse, vert_diag, vert_coup, face_east, face_north, land_mask, aggregate)
    vmem = pl.BlockSpec(memory_space=pltpu.VMEM)
    params = pltpu.CompilerParams(vmem_limit_bytes=8 * 1024 * 1024)
    array = lambda count: jax.ShapeDtypeStruct((count, levels), jnp.float32)
    cost = lambda size: pl.CostEstimate(flops=size * 10**6, bytes_accessed=size * 10**3, transcendentals=0)
    shapes = [4 * levels + size] + [2 * levels + size] * 2
    both, to_near, to_far = pl.pallas_call(
        pack_kernel,
        out_shape=tuple(array(rows) for rows in shapes),
        in_specs=[pl.BlockSpec(memory_space=pltpu.HBM)] * 7,
        out_specs=(pl.BlockSpec(memory_space=pltpu.HBM),) * 3,
        scratch_shapes=[pltpu.VMEM(arg.shape, arg.dtype) for arg in args[:5]]
        + [pltpu.SMEM(arg.shape, arg.dtype) for arg in args[5:]]
        + [pltpu.VMEM((size, levels), jnp.float32)]
        + [pltpu.SemaphoreType.DMA((7,)), pltpu.SemaphoreType.DMA((8,))],
    )(*args)
    lon_near = lax.ppermute(to_near, "lon", pair_near("lon"))
    lon_far = lax.ppermute(to_far, "lon", pair_far("lon", True))
    lat_near = lax.ppermute(both, "lat", pair_near("lat"))
    lat_far = lax.ppermute(both, "lat", pair_far("lat", False))

    def widened(block, ring, rows):
        return pl.pallas_call(
            wide_kernel,
            out_shape=array(rows),
            in_specs=[vmem] * 2,
            out_specs=vmem,
            compiler_params=params,
        )(block, ring)

    wide_far = lax.ppermute(
        widened(to_near, lon_near, 2 * levels + size + 8), "lon", pair_far("lon", True)
    )
    wide_near = lax.ppermute(widened(to_far, lon_far, 2 * levels + size), "lon", pair_near("lon"))
    corner_rows = 2 * levels + 3 * size
    corner_to_near, corner_to_far = pl.pallas_call(
        corner_kernel,
        out_shape=(array(corner_rows), array(corner_rows)),
        in_specs=[vmem] * 4,
        out_specs=(vmem, vmem),
        compiler_params=params,
    )(lon_near, lon_far, lat_near, lat_far)
    corner_near = lax.ppermute(corner_to_near, "lat", pair_near("lat"))
    corner_far = lax.ppermute(corner_to_far, "lat", pair_far("lat", False))
    blocks = lambda count: jax.ShapeDtypeStruct((count, levels, levels), jnp.float32)
    near_args = (both, lon_near, lon_far, wide_near, wide_far, lat_near, lat_far)
    close = pl.pallas_call(
        close_kernel,
        out_shape=(blocks(len(reach_cells)), blocks(len(far_cells)), blocks(len(first_targets))),
        in_specs=[vmem] * 7,
        out_specs=(vmem,) * 3,
        cost_estimate=cost(50000),
        compiler_params=params,
    )(*near_args)
    out = pl.pallas_call(
        coarse_kernel,
        out_shape=blocks(len(stencil_offsets)),
        in_specs=[vmem] * 12,
        out_specs=vmem,
        compiler_params=params,
    )(*near_args, corner_near, corner_far, *close)
    return out[None, None]


def solution(mesh):
    return jax.shard_map(
        local,
        mesh=mesh,
        in_specs=(
            P("lon", "lat", None, None),
            P("lon", "lat", None),
            P("lon", "lat", None),
            P("lon", "lat", None),
            P("lon", "lat", None),
            P("lon", "lat"),
            P("lon", "lat"),
        ),
        out_specs=P("lon", "lat", None, None, None),
        check_vma=False,
    )
```

time: 42.2 us -> 27.4 us (0.65)
  the two profiles are of different devices: /device:TPU:6 before, /device:TPU:1 now
where the time goes in v1:
time: 27.4 us; the launch traced here: 27.3 us
  starting transfers between devices  16 us (58%)
  Pallas kernels  5.46 us (20%)
  waiting for transfers between devices  4.82 us (18%)
  local copies, waits for them, and re-layouts  0.91 us (3%)
    ppermute x1, starting transfers between devices, local(): lat_far = lax.ppermute(both, 'lat', pair_far('lat', False))  4.36 us
    ppermute x1, starting transfers between devices, local(): lon_far = lax.ppermute(to_far, 'lon', pair_far('lon', True))  3.26 us
    ppermute x1, starting transfers between devices, local(): corner_far = lax.ppermute(corner_to_far, 'lat', pair_far('lat', False))  3.02 us
    ppermute x1, waiting for transfers between devices, local(): corner_far = lax.ppermute(corner_to_far, 'lat', pair_far('lat', False))  2.46 us
    ppermute x1, waiting for transfers between devices, local(): lat_far = lax.ppermute(both, 'lat', pair_far('lat', False))  2.34 us
    pallas_call x1, Pallas kernels, local(): pl.pallas_call(coarse_kernel, out_shape=blocks(len(stencil_offsets)), in_...  2.26 us
    ppermute x1, starting transfers between devices, local(): lon_near = lax.ppermute(to_near, 'lon', pair_near('lon'))  2.13 us
    ppermute x1, starting transfers between devices, local(): corner_near = lax.ppermute(corner_to_near, 'lat', pair_near('lat'))  2.08 us
  transfers between devices with their start and end apart: 8, of which 2 were waited for; matrix products, arithmetic and copies ran while one was open for 0% of the time, Pallas kernels for 5%

profile of v1, /device:TPU:1, one launch (start us, length us, event | category | flops | bytes accessed | tf_op | source)
XLA Modules:
  0.0 27.3 jit_solution(14965317358556234532)
XLA Ops:
  0.0 1.9 %shard_map.73 = (f32[544,128]{1,0:T(8,128)}, f32[288,128]{1,0:T(8,128)}, f32[288,128]{1,0:T(8,128)}) custom-call(f32[2,2,128,128]{3,2,1,0:T(8,128)} %inverse_hbm.1, f32[2,2,128]{2,1,0:T(2,128)} %diag_hbm.1, f32[2,2,128]{2,1,0:T(2,128)} %coup_hbm.1, f32[2,2,128]{2,1,0:T(2,128)} %east_hbm.1, f32[2,2,128]{2,1,0:T(2,128)} %north_hbm.1, s32[2,2]{1,0:T(2,128)} %land_hbm.1, ...), custom_call_target="tpu_custom_call" | custom-call | tf_op jit(solution)/shard_map/pallas_call | solution.py:416
  1.9 2.1 %collective-permute-start = (f32[288,128]{1,0:T(8,128)}, f32[288,128]{1,0:T(8,128)S(1)}, u32[]{:S(2)}, u32[]{:S(2)}) collective-permute-start(f32[288,128]{1,0:T(8,128)} %get-tuple-element.14.block), channel_id=1, source_target_pairs={{0,4},{4,0},{8,12},{12,8},{16,20},{20,16},{24,28},{28,24},{1,5},{5... | collective-permute-start | bytes 442376 | tf_op jit(solution)/shard_map/ppermute | solution.py:426
  4.0 3.3 %collective-permute-start.1 = (f32[288,128]{1,0:T(8,128)}, f32[288,128]{1,0:T(8,128)S(1)}, u32[]{:S(2)}, u32[]{:S(2)}) collective-permute-start(f32[288,128]{1,0:T(8,128)} %get-tuple-element.15.block), channel_id=1, source_target_pairs={{0,28},{4,8},{8,4},{12,16},{16,12},{20,24},{24,20},{28,0},{1,29},{... | collective-permute-start | bytes 442376 | tf_op jit(solution)/shard_map/ppermute | solution.py:427
  7.3 0.0 copy-start.1
  7.3 4.4 %collective-permute-start.5 = (f32[544,128]{1,0:T(8,128)}, f32[544,128]{1,0:T(8,128)S(1)}, u32[]{:S(2)}, u32[]{:S(2)}) collective-permute-start(f32[544,128]{1,0:T(8,128)} %get-tuple-element.13.refs_0_), channel_id=1, source_target_pairs={{1,2},{2,1},{5,6},{6,5},{9,10},{10,9},{13,14},{14,13},{17,18},{18,... | collective-permute-start | bytes 835592 | tf_op jit(solution)/shard_map/ppermute | solution.py:429
  11.6 0.1 collective-permute-start.4
  11.7 0.0 collective-permute-done.ring.lon_near.refs_1_
  11.7 0.0 copy-start.2
  11.7 0.9 %copy-done.2 = f32[288,128]{1,0:T(8,128)S(1)} copy-done((f32[288,128]{1,0:T(8,128)S(1)}, f32[288,128]{1,0:T(8,128)}, u32[]{:S(2)}) %copy-start.2) | copy-done | bytes 147480
  12.7 1.0 %collective-permute-start.3 = (f32[296,128]{1,0:T(8,128)S(1)}, f32[296,128]{1,0:T(8,128)S(1)}, u32[]{:S(2)}, u32[]{:S(2)}) collective-permute-start(f32[296,128]{1,0:T(8,128)S(1)} %shard_map.75), channel_id=1, source_target_pairs={{0,28},{4,8},{8,4},{12,16},{16,12},{20,24},{24,20},{28,0},{1,29},{... | collective-permute-start | bytes 454664 | tf_op jit(solution)/shard_map/ppermute | solution.py:440
  13.6 0.0 collective-permute-done.1.ring.lon_far.refs_2_
  13.6 0.0 copy-done.1
  13.6 0.0 copy-start
  13.7 0.1 collective-permute-start.2
  13.7 2.3 %collective-permute-done.5.lat_far.refs_6_ = f32[544,128]{1,0:T(8,128)S(1)} collective-permute-done((f32[544,128]{1,0:T(8,128)}, f32[544,128]{1,0:T(8,128)S(1)}, u32[]{:S(2)}, u32[]{:S(2)}) %collective-permute-start.5) | collective-permute-done | bytes 278560 | tf_op jit(solution)/shard_map/ppermute | solution.py:429
  16.1 0.0 collective-permute-done.4.lat_near.refs_5_
  16.1 2.1 %collective-permute-start.6 = (f32[352,128]{1,0:T(8,128)S(1)}, f32[352,128]{1,0:T(8,128)S(1)}, u32[]{:S(2)}, u32[]{:S(2)}) collective-permute-start(f32[352,128]{1,0:T(8,128)S(1)} %get-tuple-element.16), channel_id=1, source_target_pairs={{0,1},{1,0},{2,3},{3,2},{4,5},{5,4},{6,7},{7,6},{8,9},{9,8},{10,11... | collective-permute-start | bytes 540680 | tf_op jit(solution)/shard_map/ppermute | solution.py:452
  18.2 3.0 %collective-permute-start.7 = (f32[352,128]{1,0:T(8,128)S(1)}, f32[352,128]{1,0:T(8,128)S(1)}, u32[]{:S(2)}, u32[]{:S(2)}) collective-permute-start(f32[352,128]{1,0:T(8,128)S(1)} %get-tuple-element.17), channel_id=1, source_target_pairs={{1,2},{2,1},{5,6},{6,5},{9,10},{10,9},{13,14},{14,13},{17,18},{18,... | collective-permute-start | bytes 540680 | tf_op jit(solution)/shard_map/ppermute | solution.py:453
  21.2 0.0 collective-permute-done.2.refs_3_
  21.2 0.0 collective-permute-done.3.refs_4_
  21.3 0.0 copy-done
  21.3 1.3 %shard_map.77 = (f32[12,128,128]{2,1,0:T(8,128)S(1)}, f32[8,128,128]{2,1,0:T(8,128)S(1)}, f32[5,128,128]{2,1,0:T(8,128)S(1)}) custom-call(f32[544,128]{1,0:T(8,128)S(1)} %copy-done, f32[288,128]{1,0:T(8,128)S(1)} %collective-permute-done.ring.lon_near.refs_1_, f32[288,128]{1,0:T(8,128)S(1)} %collective-permute-done.1.ring.lon_far.refs_2_, ...), custom_call_target="tpu_custom_call" | custom-call | flops 49999998976 | bytes 50000000 | tf_op jit(solution)/shard_map/pallas_call | solution.py:456
  22.5 0.0 collective-permute-done.6.refs_7_
  22.5 2.5 %collective-permute-done.7.refs_8_ = f32[352,128]{1,0:T(8,128)S(1)} collective-permute-done((f32[352,128]{1,0:T(8,128)S(1)}, f32[352,128]{1,0:T(8,128)S(1)}, u32[]{:S(2)}, u32[]{:S(2)}) %collective-permute-start.7) | collective-permute-done | bytes 180256 | tf_op jit(solution)/shard_map/ppermute | solution.py:453
  25.0 2.3 %shard_map.78 = f32[13,128,128]{2,1,0:T(8,128)} custom-call(f32[544,128]{1,0:T(8,128)S(1)} %copy-done, f32[288,128]{1,0:T(8,128)S(1)} %collective-permute-done.ring.lon_near.refs_1_, f32[288,128]{1,0:T(8,128)S(1)} %collective-permute-done.1.ring.lon_far.refs_2_, f32[288,128]{1,0:T(8,128)S(1)} %collective-permute-done.2.refs_3_, ...), custom_call_target="tpu_custom_call" | custom-call | tf_op jit(solution)/shard_map/pallas_call | solution.py:464
  (3 shorter events, 0.1 us)
Async XLA Ops:
  1.9 9.8 %collective-permute-start = (f32[288,128]{1,0:T(8,128)}, f32[288,128]{1,0:T(8,128)S(1)}, u32[]{:S(2)}, u32[]{:S(2)}) collective-permute-start(f32[288,128]{1,0:T(8,128)} %get-tuple-element.14.block), channel_id=1, source_target_pairs={{0,4},{4,0},{8,12},{12,8},{16,20},{20,16},{24,28},{28,24},{1,5},{5... | collective-permute-start | bytes 442376 | tf_op jit(solution)/shard_map/ppermute | solution.py:426
  4.0 9.6 %collective-permute-start.1 = (f32[288,128]{1,0:T(8,128)}, f32[288,128]{1,0:T(8,128)S(1)}, u32[]{:S(2)}, u32[]{:S(2)}) collective-permute-start(f32[288,128]{1,0:T(8,128)} %get-tuple-element.15.block), channel_id=1, source_target_pairs={{0,28},{4,8},{8,4},{12,16},{16,12},{20,24},{24,20},{28,0},{1,29},{... | collective-permute-start | bytes 442376 | tf_op jit(solution)/shard_map/ppermute | solution.py:427
  7.3 6.4 %copy-start.1 = (f32[288,128]{1,0:T(8,128)S(1)}, f32[288,128]{1,0:T(8,128)}, u32[]{:S(2)}) copy-start(f32[288,128]{1,0:T(8,128)} %get-tuple-element.15.block) | copy-start | bytes 442372
  7.3 8.8 %collective-permute-start.5 = (f32[544,128]{1,0:T(8,128)}, f32[544,128]{1,0:T(8,128)S(1)}, u32[]{:S(2)}, u32[]{:S(2)}) collective-permute-start(f32[544,128]{1,0:T(8,128)} %get-tuple-element.13.refs_0_), channel_id=1, source_target_pairs={{1,2},{2,1},{5,6},{6,5},{9,10},{10,9},{13,14},{14,13},{17,18},{18,... | collective-permute-start | bytes 835592 | tf_op jit(solution)/shard_map/ppermute | solution.py:429
  11.6 4.4 %collective-permute-start.4 = (f32[544,128]{1,0:T(8,128)}, f32[544,128]{1,0:T(8,128)S(1)}, u32[]{:S(2)}, u32[]{:S(2)}) collective-permute-start(f32[544,128]{1,0:T(8,128)} %get-tuple-element.13.refs_0_), channel_id=1, source_target_pairs={{0,1},{1,0},{2,3},{3,2},{4,5},{5,4},{6,7},{7,6},{8,9},{9,8},{10,11... | collective-permute-start | bytes 835592 | tf_op jit(solution)/shard_map/ppermute | solution.py:428
  11.7 0.9 %copy-start.2 = (f32[288,128]{1,0:T(8,128)S(1)}, f32[288,128]{1,0:T(8,128)}, u32[]{:S(2)}) copy-start(f32[288,128]{1,0:T(8,128)} %get-tuple-element.14.block) | copy-start | bytes 442372
  12.7 8.6 %collective-permute-start.3 = (f32[296,128]{1,0:T(8,128)S(1)}, f32[296,128]{1,0:T(8,128)S(1)}, u32[]{:S(2)}, u32[]{:S(2)}) collective-permute-start(f32[296,128]{1,0:T(8,128)S(1)} %shard_map.75), channel_id=1, source_target_pairs={{0,28},{4,8},{8,4},{12,16},{16,12},{20,24},{24,20},{28,0},{1,29},{... | collective-permute-start | bytes 454664 | tf_op jit(solution)/shard_map/ppermute | solution.py:440
  13.6 7.6 %copy-start = (f32[544,128]{1,0:T(8,128)S(1)}, f32[544,128]{1,0:T(8,128)}, u32[]{:S(2)}) copy-start(f32[544,128]{1,0:T(8,128)} %get-tuple-element.13.refs_0_) | copy-start | bytes 835588
  13.7 7.6 %collective-permute-start.2 = (f32[288,128]{1,0:T(8,128)S(1)}, f32[288,128]{1,0:T(8,128)S(1)}, u32[]{:S(2)}, u32[]{:S(2)}) collective-permute-start(f32[288,128]{1,0:T(8,128)S(1)} %shard_map.74), channel_id=1, source_target_pairs={{0,4},{4,0},{8,12},{12,8},{16,20},{20,16},{24,28},{28,24},{1,5},{5... | collective-permute-start | bytes 442376 | tf_op jit(solution)/shard_map/ppermute | solution.py:443
  16.1 6.4 %collective-permute-start.6 = (f32[352,128]{1,0:T(8,128)S(1)}, f32[352,128]{1,0:T(8,128)S(1)}, u32[]{:S(2)}, u32[]{:S(2)}) collective-permute-start(f32[352,128]{1,0:T(8,128)S(1)} %get-tuple-element.16), channel_id=1, source_target_pairs={{0,1},{1,0},{2,3},{3,2},{4,5},{5,4},{6,7},{7,6},{8,9},{9,8},{10,11... | collective-permute-start | bytes 540680 | tf_op jit(solution)/shard_map/ppermute | solution.py:452
  18.2 6.8 %collective-permute-start.7 = (f32[352,128]{1,0:T(8,128)S(1)}, f32[352,128]{1,0:T(8,128)S(1)}, u32[]{:S(2)}, u32[]{:S(2)}) collective-permute-start(f32[352,128]{1,0:T(8,128)S(1)} %get-tuple-element.17), channel_id=1, source_target_pairs={{1,2},{2,1},{5,6},{6,5},{9,10},{10,9},{13,14},{14,13},{17,18},{18,... | collective-permute-start | bytes 540680 | tf_op jit(solution)/shard_map/ppermute | solution.py:453

commit v2 on v1

--- a/solution.py
+++ b/solution.py
@@ -63,9 +63,7 @@
     face_north,
     land,
     aggregate,
-    block,
     small_sems,
-    sems,
 ):
     lon = lax.rem(lax.axis_index("lon"), 2)
     levels = inverse.shape[-1]
@@ -85,20 +83,6 @@
         )
     ]
     for copy in small:
-        copy.start()
-    copies = []
-    for y in range(2):
-        rows = pl.ds(y * levels, levels)
-        copies.append((inverse.at[1 - lon, y], to_near.at[rows]))
-        copies.append((inverse.at[lon, y], to_far.at[rows]))
-        for x in range(2):
-            copies.append((inverse.at[x, y], both.at[pl.ds((2 * x + y) * levels, levels)]))
-    copies = [
-        pltpu.make_async_copy(source, target, sems.at[place])
-        for place, (source, target) in enumerate(copies)
-    ]
-    whole.wait()
-    for copy in copies:
         copy.start()
     for copy in small:
         copy.wait()
@@ -124,18 +108,17 @@
             live[q] / scale,
             jnp.zeros((1, levels), jnp.float32),
         ]
-        block[q * COEF_ROWS : (q + 1) * COEF_ROWS, :] = jnp.concatenate(rows, axis=0)
-    size = 4 * COEF_ROWS
-    last = [
-        pltpu.make_async_copy(block, target.at[pl.ds(base, size)], small_sems.at[place])
-        for place, (target, base) in enumerate(
-            ((to_near, 2 * levels), (to_far, 2 * levels), (both, 4 * levels))
-        )
-    ]
-    for copy in last:
-        copy.start()
-    for copy in copies + last:
-        copy.wait()
+        block = jnp.concatenate(rows, axis=0)
+        for ref, base in ((both, 4 * levels), (to_near, 2 * levels), (to_far, 2 * levels)):
+            ref[base + q * COEF_ROWS : base + (q + 1) * COEF_ROWS, :] = block
+    whole.wait()
+    even_lon = lon == 0
+    for y in range(2):
+        low, high = inverse[0, y], inverse[1, y]
+        both[y * levels : (y + 1) * levels, :] = low
+        both[(2 + y) * levels : (3 + y) * levels, :] = high
+        to_near[y * levels : (y + 1) * levels, :] = jnp.where(even_lon, high, low)
+        to_far[y * levels : (y + 1) * levels, :] = jnp.where(even_lon, low, high)
 
 
 def parities():
@@ -144,10 +127,19 @@
     return even_lon, even_lat
 
 
-def wide_kernel(block, ring, wide):
-    levels = block.shape[1]
-    wide[: 2 * levels, :] = block[: 2 * levels, :]
-    wide[2 * levels : block.shape[0], :] = ring[2 * levels :, :]
+def wide_kernel(facing_far, own, ring, wide):
+    even_lon, _ = parities()
+    levels = own.shape[1]
+    high = jnp.logical_not(even_lon) if facing_far else even_lon
+    for y in range(2):
+        low_rows = own[y * levels : (y + 1) * levels, :]
+        high_rows = own[(2 + y) * levels : (3 + y) * levels, :]
+        wide[y * levels : (y + 1) * levels, :] = jnp.where(high, high_rows, low_rows)
+    base = 2 * levels
+    coef = [ring[base + q * COEF_ROWS : base + (q + 1) * COEF_ROWS, :] for q in range(4)]
+    for y in range(2):
+        beyond = jnp.where(high, coef[y], coef[2 + y])
+        wide[base + y * COEF_ROWS : base + (y + 1) * COEF_ROWS, :] = beyond
 
 
 def corner_kernel(lon_near, lon_far, lat_near, lat_far, to_near, to_far):
@@ -211,8 +203,6 @@
             (-1, 0): (even_lon, lon_far, lon_near, half),
             (0, 1): (even_lat, lat_near, lat_far, full),
             (0, -1): (even_lat, lat_far, lat_near, full),
-            (2, 0): (even_lon, wide_near, wide_far, half),
-            (-2, 0): (even_lon, wide_far, wide_near, half),
         }
         if corner_near is not None:
             sources |= {
@@ -225,6 +215,10 @@
             }
         self.sources = sources
         self.coefs = {place: self.fetch(*source, size) for place, source in sources.items()}
+        pair = 2 * COEF_ROWS
+        for x, source in self.wide.items() if wide_near is not None else ():
+            beyond = self.fetch(*source, half, pair)
+            self.coefs[2 if x > 0 else -2, 0] = jnp.concatenate([beyond, beyond], axis=0)
         self.east = functools.cache(self.east)
         self.north = functools.cache(self.north)
         self.main = functools.cache(self.main)
@@ -304,7 +298,9 @@
 lon_cells = [(x, y) for x in (-1, 2) for y in (0, 1)]
 lat_cells = [(x, y) for x in (0, 1) for y in (-1, 2)]
 reach_cells = own_cells + lon_cells + lat_cells
-far_cells = [(x, y) for x in (-2, 3) for y in (0, 1)] + [(x, y) for x in (0, 1) for y in (-2, 3)]
+lon_far_cells = [(x, y) for x in (-2, 3) for y in (0, 1)]
+lat_far_cells = [(x, y) for x in (0, 1) for y in (-2, 3)]
+far_cells = lon_far_cells + lat_far_cells
 groups = {}
 for cell in lon_cells + lat_cells + far_cells + [(2, 2), (2, -1), (-1, 2), (-1, -1)]:
     groups.setdefault((cell[0] // 2, cell[1] // 2), []).append(cell)
@@ -347,9 +343,8 @@
     return more if parts is None else tuple(a + b for a, b in zip(parts, more))
 
 
-def close_kernel(*refs):
-    cells = Stencil(*refs[:7])
-    rows_out, smooth_out, partial = refs[7:]
+def close_kernel(own, lon_near, lon_far, lat_near, lat_far, rows_out, smooth_out, partial):
+    cells = Stencil(own, lon_near, lon_far, None, None, lat_near, lat_far)
     levels = cells.levels
     row = lax.broadcasted_iota(jnp.int32, (levels, levels), 0)
     lane = lax.broadcasted_iota(jnp.int32, (levels, levels), 1)
@@ -377,15 +372,25 @@
         terms = apply_columns(cells, sums, x, y, smooth)
         parts = plus(parts, (rest * cells.weight(x, y) - terms[0],) + terms[1:])
     sums.add((0, 0), parts[0] + left(parts[1]) + right(parts[2]))
-    for place, (x, y) in enumerate(far_cells):
+    for x, y in far_cells:
+        rest = cells.residual(rows_t, x, y)
+        sums.add((x // 2, y // 2), rest * cells.weight(x, y))
+        if (x, y) in lat_far_cells:
+            smooth = product(rest, cells.inverse(x, y)) * relax_weight
+            smooth_out[lat_far_cells.index((x, y))] = smooth
+
+
+def wide_products_kernel(own, lon_near, lon_far, wide_near, wide_far, lat_near, lat_far, rows_in, smooth_out):
+    cells = Stencil(own, lon_near, lon_far, wide_near, wide_far, lat_near, lat_far)
+    rows_t = {cell: rows_in[place] for place, cell in enumerate(reach_cells) if cell in lon_cells}
+    for place, (x, y) in enumerate(lon_far_cells):
         rest = cells.residual(rows_t, x, y)
         smooth_out[place] = product(rest, cells.inverse(x, y)) * relax_weight
-        sums.add((x // 2, y // 2), rest * cells.weight(x, y))
 
 
 def coarse_kernel(*refs):
     cells = Stencil(*refs[:9])
-    rows_in, smooth_in, partial, out = refs[9:]
+    rows_in, lat_smooth, partial, lon_smooth, out = refs[9:]
     rows_t = {cell: rows_in[place] for place, cell in enumerate(reach_cells)}
     sums = Sums(out, stencil_offsets)
     for place, target in enumerate(first_targets):
@@ -393,8 +398,10 @@
     for device, members in groups.items():
         straight = parts = None
         for x, y in members:
-            if (x, y) in far_cells:
-                smooth = smooth_in[far_cells.index((x, y))]
+            if (x, y) in lon_far_cells:
+                smooth = lon_smooth[lon_far_cells.index((x, y))]
+            elif (x, y) in lat_far_cells:
+                smooth = lat_smooth[lat_far_cells.index((x, y))]
             else:
                 rest = cells.residual(rows_t, x, y)
                 smooth = product(rest, cells.inverse(x, y)) * relax_weight
@@ -415,32 +422,31 @@
     shapes = [4 * levels + size] + [2 * levels + size] * 2
     both, to_near, to_far = pl.pallas_call(
         pack_kernel,
-        out_shape=tuple(array(rows) for rows in shapes),
+        out_shape=tuple(pltpu.VMEM((rows, levels), jnp.float32) for rows in shapes),
         in_specs=[pl.BlockSpec(memory_space=pltpu.HBM)] * 7,
-        out_specs=(pl.BlockSpec(memory_space=pltpu.HBM),) * 3,
+        out_specs=(vmem,) * 3,
         scratch_shapes=[pltpu.VMEM(arg.shape, arg.dtype) for arg in args[:5]]
         + [pltpu.SMEM(arg.shape, arg.dtype) for arg in args[5:]]
-        + [pltpu.VMEM((size, levels), jnp.float32)]
-        + [pltpu.SemaphoreType.DMA((7,)), pltpu.SemaphoreType.DMA((8,))],
-    )(*args)
+        + [pltpu.SemaphoreType.DMA((7,))],
+        compiler_params=pltpu.CompilerParams(vmem_limit_bytes=8 * 1024 * 1024),
+    )(*(pltpu.with_memory_space_constraint(arg, pltpu.HBM) for arg in args))
     lon_near = lax.ppermute(to_near, "lon", pair_near("lon"))
     lon_far = lax.ppermute(to_far, "lon", pair_far("lon", True))
     lat_near = lax.ppermute(both, "lat", pair_near("lat"))
     lat_far = lax.ppermute(both, "lat", pair_far("lat", False))
 
-    def widened(block, ring, rows):
+    def widened(facing_far, ring, spare, weight):
         return pl.pallas_call(
-            wide_kernel,
-            out_shape=array(rows),
+            functools.partial(wide_kernel, facing_far),
+            out_shape=array(2 * (levels + COEF_ROWS) + spare),
             in_specs=[vmem] * 2,
             out_specs=vmem,
+            cost_estimate=cost(weight),
             compiler_params=params,
-        )(block, ring)
-
-    wide_far = lax.ppermute(
-        widened(to_near, lon_near, 2 * levels + size + 8), "lon", pair_far("lon", True)
-    )
-    wide_near = lax.ppermute(widened(to_far, lon_far, 2 * levels + size), "lon", pair_near("lon"))
+        )(both, ring)
+
+    wide_far = lax.ppermute(widened(False, lon_near, 8, 1000), "lon", pair_far("lon", True))
+    wide_near = lax.ppermute(widened(True, lon_far, 0, 8000), "lon", pair_near("lon"))
     corner_rows = 2 * levels + 3 * size
     corner_to_near, corner_to_far = pl.pallas_call(
         corner_kernel,
@@ -452,22 +458,30 @@
     corner_near = lax.ppermute(corner_to_near, "lat", pair_near("lat"))
     corner_far = lax.ppermute(corner_to_far, "lat", pair_far("lat", False))
     blocks = lambda count: jax.ShapeDtypeStruct((count, levels, levels), jnp.float32)
-    near_args = (both, lon_near, lon_far, wide_near, wide_far, lat_near, lat_far)
     close = pl.pallas_call(
         close_kernel,
-        out_shape=(blocks(len(reach_cells)), blocks(len(far_cells)), blocks(len(first_targets))),
-        in_specs=[vmem] * 7,
+        out_shape=(blocks(len(reach_cells)), blocks(len(lat_far_cells)), blocks(len(first_targets))),
+        in_specs=[vmem] * 5,
         out_specs=(vmem,) * 3,
+        cost_estimate=cost(1),
+        compiler_params=params,
+    )(both, lon_near, lon_far, lat_near, lat_far)
+    near_args = (both, lon_near, lon_far, wide_near, wide_far, lat_near, lat_far)
+    lon_smooth = pl.pallas_call(
+        wide_products_kernel,
+        out_shape=blocks(len(lon_far_cells)),
+        in_specs=[vmem] * 8,
+        out_specs=vmem,
         cost_estimate=cost(50000),
         compiler_params=params,
-    )(*near_args)
+    )(*near_args, close[0])
     out = pl.pallas_call(
         coarse_kernel,
         out_shape=blocks(len(stencil_offsets)),
-        in_specs=[vmem] * 12,
+        in_specs=[vmem] * 13,
         out_specs=vmem,
         compiler_params=params,
-    )(*near_args, corner_near, corner_far, *close)
+    )(*near_args, corner_near, corner_far, *close, lon_smooth)
     return out[None, None]
 
 

time: 27.4 us -> 25.5 us (0.931)
  local copies, waits for them, and re-layouts: 0.91 us -> 0 us
  starting transfers between devices: 16 us -> 15.1 us
  Pallas kernels: 5.46 us -> 4.67 us
  waiting for transfers between devices: 4.82 us -> 5.48 us
    unnamed x6 -> x0, local copies, waits for them, and re-layouts: 0.91 us -> none
    ppermute x1, starting transfers between devices: 2.08 us -> 1.31 us  [local(): corner_near = lax.ppermute(corner_to_near, 'lat', pair_near('lat'))]
    ppermute x1, waiting for transfers between devices: 2.34 us -> 3.02 us  [local(): lat_far = lax.ppermute(both, 'lat', pair_far('lat', False))]
    pallas_call x3 -> x4, Pallas kernels: 1.89 us -> 1.37 us  [the longest x1 1.04 us: local(): pl.pallas_call(pack_kernel, out_shape=tuple((pltpu.VMEM((rows, levels), j...]
where the time goes in v2:
time: 25.5 us; the launch traced here: 25.3 us
  starting transfers between devices  15.1 us (59%)
  waiting for transfers between devices  5.48 us (21%)
  Pallas kernels  4.67 us (18%)
    ppermute x1, starting transfers between devices, local(): lat_far = lax.ppermute(both, 'lat', pair_far('lat', False))  4.23 us
    ppermute x1, starting transfers between devices, local(): lon_far = lax.ppermute(to_far, 'lon', pair_far('lon', True))  3.26 us
    ppermute x1, waiting for transfers between devices, local(): lat_far = lax.ppermute(both, 'lat', pair_far('lat', False))  3.02 us
    ppermute x1, starting transfers between devices, local(): corner_far = lax.ppermute(corner_to_far, 'lat', pair_far('lat', False))  3.02 us
    ppermute x1, waiting for transfers between devices, local(): corner_far = lax.ppermute(corner_to_far, 'lat', pair_far('lat', False))  2.44 us
    pallas_call x1, Pallas kernels, local(): pl.pallas_call(coarse_kernel, out_shape=blocks(len(stencil_offsets)), in_...  2.24 us
    ppermute x1, starting transfers between devices, local(): lon_near = lax.ppermute(to_near, 'lon', pair_near('lon'))  2.13 us
    ppermute x1, starting transfers between devices, local(): corner_near = lax.ppermute(corner_to_near, 'lat', pair_near('lat'))  1.31 us
  transfers between devices with their start and end apart: 8, of which 2 were waited for; matrix products, arithmetic and copies ran while one was open for 0% of the time, Pallas kernels for 5%

profile of v2, /device:TPU:1, one launch (start us, length us, event | category | flops | bytes accessed | tf_op | source)
XLA Modules:
  0.0 25.3 jit_solution(12235924202097071013)
XLA Ops:
  0.0 1.0 %shard_map.73 = (f32[544,128]{1,0:T(8,128)S(1)}, f32[288,128]{1,0:T(8,128)S(1)}, f32[288,128]{1,0:T(8,128)S(1)}) custom-call(f32[2,2,128,128]{3,2,1,0:T(8,128)} %inverse_hbm.1, f32[2,2,128]{2,1,0:T(2,128)} %diag_hbm.1, f32[2,2,128]{2,1,0:T(2,128)} %coup_hbm.1, f32[2,2,128]{2,1,0:T(2,128)} %east_hbm.1, f32[2,2,128]{2,1,0:T(2,128)} %north_hbm.1, ...), custom_call_target="tpu_custom_call" | custom-call | tf_op jit(solution)/shard_map/pallas_call | solution.py:423
  1.1 2.1 %collective-permute-start = (f32[288,128]{1,0:T(8,128)S(1)}, f32[288,128]{1,0:T(8,128)S(1)}, u32[]{:S(2)}, u32[]{:S(2)}) collective-permute-start(f32[288,128]{1,0:T(8,128)S(1)} %get-tuple-element.14), channel_id=1, source_target_pairs={{0,4},{4,0},{8,12},{12,8},{16,20},{20,16},{24,28},{28,24},{1,5},{5... | collective-permute-start | bytes 442376 | tf_op jit(solution)/shard_map/ppermute | solution.py:433
  3.2 3.3 %collective-permute-start.1 = (f32[288,128]{1,0:T(8,128)S(1)}, f32[288,128]{1,0:T(8,128)S(1)}, u32[]{:S(2)}, u32[]{:S(2)}) collective-permute-start(f32[288,128]{1,0:T(8,128)S(1)} %get-tuple-element.15), channel_id=1, source_target_pairs={{0,28},{4,8},{8,4},{12,16},{16,12},{20,24},{24,20},{28,0},{1,29},{... | collective-permute-start | bytes 442376 | tf_op jit(solution)/shard_map/ppermute | solution.py:434
  6.5 4.2 %collective-permute-start.5 = (f32[544,128]{1,0:T(8,128)S(1)}, f32[544,128]{1,0:T(8,128)S(1)}, u32[]{:S(2)}, u32[]{:S(2)}) collective-permute-start(f32[544,128]{1,0:T(8,128)S(1)} %get-tuple-element.13.own.refs_0_), channel_id=1, source_target_pairs={{1,2},{2,1},{5,6},{6,5},{9,10},{10,9},{13,14},{14,13},{17,18},{18,... | collective-permute-start | bytes 835592 | tf_op jit(solution)/shard_map/ppermute | solution.py:436
  10.7 0.1 collective-permute-start.4
  10.8 0.0 collective-permute-done.ring.lon_near.refs_1_
  10.8 1.0 %collective-permute-start.3 = (f32[280,128]{1,0:T(8,128)S(1)}, f32[280,128]{1,0:T(8,128)S(1)}, u32[]{:S(2)}, u32[]{:S(2)}) collective-permute-start(f32[280,128]{1,0:T(8,128)S(1)} %shard_map.75), channel_id=1, source_target_pairs={{0,28},{4,8},{8,4},{12,16},{16,12},{20,24},{24,20},{28,0},{1,29},{... | collective-permute-start | bytes 430088 | tf_op jit(solution)/shard_map/ppermute | solution.py:448
  11.8 0.0 collective-permute-done.1.ring.lon_far.refs_2_
  11.8 0.1 collective-permute-start.2
  11.9 3.0 %collective-permute-done.5.lat_far.refs_6_ = f32[544,128]{1,0:T(8,128)S(1)} collective-permute-done((f32[544,128]{1,0:T(8,128)S(1)}, f32[544,128]{1,0:T(8,128)S(1)}, u32[]{:S(2)}, u32[]{:S(2)}) %collective-permute-start.5) | collective-permute-done | bytes 278560 | tf_op jit(solution)/shard_map/ppermute | solution.py:436
  14.9 0.0 collective-permute-done.4.lat_near.refs_5_
  15.0 1.3 %collective-permute-start.6 = (f32[352,128]{1,0:T(8,128)S(1)}, f32[352,128]{1,0:T(8,128)S(1)}, u32[]{:S(2)}, u32[]{:S(2)}) collective-permute-start(f32[352,128]{1,0:T(8,128)S(1)} %get-tuple-element.16), channel_id=1, source_target_pairs={{0,1},{1,0},{2,3},{3,2},{4,5},{5,4},{6,7},{7,6},{8,9},{9,8},{10,11... | collective-permute-start | bytes 540680 | tf_op jit(solution)/shard_map/ppermute | solution.py:458
  16.3 3.0 %collective-permute-start.7 = (f32[352,128]{1,0:T(8,128)S(1)}, f32[352,128]{1,0:T(8,128)S(1)}, u32[]{:S(2)}, u32[]{:S(2)}) collective-permute-start(f32[352,128]{1,0:T(8,128)S(1)} %get-tuple-element.17), channel_id=1, source_target_pairs={{1,2},{2,1},{5,6},{6,5},{9,10},{10,9},{13,14},{14,13},{17,18},{18,... | collective-permute-start | bytes 540680 | tf_op jit(solution)/shard_map/ppermute | solution.py:459
  19.3 1.0 %shard_map.77 = (f32[12,128,128]{2,1,0:T(8,128)S(1)}, f32[4,128,128]{2,1,0:T(8,128)S(1)}, f32[5,128,128]{2,1,0:T(8,128)S(1)}) custom-call(f32[544,128]{1,0:T(8,128)S(1)} %get-tuple-element.13.own.refs_0_, f32[288,128]{1,0:T(8,128)S(1)} %collective-permute-done.ring.lon_near.refs_1_, f32[288,128]{1,0:T(8,128)S(1)} %collective-permute-done.1.ring.lon_far.refs_2_, ...), custom_call_target="tpu_custom_call" | custom-call | flops 1000000 | bytes 1000 | tf_op jit(solution)/shard_map/pallas_call | solution.py:461
  20.3 0.0 collective-permute-done.2.wide_near.refs_3_
  20.3 0.0 collective-permute-done.3.wide_far.refs_4_
  20.3 0.3 %shard_map.78.refs_12_ = f32[4,128,128]{2,1,0:T(8,128)S(1)} custom-call(f32[544,128]{1,0:T(8,128)S(1)} %get-tuple-element.13.own.refs_0_, f32[288,128]{1,0:T(8,128)S(1)} %collective-permute-done.ring.lon_near.refs_1_, f32[288,128]{1,0:T(8,128)S(1)} %collective-permute-done.1.ring.lon_far.refs_2_, f32[272,128]{1,0:T(8,128)S(1)} %collective-permute-done.2.wide_near.refs_3_, ...), custom_call_target="tpu_custom_call" | custom-call | flops 49999998976 | bytes 50000000 | tf_op jit(solution)/shard_map/pallas_call | solution.py:470
  20.6 0.0 collective-permute-done.6.refs_7_
  20.6 2.4 %collective-permute-done.7.refs_8_ = f32[352,128]{1,0:T(8,128)S(1)} collective-permute-done((f32[352,128]{1,0:T(8,128)S(1)}, f32[352,128]{1,0:T(8,128)S(1)}, u32[]{:S(2)}, u32[]{:S(2)}) %collective-permute-start.7) | collective-permute-done | bytes 180256 | tf_op jit(solution)/shard_map/ppermute | solution.py:459
  23.1 2.2 %shard_map.79 = f32[13,128,128]{2,1,0:T(8,128)} custom-call(f32[544,128]{1,0:T(8,128)S(1)} %get-tuple-element.13.own.refs_0_, f32[288,128]{1,0:T(8,128)S(1)} %collective-permute-done.ring.lon_near.refs_1_, f32[288,128]{1,0:T(8,128)S(1)} %collective-permute-done.1.ring.lon_far.refs_2_, f32[272,128]{1,0:T(8,128)S(1)} %collective-permute-done.2.wide_near.refs_3_, ...), custom_call_target="tpu_custom_call" | custom-call | tf_op jit(solution)/shard_map/pallas_call | solution.py:478
  (3 shorter events, 0.1 us)
Async XLA Ops:
  1.1 9.7 %collective-permute-start = (f32[288,128]{1,0:T(8,128)S(1)}, f32[288,128]{1,0:T(8,128)S(1)}, u32[]{:S(2)}, u32[]{:S(2)}) collective-permute-start(f32[288,128]{1,0:T(8,128)S(1)} %get-tuple-element.14), channel_id=1, source_target_pairs={{0,4},{4,0},{8,12},{12,8},{16,20},{20,16},{24,28},{28,24},{1,5},{5... | collective-permute-start | bytes 442376 | tf_op jit(solution)/shard_map/ppermute | solution.py:433
  3.2 8.6 %collective-permute-start.1 = (f32[288,128]{1,0:T(8,128)S(1)}, f32[288,128]{1,0:T(8,128)S(1)}, u32[]{:S(2)}, u32[]{:S(2)}) collective-permute-start(f32[288,128]{1,0:T(8,128)S(1)} %get-tuple-element.15), channel_id=1, source_target_pairs={{0,28},{4,8},{8,4},{12,16},{16,12},{20,24},{24,20},{28,0},{1,29},{... | collective-permute-start | bytes 442376 | tf_op jit(solution)/shard_map/ppermute | solution.py:434
  6.5 8.5 %collective-permute-start.5 = (f32[544,128]{1,0:T(8,128)S(1)}, f32[544,128]{1,0:T(8,128)S(1)}, u32[]{:S(2)}, u32[]{:S(2)}) collective-permute-start(f32[544,128]{1,0:T(8,128)S(1)} %get-tuple-element.13.own.refs_0_), channel_id=1, source_target_pairs={{1,2},{2,1},{5,6},{6,5},{9,10},{10,9},{13,14},{14,13},{17,18},{18,... | collective-permute-start | bytes 835592 | tf_op jit(solution)/shard_map/ppermute | solution.py:436
  10.7 4.2 %collective-permute-start.4 = (f32[544,128]{1,0:T(8,128)S(1)}, f32[544,128]{1,0:T(8,128)S(1)}, u32[]{:S(2)}, u32[]{:S(2)}) collective-permute-start(f32[544,128]{1,0:T(8,128)S(1)} %get-tuple-element.13.own.refs_0_), channel_id=1, source_target_pairs={{0,1},{1,0},{2,3},{3,2},{4,5},{5,4},{6,7},{7,6},{8,9},{9,8},{10,11... | collective-permute-start | bytes 835592 | tf_op jit(solution)/shard_map/ppermute | solution.py:435
  10.8 9.5 %collective-permute-start.3 = (f32[280,128]{1,0:T(8,128)S(1)}, f32[280,128]{1,0:T(8,128)S(1)}, u32[]{:S(2)}, u32[]{:S(2)}) collective-permute-start(f32[280,128]{1,0:T(8,128)S(1)} %shard_map.75), channel_id=1, source_target_pairs={{0,28},{4,8},{8,4},{12,16},{16,12},{20,24},{24,20},{28,0},{1,29},{... | collective-permute-start | bytes 430088 | tf_op jit(solution)/shard_map/ppermute | solution.py:448
  11.8 8.5 %collective-permute-start.2 = (f32[272,128]{1,0:T(8,128)S(1)}, f32[272,128]{1,0:T(8,128)S(1)}, u32[]{:S(2)}, u32[]{:S(2)}) collective-permute-start(f32[272,128]{1,0:T(8,128)S(1)} %shard_map.74), channel_id=1, source_target_pairs={{0,4},{4,0},{8,12},{12,8},{16,20},{20,16},{24,28},{28,24},{1,5},{5... | collective-permute-start | bytes 417800 | tf_op jit(solution)/shard_map/ppermute | solution.py:449
  15.0 5.7 %collective-permute-start.6 = (f32[352,128]{1,0:T(8,128)S(1)}, f32[352,128]{1,0:T(8,128)S(1)}, u32[]{:S(2)}, u32[]{:S(2)}) collective-permute-start(f32[352,128]{1,0:T(8,128)S(1)} %get-tuple-element.16), channel_id=1, source_target_pairs={{0,1},{1,0},{2,3},{3,2},{4,5},{5,4},{6,7},{7,6},{8,9},{9,8},{10,11... | collective-permute-start | bytes 540680 | tf_op jit(solution)/shard_map/ppermute | solution.py:458
  16.3 6.8 %collective-permute-start.7 = (f32[352,128]{1,0:T(8,128)S(1)}, f32[352,128]{1,0:T(8,128)S(1)}, u32[]{:S(2)}, u32[]{:S(2)}) collective-permute-start(f32[352,128]{1,0:T(8,128)S(1)} %get-tuple-element.17), channel_id=1, source_target_pairs={{1,2},{2,1},{5,6},{6,5},{9,10},{10,9},{13,14},{14,13},{17,18},{18,... | collective-permute-start | bytes 540680 | tf_op jit(solution)/shard_map/ppermute | solution.py:459

commit v3 on v2

--- a/solution.py
+++ b/solution.py
@@ -32,17 +32,22 @@
     return [(i, i ^ 1) for i in range(count) if i ^ 1 < count]
 
 
-def pair_far(axis, closed):
+def pair_far_closed(axis):
     count = lax.axis_size(axis)
-    pairs = [(i, i - 1 if i % 2 == 0 else i + 1) for i in range(count)]
-    if closed:
-        return [(i, j % count) for i, j in pairs]
-    return [(i, j) for i, j in pairs if 0 <= j < count]
-
-
-def second(axis, outward):
-    count = lax.axis_size(axis)
-    return [(i, (i + (2 if (i % 2 == 0) == outward else -2)) % count) for i in range(count)]
+    return [(i, (i - 1 if i % 2 == 0 else i + 1) % count) for i in range(count)]
+
+
+def exchange_lat_far(values):
+    lon_count, lat_count = lax.axis_size("lon"), lax.axis_size("lat")
+    pairs = []
+    for i in range(lon_count):
+        for j in range(lat_count):
+            partner = j - 1 if j % 2 == 0 else j + 1
+            if 0 <= partner < lat_count:
+                pairs.append((i * lat_count + j, i * lat_count + partner))
+            elif i ^ 2 < lon_count:
+                pairs.append((i * lat_count + j, (i ^ 2) * lat_count + j))
+    return lax.ppermute(values, ("lon", "lat"), pairs)
 
 
 def pack_kernel(
@@ -127,6 +132,11 @@
     return even_lon, even_lat
 
 
+def has_lat_far():
+    index = lax.axis_index("lat")
+    return index != jnp.where(lax.rem(index, 2) == 0, 0, lax.axis_size("lat") - 1)
+
+
 def wide_kernel(facing_far, own, ring, wide):
     even_lon, _ = parities()
     levels = own.shape[1]
@@ -157,12 +167,16 @@
 
     low, high = slice(0, levels), slice(levels, 2 * levels)
     base = 2 * levels
-    for out, lower, other in ((to_near, jnp.logical_not(even_lat), lat_far), (to_far, even_lat, lat_near)):
+    beyond = jnp.where(has_lat_far(), lat_far[lat, :], 0.0)
+    for out, lower, other in (
+        (to_near, jnp.logical_not(even_lat), beyond),
+        (to_far, even_lat, lat_near[lat, :]),
+    ):
         out[:levels, :] = jnp.where(lower, west(low), west(high))
         out[levels:base, :] = jnp.where(lower, east(low), east(high))
         out[base : base + size, :] = west(lon)
         out[base + size : base + 2 * size, :] = east(lon)
-        out[base + 2 * size : base + 3 * size, :] = other[lat, :]
+        out[base + 2 * size : base + 3 * size, :] = other
 
 
 def split(values):
@@ -215,6 +229,12 @@
             }
         self.sources = sources
         self.coefs = {place: self.fetch(*source, size) for place, source in sources.items()}
+        far = has_lat_far()
+        keep = {1: jnp.logical_or(even_lat, far), -1: jnp.logical_or(jnp.logical_not(even_lat), far)}
+        for place in sources:
+            if place[1] != 0:
+                inside = keep[1 if place[1] > 0 else -1]
+                self.coefs[place] = jnp.where(inside, self.coefs[place], 0.0)
         pair = 2 * COEF_ROWS
         for x, source in self.wide.items() if wide_near is not None else ():
             beyond = self.fetch(*source, half, pair)
@@ -431,9 +451,9 @@
         compiler_params=pltpu.CompilerParams(vmem_limit_bytes=8 * 1024 * 1024),
     )(*(pltpu.with_memory_space_constraint(arg, pltpu.HBM) for arg in args))
     lon_near = lax.ppermute(to_near, "lon", pair_near("lon"))
-    lon_far = lax.ppermute(to_far, "lon", pair_far("lon", True))
+    lon_far = lax.ppermute(to_far, "lon", pair_far_closed("lon"))
     lat_near = lax.ppermute(both, "lat", pair_near("lat"))
-    lat_far = lax.ppermute(both, "lat", pair_far("lat", False))
+    lat_far = exchange_lat_far(both)
 
     def widened(facing_far, ring, spare, weight):
         return pl.pallas_call(
@@ -445,7 +465,7 @@
             compiler_params=params,
         )(both, ring)
 
-    wide_far = lax.ppermute(widened(False, lon_near, 8, 1000), "lon", pair_far("lon", True))
+    wide_far = lax.ppermute(widened(False, lon_near, 8, 1000), "lon", pair_far_closed("lon"))
     wide_near = lax.ppermute(widened(True, lon_far, 0, 8000), "lon", pair_near("lon"))
     corner_rows = 2 * levels + 3 * size
     corner_to_near, corner_to_far = pl.pallas_call(
@@ -456,7 +476,7 @@
         compiler_params=params,
     )(lon_near, lon_far, lat_near, lat_far)
     corner_near = lax.ppermute(corner_to_near, "lat", pair_near("lat"))
-    corner_far = lax.ppermute(corner_to_far, "lat", pair_far("lat", False))
+    corner_far = exchange_lat_far(corner_to_far)
     blocks = lambda count: jax.ShapeDtypeStruct((count, levels, levels), jnp.float32)
     close = pl.pallas_call(
         close_kernel,

time: 25.5 us -> 24.2 us (0.949)
  the two profiles are of different devices: /device:TPU:1 before, /device:TPU:0 now
where the time goes in v3:
time: 24.2 us; the launch traced here: 24 us
  starting transfers between devices  15.3 us (63%)
  Pallas kernels  4.66 us (19%)
  waiting for transfers between devices  4 us (17%)
    ppermute x1, starting transfers between devices, local(): lax.ppermute(widened(False, lon_near, 8, 1000), 'lon', pair_far_closed('l...  5.58 us
    ppermute x1, starting transfers between devices, local(): lon_far = lax.ppermute(to_far, 'lon', pair_far_closed('lon'))  3.54 us
    ppermute x1, starting transfers between devices, local(): lon_near = lax.ppermute(to_near, 'lon', pair_near('lon'))  3.03 us
    ppermute x1, waiting for transfers between devices, local(): lax.ppermute(widened(True, lon_far, 0, 8000), 'lon', pair_near('lon'))  2.5 us
    pallas_call x1, Pallas kernels, local(): pl.pallas_call(coarse_kernel, out_shape=blocks(len(stencil_offsets)), in_...  2.25 us
    ppermute x1, starting transfers between devices, local(): lat_near = lax.ppermute(both, 'lat', pair_near('lat'))  1.6 us
    ppermute x2, starting transfers between devices, exchange_lat_far(): return lax.ppermute(values, ('lon', 'lat'), pairs)  1.39 us
    ppermute x1, waiting for transfers between devices, local(): lon_near = lax.ppermute(to_near, 'lon', pair_near('lon'))  1.11 us
  transfers between devices with their start and end apart: 8, of which 3 were waited for; matrix products, arithmetic and copies ran while one was open for 0% of the time, Pallas kernels for 6%

profile of v3, /device:TPU:0, one launch (start us, length us, event | category | flops | bytes accessed | tf_op | source)
XLA Modules:
  0.0 24.0 jit_solution(10443325994961732917)
XLA Ops:
  0.0 1.0 %shard_map.73 = (f32[544,128]{1,0:T(8,128)S(1)}, f32[288,128]{1,0:T(8,128)S(1)}, f32[288,128]{1,0:T(8,128)S(1)}) custom-call(f32[2,2,128,128]{3,2,1,0:T(8,128)} %inverse_hbm.1, f32[2,2,128]{2,1,0:T(2,128)} %diag_hbm.1, f32[2,2,128]{2,1,0:T(2,128)} %coup_hbm.1, f32[2,2,128]{2,1,0:T(2,128)} %east_hbm.1, f32[2,2,128]{2,1,0:T(2,128)} %north_hbm.1, ...), custom_call_target="tpu_custom_call" | custom-call | tf_op jit(solution)/shard_map/pallas_call | solution.py:443
  1.1 3.0 %collective-permute-start = (f32[288,128]{1,0:T(8,128)S(1)}, f32[288,128]{1,0:T(8,128)S(1)}, u32[]{:S(2)}, u32[]{:S(2)}) collective-permute-start(f32[288,128]{1,0:T(8,128)S(1)} %get-tuple-element.14), channel_id=1, source_target_pairs={{0,4},{4,0},{8,12},{12,8},{16,20},{20,16},{24,28},{28,24},{1,5},{5... | collective-permute-start | bytes 442376 | tf_op jit(solution)/shard_map/ppermute | solution.py:453
  4.1 3.5 %collective-permute-start.1 = (f32[288,128]{1,0:T(8,128)S(1)}, f32[288,128]{1,0:T(8,128)S(1)}, u32[]{:S(2)}, u32[]{:S(2)}) collective-permute-start(f32[288,128]{1,0:T(8,128)S(1)} %get-tuple-element.15), channel_id=1, source_target_pairs={{0,28},{4,8},{8,4},{12,16},{16,12},{20,24},{24,20},{28,0},{1,29},{... | collective-permute-start | bytes 442376 | tf_op jit(solution)/shard_map/ppermute | solution.py:454
  7.6 0.0 collective-permute-start.5
  7.6 1.6 %collective-permute-start.4 = (f32[544,128]{1,0:T(8,128)S(1)}, f32[544,128]{1,0:T(8,128)S(1)}, u32[]{:S(2)}, u32[]{:S(2)}) collective-permute-start(f32[544,128]{1,0:T(8,128)S(1)} %get-tuple-element.13.own.refs_0_), channel_id=1, source_target_pairs={{0,1},{1,0},{2,3},{3,2},{4,5},{5,4},{6,7},{7,6},{8,9},{9,8},{10,11... | collective-permute-start | bytes 835592 | tf_op jit(solution)/shard_map/ppermute | solution.py:455
  9.2 1.1 %collective-permute-done.ring.lon_near.refs_1_ = f32[288,128]{1,0:T(8,128)S(1)} collective-permute-done((f32[288,128]{1,0:T(8,128)S(1)}, f32[288,128]{1,0:T(8,128)S(1)}, u32[]{:S(2)}, u32[]{:S(2)}) %collective-permute-start) | collective-permute-done | bytes 147488 | tf_op jit(solution)/shard_map/ppermute | solution.py:453
  10.4 5.6 %collective-permute-start.3 = (f32[280,128]{1,0:T(8,128)S(1)}, f32[280,128]{1,0:T(8,128)S(1)}, u32[]{:S(2)}, u32[]{:S(2)}) collective-permute-start(f32[280,128]{1,0:T(8,128)S(1)} %shard_map.75), channel_id=1, source_target_pairs={{0,28},{4,8},{8,4},{12,16},{16,12},{20,24},{24,20},{28,0},{1,29},{... | collective-permute-start | bytes 430088 | tf_op jit(solution)/shard_map/ppermute | solution.py:468
  16.0 0.0 collective-permute-done.1.ring.lon_far.refs_2_
  16.0 0.1 collective-permute-start.2
  16.1 0.0 collective-permute-done.5.lat_far.refs_6_
  16.1 0.0 collective-permute-done.4.lat_near.refs_5_
  16.1 0.1 shard_map.76
  16.2 0.1 collective-permute-start.6
  16.2 1.4 %collective-permute-start.7 = (f32[352,128]{1,0:T(8,128)S(1)}, f32[352,128]{1,0:T(8,128)S(1)}, u32[]{:S(2)}, u32[]{:S(2)}) collective-permute-start(f32[352,128]{1,0:T(8,128)S(1)} %get-tuple-element.17), channel_id=1, source_target_pairs={{0,8},{1,2},{2,1},{3,11},{4,12},{5,6},{6,5},{7,15},{8,0},{9,10},{1... | collective-permute-start | bytes 540680 | tf_op jit(solution)/shard_map/ppermute | solution.py:50
  17.6 1.0 %shard_map.77 = (f32[12,128,128]{2,1,0:T(8,128)S(1)}, f32[4,128,128]{2,1,0:T(8,128)S(1)}, f32[5,128,128]{2,1,0:T(8,128)S(1)}) custom-call(f32[544,128]{1,0:T(8,128)S(1)} %get-tuple-element.13.own.refs_0_, f32[288,128]{1,0:T(8,128)S(1)} %collective-permute-done.ring.lon_near.refs_1_, f32[288,128]{1,0:T(8,128)S(1)} %collective-permute-done.1.ring.lon_far.refs_2_, ...), custom_call_target="tpu_custom_call" | custom-call | flops 1000000 | bytes 1000 | tf_op jit(solution)/shard_map/pallas_call | solution.py:481
  18.6 2.5 %collective-permute-done.2.wide_near.refs_3_ = f32[272,128]{1,0:T(8,128)S(1)} collective-permute-done((f32[272,128]{1,0:T(8,128)S(1)}, f32[272,128]{1,0:T(8,128)S(1)}, u32[]{:S(2)}, u32[]{:S(2)}) %collective-permute-start.2) | collective-permute-done | bytes 139296 | tf_op jit(solution)/shard_map/ppermute | solution.py:469
  21.1 0.0 collective-permute-done.3.wide_far.refs_4_
  21.1 0.3 %shard_map.78.refs_12_ = f32[4,128,128]{2,1,0:T(8,128)S(1)} custom-call(f32[544,128]{1,0:T(8,128)S(1)} %get-tuple-element.13.own.refs_0_, f32[288,128]{1,0:T(8,128)S(1)} %collective-permute-done.ring.lon_near.refs_1_, f32[288,128]{1,0:T(8,128)S(1)} %collective-permute-done.1.ring.lon_far.refs_2_, f32[272,128]{1,0:T(8,128)S(1)} %collective-permute-done.2.wide_near.refs_3_, ...), custom_call_target="tpu_custom_call" | custom-call | flops 49999998976 | bytes 50000000 | tf_op jit(solution)/shard_map/pallas_call | solution.py:490
  21.4 0.0 collective-permute-done.6.refs_7_
  21.4 0.4 %collective-permute-done.7.refs_8_ = f32[352,128]{1,0:T(8,128)S(1)} collective-permute-done((f32[352,128]{1,0:T(8,128)S(1)}, f32[352,128]{1,0:T(8,128)S(1)}, u32[]{:S(2)}, u32[]{:S(2)}) %collective-permute-start.7) | collective-permute-done | bytes 180256 | tf_op jit(solution)/shard_map/ppermute | solution.py:50
  21.8 2.3 %shard_map.79 = f32[13,128,128]{2,1,0:T(8,128)} custom-call(f32[544,128]{1,0:T(8,128)S(1)} %get-tuple-element.13.own.refs_0_, f32[288,128]{1,0:T(8,128)S(1)} %collective-permute-done.ring.lon_near.refs_1_, f32[288,128]{1,0:T(8,128)S(1)} %collective-permute-done.1.ring.lon_far.refs_2_, f32[272,128]{1,0:T(8,128)S(1)} %collective-permute-done.2.wide_near.refs_3_, ...), custom_call_target="tpu_custom_call" | custom-call | tf_op jit(solution)/shard_map/pallas_call | solution.py:498
  (2 shorter events, 0.0 us)
Async XLA Ops:
  1.1 9.3 %collective-permute-start = (f32[288,128]{1,0:T(8,128)S(1)}, f32[288,128]{1,0:T(8,128)S(1)}, u32[]{:S(2)}, u32[]{:S(2)}) collective-permute-start(f32[288,128]{1,0:T(8,128)S(1)} %get-tuple-element.14), channel_id=1, source_target_pairs={{0,4},{4,0},{8,12},{12,8},{16,20},{20,16},{24,28},{28,24},{1,5},{5... | collective-permute-start | bytes 442376 | tf_op jit(solution)/shard_map/ppermute | solution.py:453
  4.1 11.9 %collective-permute-start.1 = (f32[288,128]{1,0:T(8,128)S(1)}, f32[288,128]{1,0:T(8,128)S(1)}, u32[]{:S(2)}, u32[]{:S(2)}) collective-permute-start(f32[288,128]{1,0:T(8,128)S(1)} %get-tuple-element.15), channel_id=1, source_target_pairs={{0,28},{4,8},{8,4},{12,16},{16,12},{20,24},{24,20},{28,0},{1,29},{... | collective-permute-start | bytes 442376 | tf_op jit(solution)/shard_map/ppermute | solution.py:454
  7.6 8.4 %collective-permute-start.5 = (f32[544,128]{1,0:T(8,128)S(1)}, f32[544,128]{1,0:T(8,128)S(1)}, u32[]{:S(2)}, u32[]{:S(2)}) collective-permute-start(f32[544,128]{1,0:T(8,128)S(1)} %get-tuple-element.13.own.refs_0_), channel_id=1, source_target_pairs={{0,8},{1,2},{2,1},{3,11},{4,12},{5,6},{6,5},{7,15},{8,0},{9,10},{1... | collective-permute-start | bytes 835592 | tf_op jit(solution)/shard_map/ppermute | solution.py:50
  7.6 8.5 %collective-permute-start.4 = (f32[544,128]{1,0:T(8,128)S(1)}, f32[544,128]{1,0:T(8,128)S(1)}, u32[]{:S(2)}, u32[]{:S(2)}) collective-permute-start(f32[544,128]{1,0:T(8,128)S(1)} %get-tuple-element.13.own.refs_0_), channel_id=1, source_target_pairs={{0,1},{1,0},{2,3},{3,2},{4,5},{5,4},{6,7},{7,6},{8,9},{9,8},{10,11... | collective-permute-start | bytes 835592 | tf_op jit(solution)/shard_map/ppermute | solution.py:455
  10.4 10.7 %collective-permute-start.3 = (f32[280,128]{1,0:T(8,128)S(1)}, f32[280,128]{1,0:T(8,128)S(1)}, u32[]{:S(2)}, u32[]{:S(2)}) collective-permute-start(f32[280,128]{1,0:T(8,128)S(1)} %shard_map.75), channel_id=1, source_target_pairs={{0,28},{4,8},{8,4},{12,16},{16,12},{20,24},{24,20},{28,0},{1,29},{... | collective-permute-start | bytes 430088 | tf_op jit(solution)/shard_map/ppermute | solution.py:468
  16.0 5.1 %collective-permute-start.2 = (f32[272,128]{1,0:T(8,128)S(1)}, f32[272,128]{1,0:T(8,128)S(1)}, u32[]{:S(2)}, u32[]{:S(2)}) collective-permute-start(f32[272,128]{1,0:T(8,128)S(1)} %shard_map.74), channel_id=1, source_target_pairs={{0,4},{4,0},{8,12},{12,8},{16,20},{20,16},{24,28},{28,24},{1,5},{5... | collective-permute-start | bytes 417800 | tf_op jit(solution)/shard_map/ppermute | solution.py:469
  16.2 5.3 %collective-permute-start.6 = (f32[352,128]{1,0:T(8,128)S(1)}, f32[352,128]{1,0:T(8,128)S(1)}, u32[]{:S(2)}, u32[]{:S(2)}) collective-permute-start(f32[352,128]{1,0:T(8,128)S(1)} %get-tuple-element.16), channel_id=1, source_target_pairs={{0,1},{1,0},{2,3},{3,2},{4,5},{5,4},{6,7},{7,6},{8,9},{9,8},{10,11... | collective-permute-start | bytes 540680 | tf_op jit(solution)/shard_map/ppermute | solution.py:478
  16.2 5.6 %collective-permute-start.7 = (f32[352,128]{1,0:T(8,128)S(1)}, f32[352,128]{1,0:T(8,128)S(1)}, u32[]{:S(2)}, u32[]{:S(2)}) collective-permute-start(f32[352,128]{1,0:T(8,128)S(1)} %get-tuple-element.17), channel_id=1, source_target_pairs={{0,8},{1,2},{2,1},{3,11},{4,12},{5,6},{6,5},{7,15},{8,0},{9,10},{1... | collective-permute-start | bytes 540680 | tf_op jit(solution)/shard_map/ppermute | solution.py:50

commit v4 on v3

--- a/solution.py
+++ b/solution.py
@@ -185,8 +185,11 @@
 
 
 def product(left, right):
+    return product_of_parts(left, *split(right))
+
+
+def product_of_parts(left, right_high, right_low):
     left_high, left_low = split(left)
-    right_high, right_low = split(right)
     return jnp.dot(
         jnp.concatenate([left_high, left_high, left_low], axis=1),
         jnp.concatenate([right_high, right_low, right_high], axis=0),
@@ -265,6 +268,18 @@
         lon = self.east(x, y) + self.east(x - 1, y)
         return self.coef(x, y, DIAG) + lon + self.north(x, y) + self.north(x, y - 1)
 
+    def outer_face(self, x, y):
+        if x in (0, 1):
+            return self.east(x - 1, y) if x == 0 else self.east(x, y)
+        return self.north(x, y - 1) if y == 0 else self.north(x, y)
+
+    def inner_main(self, x, y):
+        if x in (0, 1):
+            inner = self.east(0, y) + self.north(x, y) + self.north(x, y - 1)
+        else:
+            inner = self.north(x, 0) + self.east(x, y) + self.east(x - 1, y)
+        return self.coef(x, y, DIAG) + inner
+
     def lon_faces(self, x, y):
         above = self.east(x, y) * self.weight(x + 1, y)
         below = self.east(x - 1, y) * self.weight(x - 1, y)
@@ -293,12 +308,12 @@
             start = (2 * (x % 2) + y % 2) * levels
         return self.fetch(*self.sources[lon, lat][:3], start, levels)
 
-    def residual(self, rows_t, x, y):
+    def residual(self, rows_t, x, y, main=None):
         total = None
         if (x, y) in rows_t:
             block = rows_t[x, y]
             total = (
-                block * self.main(x, y)
+                block * (self.main if main is None else main)(x, y)
                 - left(block * self.coef(x, y, UP))
                 - right(block * self.coef(x, y, DOWN))
             )
@@ -317,12 +332,14 @@
 own_cells = [(x, y) for x in (0, 1) for y in (0, 1)]
 lon_cells = [(x, y) for x in (-1, 2) for y in (0, 1)]
 lat_cells = [(x, y) for x in (0, 1) for y in (-1, 2)]
-reach_cells = own_cells + lon_cells + lat_cells
+near_cells = lon_cells + lat_cells
+reach_cells = own_cells + near_cells
 lon_far_cells = [(x, y) for x in (-2, 3) for y in (0, 1)]
 lat_far_cells = [(x, y) for x in (0, 1) for y in (-2, 3)]
 far_cells = lon_far_cells + lat_far_cells
+corner_cells = [(2, 2), (2, -1), (-1, 2), (-1, -1)]
 groups = {}
-for cell in lon_cells + lat_cells + far_cells + [(2, 2), (2, -1), (-1, 2), (-1, -1)]:
+for cell in corner_cells + lon_far_cells + lon_cells + lat_far_cells + lat_cells:
     groups.setdefault((cell[0] // 2, cell[1] // 2), []).append(cell)
 first_targets = [(0, 0), (1, 0), (-1, 0), (0, 1), (0, -1)]
 
@@ -363,7 +380,7 @@
     return more if parts is None else tuple(a + b for a, b in zip(parts, more))
 
 
-def close_kernel(own, lon_near, lon_far, lat_near, lat_far, rows_out, smooth_out, partial):
+def close_kernel(own, lon_near, lon_far, lat_near, lat_far, rows_out, smooth_out, partial, rest_out, high_out, low_out):
     cells = Stencil(own, lon_near, lon_far, None, None, lat_near, lat_far)
     levels = cells.levels
     row = lax.broadcasted_iota(jnp.int32, (levels, levels), 0)
@@ -398,6 +415,9 @@
         if (x, y) in lat_far_cells:
             smooth = product(rest, cells.inverse(x, y)) * relax_weight
             smooth_out[lat_far_cells.index((x, y))] = smooth
+    for place, (x, y) in enumerate(near_cells):
+        rest_out[place] = cells.residual(rows_t, x, y, cells.inner_main)
+        high_out[place], low_out[place] = split(cells.inverse(x, y))
 
 
 def wide_products_kernel(own, lon_near, lon_far, wide_near, wide_far, lat_near, lat_far, rows_in, smooth_out):
@@ -408,13 +428,23 @@
         smooth_out[place] = product(rest, cells.inverse(x, y)) * relax_weight
 
 
+def targets_of(device, members):
+    return {device}.union(*(lateral_targets(*cell) for cell in members))
+
+
+last_group = {
+    target: device for device, members in groups.items() for target in targets_of(device, members)
+}
+
+
 def coarse_kernel(*refs):
     cells = Stencil(*refs[:9])
-    rows_in, lat_smooth, partial, lon_smooth, out = refs[9:]
+    rows_in, lat_smooth, partial, rest_in, high_in, low_in, lon_smooth, out, blocks, sems = refs[9:]
     rows_t = {cell: rows_in[place] for place, cell in enumerate(reach_cells)}
-    sums = Sums(out, stencil_offsets)
+    sums = Sums(blocks, stencil_offsets)
     for place, target in enumerate(first_targets):
         sums.add(target, partial[place])
+    copies = []
     for device, members in groups.items():
         straight = parts = None
         for x, y in members:
@@ -423,12 +453,25 @@
             elif (x, y) in lat_far_cells:
                 smooth = lat_smooth[lat_far_cells.index((x, y))]
             else:
-                rest = cells.residual(rows_t, x, y)
-                smooth = product(rest, cells.inverse(x, y)) * relax_weight
+                if (x, y) in near_cells:
+                    place = near_cells.index((x, y))
+                    rest = rest_in[place] + rows_t[x, y] * cells.outer_face(x, y)
+                    smooth = product_of_parts(rest, high_in[place], low_in[place])
+                else:
+                    rest = cells.residual(rows_t, x, y)
+                    smooth = product(rest, cells.inverse(x, y))
+                smooth = smooth * relax_weight
                 term = rest * cells.weight(x, y)
                 straight = term if straight is None else straight + term
             parts = plus(parts, apply_columns(cells, sums, x, y, smooth))
         sums.add(device, straight - parts[0] + left(parts[1]) + right(parts[2]))
+        for target, last in last_group.items():
+            if last == device:
+                place = sums.slots[target]
+                copies.append(pltpu.make_async_copy(blocks.at[place], out.at[place], sems.at[place]))
+                copies[-1].start()
+    for copy in copies:
+        copy.wait()
 
 
 def local(inverse, vert_diag, vert_coup, face_east, face_north, land_mask, aggregate):
@@ -480,9 +523,12 @@
     blocks = lambda count: jax.ShapeDtypeStruct((count, levels, levels), jnp.float32)
     close = pl.pallas_call(
         close_kernel,
-        out_shape=(blocks(len(reach_cells)), blocks(len(lat_far_cells)), blocks(len(first_targets))),
+        out_shape=(
+            *(blocks(len(cells)) for cells in (reach_cells, lat_far_cells, first_targets, near_cells)),
+            *(jax.ShapeDtypeStruct((len(near_cells), levels, levels), jnp.bfloat16),) * 2,
+        ),
         in_specs=[vmem] * 5,
-        out_specs=(vmem,) * 3,
+        out_specs=(vmem,) * 6,
         cost_estimate=cost(1),
         compiler_params=params,
     )(both, lon_near, lon_far, lat_near, lat_far)
@@ -498,8 +544,12 @@
     out = pl.pallas_call(
         coarse_kernel,
         out_shape=blocks(len(stencil_offsets)),
-        in_specs=[vmem] * 13,
-        out_specs=vmem,
+        in_specs=[vmem] * 16,
+        out_specs=pl.BlockSpec(memory_space=pltpu.HBM),
+        scratch_shapes=[
+            pltpu.VMEM((len(stencil_offsets), levels, levels), jnp.float32),
+            pltpu.SemaphoreType.DMA((len(stencil_offsets),)),
+        ],
         compiler_params=params,
     )(*near_args, corner_near, corner_far, *close, lon_smooth)
     return out[None, None]

time: 24.2 us -> 23.8 us (0.983)
  waiting for transfers between devices: 4 us -> 3.67 us
    pallas_call x1, Pallas kernels: 2.25 us -> 1.9 us  [local(): pl.pallas_call(coarse_kernel, out_shape=blocks(len(stencil_offsets)), in_...]
    ppermute x1, waiting for transfers between devices: 2.5 us -> 2.16 us  [local(): lax.ppermute(widened(True, lon_far, 0, 8000), 'lon', pair_near('lon'))]
    pallas_call x1, Pallas kernels: 1 us -> 1.33 us  [local(): pl.pallas_call(close_kernel, out_shape=(*(blocks(len(cells)) for cells in...]
  transfers between devices with their start and end apart: 8 -> 8, of which waited for: 3 -> 3; matrix products, arithmetic and copies ran while one was open for 0% -> 0% of each run, Pallas kernels for 6% -> 7%
where the time goes in v4:
time: 23.8 us; the launch traced here: 23.7 us
  starting transfers between devices  15.3 us (64%)
  Pallas kernels  4.64 us (19%)
  waiting for transfers between devices  3.67 us (15%)
    ppermute x1, starting transfers between devices, local(): lax.ppermute(widened(False, lon_near, 8, 1000), 'lon', pair_far_closed('l...  5.58 us
    ppermute x1, starting transfers between devices, local(): lon_far = lax.ppermute(to_far, 'lon', pair_far_closed('lon'))  3.54 us
    ppermute x1, starting transfers between devices, local(): lon_near = lax.ppermute(to_near, 'lon', pair_near('lon'))  3.03 us
    ppermute x1, waiting for transfers between devices, local(): lax.ppermute(widened(True, lon_far, 0, 8000), 'lon', pair_near('lon'))  2.16 us
    pallas_call x1, Pallas kernels, local(): pl.pallas_call(coarse_kernel, out_shape=blocks(len(stencil_offsets)), in_...  1.9 us
    ppermute x1, starting transfers between devices, local(): lat_near = lax.ppermute(both, 'lat', pair_near('lat'))  1.6 us
    ppermute x2, starting transfers between devices, exchange_lat_far(): return lax.ppermute(values, ('lon', 'lat'), pairs)  1.39 us
    pallas_call x1, Pallas kernels, local(): pl.pallas_call(close_kernel, out_shape=(*(blocks(len(cells)) for cells in...  1.33 us
  transfers between devices with their start and end apart: 8, of which 3 were waited for; matrix products, arithmetic and copies ran while one was open for 0% of the time, Pallas kernels for 7%

profile of v4, /device:TPU:0, one launch (start us, length us, event | category | flops | bytes accessed | tf_op | source)
XLA Modules:
  0.0 23.7 jit_solution(18324076817437744548)
XLA Ops:
  0.0 1.0 %shard_map.73 = (f32[544,128]{1,0:T(8,128)S(1)}, f32[288,128]{1,0:T(8,128)S(1)}, f32[288,128]{1,0:T(8,128)S(1)}) custom-call(f32[2,2,128,128]{3,2,1,0:T(8,128)} %inverse_hbm.1, f32[2,2,128]{2,1,0:T(2,128)} %diag_hbm.1, f32[2,2,128]{2,1,0:T(2,128)} %coup_hbm.1, f32[2,2,128]{2,1,0:T(2,128)} %east_hbm.1, f32[2,2,128]{2,1,0:T(2,128)} %north_hbm.1, ...), custom_call_target="tpu_custom_call" | custom-call | tf_op jit(solution)/shard_map/pallas_call | solution.py:486
  1.1 3.0 %collective-permute-start = (f32[288,128]{1,0:T(8,128)S(1)}, f32[288,128]{1,0:T(8,128)S(1)}, u32[]{:S(2)}, u32[]{:S(2)}) collective-permute-start(f32[288,128]{1,0:T(8,128)S(1)} %get-tuple-element.17), channel_id=1, source_target_pairs={{0,4},{4,0},{8,12},{12,8},{16,20},{20,16},{24,28},{28,24},{1,5},{5... | collective-permute-start | bytes 442376 | tf_op jit(solution)/shard_map/ppermute | solution.py:496
  4.1 3.5 %collective-permute-start.1 = (f32[288,128]{1,0:T(8,128)S(1)}, f32[288,128]{1,0:T(8,128)S(1)}, u32[]{:S(2)}, u32[]{:S(2)}) collective-permute-start(f32[288,128]{1,0:T(8,128)S(1)} %get-tuple-element.18), channel_id=1, source_target_pairs={{0,28},{4,8},{8,4},{12,16},{16,12},{20,24},{24,20},{28,0},{1,29},{... | collective-permute-start | bytes 442376 | tf_op jit(solution)/shard_map/ppermute | solution.py:497
  7.6 0.0 collective-permute-start.5
  7.6 1.6 %collective-permute-start.4 = (f32[544,128]{1,0:T(8,128)S(1)}, f32[544,128]{1,0:T(8,128)S(1)}, u32[]{:S(2)}, u32[]{:S(2)}) collective-permute-start(f32[544,128]{1,0:T(8,128)S(1)} %get-tuple-element.16.own.refs_0_), channel_id=1, source_target_pairs={{0,1},{1,0},{2,3},{3,2},{4,5},{5,4},{6,7},{7,6},{8,9},{9,8},{10,11... | collective-permute-start | bytes 835592 | tf_op jit(solution)/shard_map/ppermute | solution.py:498
  9.2 1.1 %collective-permute-done.ring.lon_near.refs_1_ = f32[288,128]{1,0:T(8,128)S(1)} collective-permute-done((f32[288,128]{1,0:T(8,128)S(1)}, f32[288,128]{1,0:T(8,128)S(1)}, u32[]{:S(2)}, u32[]{:S(2)}) %collective-permute-start) | collective-permute-done | bytes 147488 | tf_op jit(solution)/shard_map/ppermute | solution.py:496
  10.4 5.6 %collective-permute-start.3 = (f32[280,128]{1,0:T(8,128)S(1)}, f32[280,128]{1,0:T(8,128)S(1)}, u32[]{:S(2)}, u32[]{:S(2)}) collective-permute-start(f32[280,128]{1,0:T(8,128)S(1)} %shard_map.75), channel_id=1, source_target_pairs={{0,28},{4,8},{8,4},{12,16},{16,12},{20,24},{24,20},{28,0},{1,29},{... | collective-permute-start | bytes 430088 | tf_op jit(solution)/shard_map/ppermute | solution.py:511
  16.0 0.0 collective-permute-done.1.ring.lon_far.refs_2_
  16.0 0.1 collective-permute-start.2
  16.1 0.0 collective-permute-done.5.lat_far.refs_6_
  16.1 0.0 collective-permute-done.4.lat_near.refs_5_
  16.1 0.1 shard_map.76
  16.2 0.1 collective-permute-start.6
  16.2 1.4 %collective-permute-start.7 = (f32[352,128]{1,0:T(8,128)S(1)}, f32[352,128]{1,0:T(8,128)S(1)}, u32[]{:S(2)}, u32[]{:S(2)}) collective-permute-start(f32[352,128]{1,0:T(8,128)S(1)} %get-tuple-element.20), channel_id=1, source_target_pairs={{0,8},{1,2},{2,1},{3,11},{4,12},{5,6},{6,5},{7,15},{8,0},{9,10},{1... | collective-permute-start | bytes 540680 | tf_op jit(solution)/shard_map/ppermute | solution.py:50
  17.6 1.3 %shard_map.77 = (f32[12,128,128]{2,1,0:T(8,128)S(1)}, f32[4,128,128]{2,1,0:T(8,128)S(1)}, f32[5,128,128]{2,1,0:T(8,128)S(1)}, f32[8,128,128]{2,1,0:T(8,128)S(1)}...) custom-call(f32[544,128]{1,0:T(8,128)S(1)} %get-tuple-element.16.own.refs_0_, ...), custom_call_target="tpu_custom_call" | custom-call | flops 1000000 | bytes 1000 | tf_op jit(solution)/shard_map/pallas_call | solution.py:524
  19.0 2.2 %collective-permute-done.2.wide_near.refs_3_ = f32[272,128]{1,0:T(8,128)S(1)} collective-permute-done((f32[272,128]{1,0:T(8,128)S(1)}, f32[272,128]{1,0:T(8,128)S(1)}, u32[]{:S(2)}, u32[]{:S(2)}) %collective-permute-start.2) | collective-permute-done | bytes 139296 | tf_op jit(solution)/shard_map/ppermute | solution.py:512
  21.1 0.0 collective-permute-done.3.wide_far.refs_4_
  21.1 0.3 %shard_map.78.refs_15_ = f32[4,128,128]{2,1,0:T(8,128)S(1)} custom-call(f32[544,128]{1,0:T(8,128)S(1)} %get-tuple-element.16.own.refs_0_, f32[288,128]{1,0:T(8,128)S(1)} %collective-permute-done.ring.lon_near.refs_1_, f32[288,128]{1,0:T(8,128)S(1)} %collective-permute-done.1.ring.lon_far.refs_2_, f32[272,128]{1,0:T(8,128)S(1)} %collective-permute-done.2.wide_near.refs_3_, ...), custom_call_target="tpu_custom_call" | custom-call | flops 49999998976 | bytes 50000000 | tf_op jit(solution)/shard_map/pallas_call | solution.py:536
  21.4 0.0 collective-permute-done.6.refs_7_
  21.4 0.4 %collective-permute-done.7.refs_8_ = f32[352,128]{1,0:T(8,128)S(1)} collective-permute-done((f32[352,128]{1,0:T(8,128)S(1)}, f32[352,128]{1,0:T(8,128)S(1)}, u32[]{:S(2)}, u32[]{:S(2)}) %collective-permute-start.7) | collective-permute-done | bytes 180256 | tf_op jit(solution)/shard_map/ppermute | solution.py:50
  21.8 1.9 %shard_map.79 = f32[13,128,128]{2,1,0:T(8,128)} custom-call(f32[544,128]{1,0:T(8,128)S(1)} %get-tuple-element.16.own.refs_0_, f32[288,128]{1,0:T(8,128)S(1)} %collective-permute-done.ring.lon_near.refs_1_, f32[288,128]{1,0:T(8,128)S(1)} %collective-permute-done.1.ring.lon_far.refs_2_, f32[272,128]{1,0:T(8,128)S(1)} %collective-permute-done.2.wide_near.refs_3_, ...), custom_call_target="tpu_custom_call" | custom-call | tf_op jit(solution)/shard_map/pallas_call | solution.py:544
  (2 shorter events, 0.0 us)
Async XLA Ops:
  1.1 9.3 %collective-permute-start = (f32[288,128]{1,0:T(8,128)S(1)}, f32[288,128]{1,0:T(8,128)S(1)}, u32[]{:S(2)}, u32[]{:S(2)}) collective-permute-start(f32[288,128]{1,0:T(8,128)S(1)} %get-tuple-element.17), channel_id=1, source_target_pairs={{0,4},{4,0},{8,12},{12,8},{16,20},{20,16},{24,28},{28,24},{1,5},{5... | collective-permute-start | bytes 442376 | tf_op jit(solution)/shard_map/ppermute | solution.py:496
  4.1 11.9 %collective-permute-start.1 = (f32[288,128]{1,0:T(8,128)S(1)}, f32[288,128]{1,0:T(8,128)S(1)}, u32[]{:S(2)}, u32[]{:S(2)}) collective-permute-start(f32[288,128]{1,0:T(8,128)S(1)} %get-tuple-element.18), channel_id=1, source_target_pairs={{0,28},{4,8},{8,4},{12,16},{16,12},{20,24},{24,20},{28,0},{1,29},{... | collective-permute-start | bytes 442376 | tf_op jit(solution)/shard_map/ppermute | solution.py:497
  7.6 8.4 %collective-permute-start.5 = (f32[544,128]{1,0:T(8,128)S(1)}, f32[544,128]{1,0:T(8,128)S(1)}, u32[]{:S(2)}, u32[]{:S(2)}) collective-permute-start(f32[544,128]{1,0:T(8,128)S(1)} %get-tuple-element.16.own.refs_0_), channel_id=1, source_target_pairs={{0,8},{1,2},{2,1},{3,11},{4,12},{5,6},{6,5},{7,15},{8,0},{9,10},{1... | collective-permute-start | bytes 835592 | tf_op jit(solution)/shard_map/ppermute | solution.py:50
  7.6 8.5 %collective-permute-start.4 = (f32[544,128]{1,0:T(8,128)S(1)}, f32[544,128]{1,0:T(8,128)S(1)}, u32[]{:S(2)}, u32[]{:S(2)}) collective-permute-start(f32[544,128]{1,0:T(8,128)S(1)} %get-tuple-element.16.own.refs_0_), channel_id=1, source_target_pairs={{0,1},{1,0},{2,3},{3,2},{4,5},{5,4},{6,7},{7,6},{8,9},{9,8},{10,11... | collective-permute-start | bytes 835592 | tf_op jit(solution)/shard_map/ppermute | solution.py:498
  10.4 10.7 %collective-permute-start.3 = (f32[280,128]{1,0:T(8,128)S(1)}, f32[280,128]{1,0:T(8,128)S(1)}, u32[]{:S(2)}, u32[]{:S(2)}) collective-permute-start(f32[280,128]{1,0:T(8,128)S(1)} %shard_map.75), channel_id=1, source_target_pairs={{0,28},{4,8},{8,4},{12,16},{16,12},{20,24},{24,20},{28,0},{1,29},{... | collective-permute-start | bytes 430088 | tf_op jit(solution)/shard_map/ppermute | solution.py:511
  16.0 5.1 %collective-permute-start.2 = (f32[272,128]{1,0:T(8,128)S(1)}, f32[272,128]{1,0:T(8,128)S(1)}, u32[]{:S(2)}, u32[]{:S(2)}) collective-permute-start(f32[272,128]{1,0:T(8,128)S(1)} %shard_map.74), channel_id=1, source_target_pairs={{0,4},{4,0},{8,12},{12,8},{16,20},{20,16},{24,28},{28,24},{1,5},{5... | collective-permute-start | bytes 417800 | tf_op jit(solution)/shard_map/ppermute | solution.py:512
  16.2 5.3 %collective-permute-start.6 = (f32[352,128]{1,0:T(8,128)S(1)}, f32[352,128]{1,0:T(8,128)S(1)}, u32[]{:S(2)}, u32[]{:S(2)}) collective-permute-start(f32[352,128]{1,0:T(8,128)S(1)} %get-tuple-element.19), channel_id=1, source_target_pairs={{0,1},{1,0},{2,3},{3,2},{4,5},{5,4},{6,7},{7,6},{8,9},{9,8},{10,11... | collective-permute-start | bytes 540680 | tf_op jit(solution)/shard_map/ppermute | solution.py:521
  16.2 5.6 %collective-permute-start.7 = (f32[352,128]{1,0:T(8,128)S(1)}, f32[352,128]{1,0:T(8,128)S(1)}, u32[]{:S(2)}, u32[]{:S(2)}) collective-permute-start(f32[352,128]{1,0:T(8,128)S(1)} %get-tuple-element.20), channel_id=1, source_target_pairs={{0,8},{1,2},{2,1},{3,11},{4,12},{5,6},{6,5},{7,15},{8,0},{9,10},{1... | collective-permute-start | bytes 540680 | tf_op jit(solution)/shard_map/ppermute | solution.py:50

commit v5 on v4

--- a/solution.py
+++ b/solution.py
@@ -25,6 +25,7 @@
 ]
 DIAG, UP, DOWN, EAST, NORTH, OPEN, WEIGHT = range(7)
 COEF_ROWS = 8
+CORNER_ROWS = 2 * (COEF_ROWS + 2 * 4) + 2 * 4
 
 
 def pair_near(axis):
@@ -155,28 +156,39 @@
 def corner_kernel(lon_near, lon_far, lat_near, lat_far, to_near, to_far):
     even_lon, even_lat = parities()
     levels = lon_near.shape[1]
-    size = 4 * COEF_ROWS
-    lon = slice(2 * levels, 2 * levels + size)
-    lat = slice(4 * levels, 4 * levels + size)
-
-    def west(rows):
-        return jnp.where(even_lon, lon_far[rows, :], lon_near[rows, :])
-
-    def east(rows):
-        return jnp.where(even_lon, lon_near[rows, :], lon_far[rows, :])
-
-    low, high = slice(0, levels), slice(levels, 2 * levels)
     base = 2 * levels
+
+    def block(values, q, first=0):
+        return values[q * COEF_ROWS + first : q * COEF_ROWS + (WEIGHT + 1 if first else COEF_ROWS), :]
+
+    def sides(rows):
+        near, far = lon_near[rows, :], lon_far[rows, :]
+        return jnp.where(even_lon, far, near), jnp.where(even_lon, near, far)
+
+    low = sides(slice(0, levels))
+    high = sides(slice(levels, base))
+    coefs = sides(slice(base, lon_near.shape[0]))
+    lat = slice(2 * base, lat_near.shape[0])
     beyond = jnp.where(has_lat_far(), lat_far[lat, :], 0.0)
     for out, lower, other in (
         (to_near, jnp.logical_not(even_lat), beyond),
         (to_far, even_lat, lat_near[lat, :]),
     ):
-        out[:levels, :] = jnp.where(lower, west(low), west(high))
-        out[levels:base, :] = jnp.where(lower, east(low), east(high))
-        out[base : base + size, :] = west(lon)
-        out[base + size : base + 2 * size, :] = east(lon)
-        out[base + 2 * size : base + 3 * size, :] = other
+        rows = []
+        for place, facing in enumerate((1, 0)):
+            out[place * levels : (place + 1) * levels, :] = jnp.where(lower, low[place], high[place])
+            choices = []
+            for y in (0, 1):
+                corner, beside, behind = 2 * facing + y, 2 * (1 - facing) + y, 2 * facing + 1 - y
+                choices.append(
+                    [block(coefs[place], corner)]
+                    + [block(coefs[place], q, EAST) for q in (beside, behind)]
+                )
+            rows += [jnp.where(lower, *pair) for pair in zip(*choices)]
+        for x in (0, 1):
+            choices = (block(other, 2 * x + y, EAST) for y in (0, 1))
+            rows.append(jnp.where(lower, *choices))
+        out[base : base + CORNER_ROWS, :] = jnp.concatenate(rows, axis=0)
 
 
 def split(values):
@@ -221,15 +233,6 @@
             (0, 1): (even_lat, lat_near, lat_far, full),
             (0, -1): (even_lat, lat_far, lat_near, full),
         }
-        if corner_near is not None:
-            sources |= {
-                (-1, 1): (even_lat, corner_near, corner_far, half),
-                (-1, -1): (even_lat, corner_far, corner_near, half),
-                (1, 1): (even_lat, corner_near, corner_far, half + size),
-                (1, -1): (even_lat, corner_far, corner_near, half + size),
-                (0, 2): (even_lat, corner_near, corner_far, half + 2 * size),
-                (0, -2): (even_lat, corner_far, corner_near, half + 2 * size),
-            }
         self.sources = sources
         self.coefs = {place: self.fetch(*source, size) for place, source in sources.items()}
         far = has_lat_far()
@@ -238,6 +241,20 @@
             if place[1] != 0:
                 inside = keep[1 if place[1] > 0 else -1]
                 self.coefs[place] = jnp.where(inside, self.coefs[place], 0.0)
+        self.parts = {}
+        if corner_near is not None:
+            self.corners = {1: (even_lat, corner_near, corner_far), -1: (even_lat, corner_far, corner_near)}
+            for side, source in self.corners.items():
+                rows = jnp.where(keep[side], self.fetch(*source, half, CORNER_ROWS), 0.0)
+                facing, behind, beyond = (2, 3, 4) if side > 0 else (-1, -2, -3)
+                start = 0
+                for x, beside in ((-1, -2), (2, 3)):
+                    self.parts[x, facing] = (rows, start)
+                    self.parts[beside, facing] = (rows, start + COEF_ROWS - EAST)
+                    self.parts[x, behind] = (rows, start + COEF_ROWS + 4 - EAST)
+                    start += COEF_ROWS + 8
+                for x in (0, 1):
+                    self.parts[x, beyond] = (rows, start + 4 * x - EAST)
         pair = 2 * COEF_ROWS
         for x, source in self.wide.items() if wide_near is not None else ():
             beyond = self.fetch(*source, half, pair)
@@ -252,6 +269,9 @@
         return jnp.where(flag, first[start : start + count, :], other[start : start + count, :])
 
     def coef(self, x, y, row):
+        if (x, y) in self.parts:
+            rows, start = self.parts[x, y]
+            return rows[start + row : start + row + 1, :]
         at = (2 * (x % 2) + y % 2) * COEF_ROWS + row
         return self.coefs[x // 2, y // 2][at : at + 1, :]
 
@@ -301,7 +321,7 @@
         if x in self.wide:
             return self.fetch(*self.wide[x], y % 2 * levels, levels)
         if lon != 0 and lat != 0:
-            start = 0 if lon < 0 else levels
+            return self.fetch(*self.corners[lat], 0 if lon < 0 else levels, levels)
         elif lon != 0:
             start = y % 2 * levels
         else:
@@ -413,7 +433,7 @@
         rest = cells.residual(rows_t, x, y)
         sums.add((x // 2, y // 2), rest * cells.weight(x, y))
         if (x, y) in lat_far_cells:
-            smooth = product(rest, cells.inverse(x, y)) * relax_weight
+            smooth = product(rest, cells.inverse(x, y))
             smooth_out[lat_far_cells.index((x, y))] = smooth
     for place, (x, y) in enumerate(near_cells):
         rest_out[place] = cells.residual(rows_t, x, y, cells.inner_main)
@@ -425,51 +445,76 @@
     rows_t = {cell: rows_in[place] for place, cell in enumerate(reach_cells) if cell in lon_cells}
     for place, (x, y) in enumerate(lon_far_cells):
         rest = cells.residual(rows_t, x, y)
-        smooth_out[place] = product(rest, cells.inverse(x, y)) * relax_weight
-
-
-def targets_of(device, members):
-    return {device}.union(*(lateral_targets(*cell) for cell in members))
-
-
-last_group = {
-    target: device for device, members in groups.items() for target in targets_of(device, members)
-}
+        smooth_out[place] = product(rest, cells.inverse(x, y))
+
+
+product_cells = corner_cells + near_cells
+
+
+target_order = [(-2, 0), (2, 0), (0, -2), (0, 2)] + [
+    target for target in stencil_offsets if 2 not in target and -2 not in target
+]
 
 
 def coarse_kernel(*refs):
     cells = Stencil(*refs[:9])
-    rows_in, lat_smooth, partial, rest_in, high_in, low_in, lon_smooth, out, blocks, sems = refs[9:]
+    rows_in, lat_smooth, partial, rest_in, high_in, low_in, lon_smooth = refs[9:16]
+    out, blocks, rests, smooths, sems = refs[16:]
+    levels = cells.levels
     rows_t = {cell: rows_in[place] for place, cell in enumerate(reach_cells)}
-    sums = Sums(blocks, stencil_offsets)
-    for place, target in enumerate(first_targets):
-        sums.add(target, partial[place])
+    smooth_of, rest_of = {}, {}
+    for place, cell in enumerate(lon_far_cells):
+        smooth_of[cell] = lon_smooth.at[place]
+    for place, cell in enumerate(lat_far_cells):
+        smooth_of[cell] = lat_smooth.at[place]
+    for place, (x, y) in enumerate(product_cells):
+        if (x, y) in near_cells:
+            known = near_cells.index((x, y))
+            rest = rest_in[known] + rows_t[x, y] * cells.outer_face(x, y)
+            smooths[place] = product_of_parts(rest, high_in[known], low_in[known])
+        else:
+            rest = cells.residual(rows_t, x, y)
+            smooths[place] = product(rest, cells.inverse(x, y))
+        rests[place] = rest
+        rest_of[x, y], smooth_of[x, y] = rests.at[place], smooths.at[place]
+    lateral, own = {}, {}
+    for device, members in groups.items():
+        for x, y in members:
+            lon_target, lat_target = lateral_targets(x, y)
+            for target, faces in ((lon_target, cells.lon_faces), (lat_target, cells.lat_faces)):
+                lateral.setdefault(target, []).append(((x, y), faces(x, y)[1] * relax_weight))
+            weight = cells.weight(x, y) * relax_weight
+            factors = (
+                cells.own_diag(x, y) * relax_weight,
+                weight * cells.coef(x, y, UP),
+                weight * cells.coef(x, y, DOWN),
+            )
+            own.setdefault(device, []).append(((x, y), factors))
+    slots = {target: place for place, target in enumerate(stencil_offsets)}
     copies = []
-    for device, members in groups.items():
-        straight = parts = None
-        for x, y in members:
-            if (x, y) in lon_far_cells:
-                smooth = lon_smooth[lon_far_cells.index((x, y))]
-            elif (x, y) in lat_far_cells:
-                smooth = lat_smooth[lat_far_cells.index((x, y))]
-            else:
-                if (x, y) in near_cells:
-                    place = near_cells.index((x, y))
-                    rest = rest_in[place] + rows_t[x, y] * cells.outer_face(x, y)
-                    smooth = product_of_parts(rest, high_in[place], low_in[place])
-                else:
-                    rest = cells.residual(rows_t, x, y)
-                    smooth = product(rest, cells.inverse(x, y))
-                smooth = smooth * relax_weight
-                term = rest * cells.weight(x, y)
-                straight = term if straight is None else straight + term
-            parts = plus(parts, apply_columns(cells, sums, x, y, smooth))
-        sums.add(device, straight - parts[0] + left(parts[1]) + right(parts[2]))
-        for target, last in last_group.items():
-            if last == device:
-                place = sums.slots[target]
-                copies.append(pltpu.make_async_copy(blocks.at[place], out.at[place], sems.at[place]))
-                copies[-1].start()
+    strip = levels // 4
+    for target in target_order:
+        for start in range(0, levels, strip):
+            rows = slice(start, start + strip)
+            total = None
+            if target in first_targets:
+                total = partial[first_targets.index(target), rows, :]
+            for cell, factor in lateral.get(target, ()):
+                term = smooth_of[cell][rows, :] * factor
+                total = term if total is None else total + term
+            parts = None
+            for cell, factors in own.get(target, ()):
+                smooth = smooth_of[cell][rows, :]
+                terms = [smooth * factor for factor in factors]
+                if cell in rest_of:
+                    terms[0] = terms[0] - rest_of[cell][rows, :] * cells.weight(*cell)
+                parts = plus(parts, tuple(terms))
+            if parts is not None:
+                total = total - parts[0] + left(parts[1]) + right(parts[2])
+            blocks[slots[target], rows, :] = total
+        place = slots[target]
+        copies.append(pltpu.make_async_copy(blocks.at[place], out.at[place], sems.at[place]))
+        copies[-1].start()
     for copy in copies:
         copy.wait()
 
@@ -510,7 +555,7 @@
 
     wide_far = lax.ppermute(widened(False, lon_near, 8, 1000), "lon", pair_far_closed("lon"))
     wide_near = lax.ppermute(widened(True, lon_far, 0, 8000), "lon", pair_near("lon"))
-    corner_rows = 2 * levels + 3 * size
+    corner_rows = 2 * levels + CORNER_ROWS
     corner_to_near, corner_to_far = pl.pallas_call(
         corner_kernel,
         out_shape=(array(corner_rows), array(corner_rows)),
@@ -548,6 +593,7 @@
         out_specs=pl.BlockSpec(memory_space=pltpu.HBM),
         scratch_shapes=[
             pltpu.VMEM((len(stencil_offsets), levels, levels), jnp.float32),
+            *(pltpu.VMEM((len(product_cells), levels, levels), jnp.float32),) * 2,
             pltpu.SemaphoreType.DMA((len(stencil_offsets),)),
         ],
         compiler_params=params,

time: 23.8 us -> 23.4 us (0.983)
  waiting for transfers between devices: 3.67 us -> 3.38 us
    ppermute x2, waiting for transfers between devices: 0.38 us -> 0.08 us  [exchange_lat_far(): return lax.ppermute(values, ('lon', 'lat'), pairs)]
where the time goes in v5:
time: 23.4 us; the launch traced here: 23.2 us
  starting transfers between devices  15.3 us (65%)
  Pallas kernels  4.45 us (19%)
  waiting for transfers between devices  3.38 us (14%)
    ppermute x1, starting transfers between devices, local(): lax.ppermute(widened(False, lon_near, 8, 1000), 'lon', pair_far_closed('l...  5.58 us
    ppermute x1, starting transfers between devices, local(): lon_far = lax.ppermute(to_far, 'lon', pair_far_closed('lon'))  3.54 us
    ppermute x1, starting transfers between devices, local(): lon_near = lax.ppermute(to_near, 'lon', pair_near('lon'))  3.03 us
    ppermute x1, waiting for transfers between devices, local(): lax.ppermute(widened(True, lon_far, 0, 8000), 'lon', pair_near('lon'))  2.18 us
    pallas_call x1, Pallas kernels, local(): pl.pallas_call(coarse_kernel, out_shape=blocks(len(stencil_offsets)), in_...  1.73 us
    ppermute x1, starting transfers between devices, local(): lat_near = lax.ppermute(both, 'lat', pair_near('lat'))  1.6 us
    ppermute x2, starting transfers between devices, exchange_lat_far(): return lax.ppermute(values, ('lon', 'lat'), pairs)  1.39 us
    pallas_call x1, Pallas kernels, local(): pl.pallas_call(close_kernel, out_shape=(*(blocks(len(cells)) for cells in...  1.32 us
  transfers between devices with their start and end apart: 8, of which 3 were waited for; matrix products, arithmetic and copies ran while one was open for 0% of the time, Pallas kernels for 7%

profile of v5, /device:TPU:0, one launch (start us, length us, event | category | flops | bytes accessed | tf_op | source)
XLA Modules:
  0.0 23.2 jit_solution(4647695996767097979)
XLA Ops:
  0.0 1.0 %shard_map.73 = (f32[544,128]{1,0:T(8,128)S(1)}, f32[288,128]{1,0:T(8,128)S(1)}, f32[288,128]{1,0:T(8,128)S(1)}) custom-call(f32[2,2,128,128]{3,2,1,0:T(8,128)} %inverse_hbm.1, f32[2,2,128]{2,1,0:T(2,128)} %diag_hbm.1, f32[2,2,128]{2,1,0:T(2,128)} %coup_hbm.1, f32[2,2,128]{2,1,0:T(2,128)} %east_hbm.1, f32[2,2,128]{2,1,0:T(2,128)} %north_hbm.1, ...), custom_call_target="tpu_custom_call" | custom-call | tf_op jit(solution)/shard_map/pallas_call | solution.py:531
  1.1 3.0 %collective-permute-start = (f32[288,128]{1,0:T(8,128)S(1)}, f32[288,128]{1,0:T(8,128)S(1)}, u32[]{:S(2)}, u32[]{:S(2)}) collective-permute-start(f32[288,128]{1,0:T(8,128)S(1)} %get-tuple-element.17), channel_id=1, source_target_pairs={{0,4},{4,0},{8,12},{12,8},{16,20},{20,16},{24,28},{28,24},{1,5},{5... | collective-permute-start | bytes 442376 | tf_op jit(solution)/shard_map/ppermute | solution.py:541
  4.1 3.5 %collective-permute-start.1 = (f32[288,128]{1,0:T(8,128)S(1)}, f32[288,128]{1,0:T(8,128)S(1)}, u32[]{:S(2)}, u32[]{:S(2)}) collective-permute-start(f32[288,128]{1,0:T(8,128)S(1)} %get-tuple-element.18), channel_id=1, source_target_pairs={{0,28},{4,8},{8,4},{12,16},{16,12},{20,24},{24,20},{28,0},{1,29},{... | collective-permute-start | bytes 442376 | tf_op jit(solution)/shard_map/ppermute | solution.py:542
  7.6 0.0 collective-permute-start.5
  7.6 1.6 %collective-permute-start.4 = (f32[544,128]{1,0:T(8,128)S(1)}, f32[544,128]{1,0:T(8,128)S(1)}, u32[]{:S(2)}, u32[]{:S(2)}) collective-permute-start(f32[544,128]{1,0:T(8,128)S(1)} %get-tuple-element.16.own.refs_0_), channel_id=1, source_target_pairs={{0,1},{1,0},{2,3},{3,2},{4,5},{5,4},{6,7},{7,6},{8,9},{9,8},{10,11... | collective-permute-start | bytes 835592 | tf_op jit(solution)/shard_map/ppermute | solution.py:543
  9.2 1.1 %collective-permute-done.ring.lon_near.refs_1_ = f32[288,128]{1,0:T(8,128)S(1)} collective-permute-done((f32[288,128]{1,0:T(8,128)S(1)}, f32[288,128]{1,0:T(8,128)S(1)}, u32[]{:S(2)}, u32[]{:S(2)}) %collective-permute-start) | collective-permute-done | bytes 147488 | tf_op jit(solution)/shard_map/ppermute | solution.py:541
  10.4 5.6 %collective-permute-start.3 = (f32[280,128]{1,0:T(8,128)S(1)}, f32[280,128]{1,0:T(8,128)S(1)}, u32[]{:S(2)}, u32[]{:S(2)}) collective-permute-start(f32[280,128]{1,0:T(8,128)S(1)} %shard_map.75), channel_id=1, source_target_pairs={{0,28},{4,8},{8,4},{12,16},{16,12},{20,24},{24,20},{28,0},{1,29},{... | collective-permute-start | bytes 430088 | tf_op jit(solution)/shard_map/ppermute | solution.py:556
  16.0 0.0 collective-permute-done.1.ring.lon_far.refs_2_
  16.0 0.1 collective-permute-start.2
  16.1 0.0 collective-permute-done.5.lat_far.refs_6_
  16.1 0.0 collective-permute-done.4.lat_near.refs_5_
  16.1 0.1 shard_map.76
  16.2 0.1 collective-permute-start.6
  16.2 1.4 %collective-permute-start.7 = (f32[296,128]{1,0:T(8,128)S(1)}, f32[296,128]{1,0:T(8,128)S(1)}, u32[]{:S(2)}, u32[]{:S(2)}) collective-permute-start(f32[296,128]{1,0:T(8,128)S(1)} %get-tuple-element.20), channel_id=1, source_target_pairs={{0,8},{1,2},{2,1},{3,11},{4,12},{5,6},{6,5},{7,15},{8,0},{9,10},{1... | collective-permute-start | bytes 454664 | tf_op jit(solution)/shard_map/ppermute | solution.py:51
  17.6 1.3 %shard_map.77 = (f32[12,128,128]{2,1,0:T(8,128)S(1)}, f32[4,128,128]{2,1,0:T(8,128)S(1)}, f32[5,128,128]{2,1,0:T(8,128)S(1)}, f32[8,128,128]{2,1,0:T(8,128)S(1)}...) custom-call(f32[544,128]{1,0:T(8,128)S(1)} %get-tuple-element.16.own.refs_0_, ...), custom_call_target="tpu_custom_call" | custom-call | flops 1000000 | bytes 1000 | tf_op jit(solution)/shard_map/pallas_call | solution.py:569
  18.9 2.2 %collective-permute-done.2.wide_near.refs_3_ = f32[272,128]{1,0:T(8,128)S(1)} collective-permute-done((f32[272,128]{1,0:T(8,128)S(1)}, f32[272,128]{1,0:T(8,128)S(1)}, u32[]{:S(2)}, u32[]{:S(2)}) %collective-permute-start.2) | collective-permute-done | bytes 139296 | tf_op jit(solution)/shard_map/ppermute | solution.py:557
  21.1 0.0 collective-permute-done.3.wide_far.refs_4_
  21.1 0.3 %shard_map.78.refs_15_ = f32[4,128,128]{2,1,0:T(8,128)S(1)} custom-call(f32[544,128]{1,0:T(8,128)S(1)} %get-tuple-element.16.own.refs_0_, f32[288,128]{1,0:T(8,128)S(1)} %collective-permute-done.ring.lon_near.refs_1_, f32[288,128]{1,0:T(8,128)S(1)} %collective-permute-done.1.ring.lon_far.refs_2_, f32[272,128]{1,0:T(8,128)S(1)} %collective-permute-done.2.wide_near.refs_3_, ...), custom_call_target="tpu_custom_call" | custom-call | flops 49999998976 | bytes 50000000 | tf_op jit(solution)/shard_map/pallas_call | solution.py:581
  21.4 0.0 collective-permute-done.6.refs_7_
  21.4 0.1 collective-permute-done.7.refs_8_
  21.5 1.7 %shard_map.79 = f32[13,128,128]{2,1,0:T(8,128)} custom-call(f32[544,128]{1,0:T(8,128)S(1)} %get-tuple-element.16.own.refs_0_, f32[288,128]{1,0:T(8,128)S(1)} %collective-permute-done.ring.lon_near.refs_1_, f32[288,128]{1,0:T(8,128)S(1)} %collective-permute-done.1.ring.lon_far.refs_2_, f32[272,128]{1,0:T(8,128)S(1)} %collective-permute-done.2.wide_near.refs_3_, ...), custom_call_target="tpu_custom_call" | custom-call | tf_op jit(solution)/shard_map/pallas_call | solution.py:589
  (2 shorter events, 0.0 us)
Async XLA Ops:
  1.1 9.3 %collective-permute-start = (f32[288,128]{1,0:T(8,128)S(1)}, f32[288,128]{1,0:T(8,128)S(1)}, u32[]{:S(2)}, u32[]{:S(2)}) collective-permute-start(f32[288,128]{1,0:T(8,128)S(1)} %get-tuple-element.17), channel_id=1, source_target_pairs={{0,4},{4,0},{8,12},{12,8},{16,20},{20,16},{24,28},{28,24},{1,5},{5... | collective-permute-start | bytes 442376 | tf_op jit(solution)/shard_map/ppermute | solution.py:541
  4.1 11.9 %collective-permute-start.1 = (f32[288,128]{1,0:T(8,128)S(1)}, f32[288,128]{1,0:T(8,128)S(1)}, u32[]{:S(2)}, u32[]{:S(2)}) collective-permute-start(f32[288,128]{1,0:T(8,128)S(1)} %get-tuple-element.18), channel_id=1, source_target_pairs={{0,28},{4,8},{8,4},{12,16},{16,12},{20,24},{24,20},{28,0},{1,29},{... | collective-permute-start | bytes 442376 | tf_op jit(solution)/shard_map/ppermute | solution.py:542
  7.6 8.4 %collective-permute-start.5 = (f32[544,128]{1,0:T(8,128)S(1)}, f32[544,128]{1,0:T(8,128)S(1)}, u32[]{:S(2)}, u32[]{:S(2)}) collective-permute-start(f32[544,128]{1,0:T(8,128)S(1)} %get-tuple-element.16.own.refs_0_), channel_id=1, source_target_pairs={{0,8},{1,2},{2,1},{3,11},{4,12},{5,6},{6,5},{7,15},{8,0},{9,10},{1... | collective-permute-start | bytes 835592 | tf_op jit(solution)/shard_map/ppermute | solution.py:51
  7.6 8.5 %collective-permute-start.4 = (f32[544,128]{1,0:T(8,128)S(1)}, f32[544,128]{1,0:T(8,128)S(1)}, u32[]{:S(2)}, u32[]{:S(2)}) collective-permute-start(f32[544,128]{1,0:T(8,128)S(1)} %get-tuple-element.16.own.refs_0_), channel_id=1, source_target_pairs={{0,1},{1,0},{2,3},{3,2},{4,5},{5,4},{6,7},{7,6},{8,9},{9,8},{10,11... | collective-permute-start | bytes 835592 | tf_op jit(solution)/shard_map/ppermute | solution.py:543
  10.4 10.7 %collective-permute-start.3 = (f32[280,128]{1,0:T(8,128)S(1)}, f32[280,128]{1,0:T(8,128)S(1)}, u32[]{:S(2)}, u32[]{:S(2)}) collective-permute-start(f32[280,128]{1,0:T(8,128)S(1)} %shard_map.75), channel_id=1, source_target_pairs={{0,28},{4,8},{8,4},{12,16},{16,12},{20,24},{24,20},{28,0},{1,29},{... | collective-permute-start | bytes 430088 | tf_op jit(solution)/shard_map/ppermute | solution.py:556
  16.0 5.1 %collective-permute-start.2 = (f32[272,128]{1,0:T(8,128)S(1)}, f32[272,128]{1,0:T(8,128)S(1)}, u32[]{:S(2)}, u32[]{:S(2)}) collective-permute-start(f32[272,128]{1,0:T(8,128)S(1)} %shard_map.74), channel_id=1, source_target_pairs={{0,4},{4,0},{8,12},{12,8},{16,20},{20,16},{24,28},{28,24},{1,5},{5... | collective-permute-start | bytes 417800 | tf_op jit(solution)/shard_map/ppermute | solution.py:557
  16.2 5.2 %collective-permute-start.6 = (f32[296,128]{1,0:T(8,128)S(1)}, f32[296,128]{1,0:T(8,128)S(1)}, u32[]{:S(2)}, u32[]{:S(2)}) collective-permute-start(f32[296,128]{1,0:T(8,128)S(1)} %get-tuple-element.19), channel_id=1, source_target_pairs={{0,1},{1,0},{2,3},{3,2},{4,5},{5,4},{6,7},{7,6},{8,9},{9,8},{10,11... | collective-permute-start | bytes 454664 | tf_op jit(solution)/shard_map/ppermute | solution.py:566
  16.2 5.3 %collective-permute-start.7 = (f32[296,128]{1,0:T(8,128)S(1)}, f32[296,128]{1,0:T(8,128)S(1)}, u32[]{:S(2)}, u32[]{:S(2)}) collective-permute-start(f32[296,128]{1,0:T(8,128)S(1)} %get-tuple-element.20), channel_id=1, source_target_pairs={{0,8},{1,2},{2,1},{3,11},{4,12},{5,6},{6,5},{7,15},{8,0},{9,10},{1... | collective-permute-start | bytes 454664 | tf_op jit(solution)/shard_map/ppermute | solution.py:51

commit v6 on v5

--- a/solution.py
+++ b/solution.py
@@ -153,7 +153,7 @@
         wide[base + y * COEF_ROWS : base + (y + 1) * COEF_ROWS, :] = beyond
 
 
-def corner_kernel(lon_near, lon_far, lat_near, lat_far, to_near, to_far):
+def fill_corner(lon_near, lon_far, lat_near, lat_far, out, near):
     even_lon, even_lat = parities()
     levels = lon_near.shape[1]
     base = 2 * levels
@@ -169,26 +169,27 @@
     high = sides(slice(levels, base))
     coefs = sides(slice(base, lon_near.shape[0]))
     lat = slice(2 * base, lat_near.shape[0])
-    beyond = jnp.where(has_lat_far(), lat_far[lat, :], 0.0)
-    for out, lower, other in (
-        (to_near, jnp.logical_not(even_lat), beyond),
-        (to_far, even_lat, lat_near[lat, :]),
-    ):
-        rows = []
-        for place, facing in enumerate((1, 0)):
-            out[place * levels : (place + 1) * levels, :] = jnp.where(lower, low[place], high[place])
-            choices = []
-            for y in (0, 1):
-                corner, beside, behind = 2 * facing + y, 2 * (1 - facing) + y, 2 * facing + 1 - y
-                choices.append(
-                    [block(coefs[place], corner)]
-                    + [block(coefs[place], q, EAST) for q in (beside, behind)]
-                )
-            rows += [jnp.where(lower, *pair) for pair in zip(*choices)]
-        for x in (0, 1):
-            choices = (block(other, 2 * x + y, EAST) for y in (0, 1))
-            rows.append(jnp.where(lower, *choices))
-        out[base : base + CORNER_ROWS, :] = jnp.concatenate(rows, axis=0)
+    lower = jnp.logical_not(even_lat) if near else even_lat
+    other = jnp.where(has_lat_far(), lat_far[lat, :], 0.0) if near else lat_near[lat, :]
+    rows = []
+    for place, facing in enumerate((1, 0)):
+        out[place * levels : (place + 1) * levels, :] = jnp.where(lower, low[place], high[place])
+        choices = []
+        for y in (0, 1):
+            corner, beside, behind = 2 * facing + y, 2 * (1 - facing) + y, 2 * facing + 1 - y
+            choices.append(
+                [block(coefs[place], corner)]
+                + [block(coefs[place], q, EAST) for q in (beside, behind)]
+            )
+        rows += [jnp.where(lower, *pair) for pair in zip(*choices)]
+    for x in (0, 1):
+        choices = (block(other, 2 * x + y, EAST) for y in (0, 1))
+        rows.append(jnp.where(lower, *choices))
+    out[base : base + CORNER_ROWS, :] = jnp.concatenate(rows, axis=0)
+
+
+def corner_kernel(lon_near, lon_far, lat_near, lat_far, to_far):
+    fill_corner(lon_near, lon_far, lat_near, lat_far, to_far, False)
 
 
 def split(values):
@@ -400,7 +401,8 @@
     return more if parts is None else tuple(a + b for a, b in zip(parts, more))
 
 
-def close_kernel(own, lon_near, lon_far, lat_near, lat_far, rows_out, smooth_out, partial, rest_out, high_out, low_out):
+def close_kernel(own, lon_near, lon_far, lat_near, lat_far, rows_out, smooth_out, partial, rest_out, high_out, low_out, to_near):
+    fill_corner(lon_near, lon_far, lat_near, lat_far, to_near, True)
     cells = Stencil(own, lon_near, lon_far, None, None, lat_near, lat_far)
     levels = cells.levels
     row = lax.broadcasted_iota(jnp.int32, (levels, levels), 0)
@@ -556,27 +558,28 @@
     wide_far = lax.ppermute(widened(False, lon_near, 8, 1000), "lon", pair_far_closed("lon"))
     wide_near = lax.ppermute(widened(True, lon_far, 0, 8000), "lon", pair_near("lon"))
     corner_rows = 2 * levels + CORNER_ROWS
-    corner_to_near, corner_to_far = pl.pallas_call(
+    corner_to_far = pl.pallas_call(
         corner_kernel,
-        out_shape=(array(corner_rows), array(corner_rows)),
+        out_shape=array(corner_rows),
         in_specs=[vmem] * 4,
-        out_specs=(vmem, vmem),
+        out_specs=vmem,
         compiler_params=params,
     )(lon_near, lon_far, lat_near, lat_far)
-    corner_near = lax.ppermute(corner_to_near, "lat", pair_near("lat"))
     corner_far = exchange_lat_far(corner_to_far)
     blocks = lambda count: jax.ShapeDtypeStruct((count, levels, levels), jnp.float32)
-    close = pl.pallas_call(
+    *close, corner_to_near = pl.pallas_call(
         close_kernel,
         out_shape=(
             *(blocks(len(cells)) for cells in (reach_cells, lat_far_cells, first_targets, near_cells)),
             *(jax.ShapeDtypeStruct((len(near_cells), levels, levels), jnp.bfloat16),) * 2,
+            array(corner_rows),
         ),
         in_specs=[vmem] * 5,
-        out_specs=(vmem,) * 6,
+        out_specs=(vmem,) * 7,
         cost_estimate=cost(1),
         compiler_params=params,
     )(both, lon_near, lon_far, lat_near, lat_far)
+    corner_near = lax.ppermute(corner_to_near, "lat", pair_near("lat"))
     near_args = (both, lon_near, lon_far, wide_near, wide_far, lat_near, lat_far)
     lon_smooth = pl.pallas_call(
         wide_products_kernel,

time: 23.4 us -> 23.3 us (level)
  transfers between devices with their start and end apart: 8 -> 8, of which waited for: 3 -> 2; matrix products, arithmetic and copies ran while one was open for 0% -> 0% of each run, Pallas kernels for 7% -> 7%
where the time goes in v6:
time: 23.3 us; the launch traced here: 23.2 us
  starting transfers between devices  15.3 us (66%)
  Pallas kernels  4.46 us (19%)
  waiting for transfers between devices  3.31 us (14%)
    ppermute x1, starting transfers between devices, local(): lax.ppermute(widened(False, lon_near, 8, 1000), 'lon', pair_far_closed('l...  5.58 us
    ppermute x1, starting transfers between devices, local(): lon_far = lax.ppermute(to_far, 'lon', pair_far_closed('lon'))  3.54 us
    ppermute x1, starting transfers between devices, local(): lon_near = lax.ppermute(to_near, 'lon', pair_near('lon'))  3.03 us
    ppermute x1, waiting for transfers between devices, local(): lax.ppermute(widened(True, lon_far, 0, 8000), 'lon', pair_near('lon'))  2.18 us
    pallas_call x1, Pallas kernels, local(): pl.pallas_call(coarse_kernel, out_shape=blocks(len(stencil_offsets)), in_...  1.74 us
    ppermute x1, starting transfers between devices, local(): lat_near = lax.ppermute(both, 'lat', pair_near('lat'))  1.6 us
    ppermute x2, starting transfers between devices, exchange_lat_far(): return lax.ppermute(values, ('lon', 'lat'), pairs)  1.39 us
    pallas_call x1, Pallas kernels, local(): pl.pallas_call(close_kernel, out_shape=(*(blocks(len(cells)) for cells in...  1.32 us
  transfers between devices with their start and end apart: 8, of which 2 were waited for; matrix products, arithmetic and copies ran while one was open for 0% of the time, Pallas kernels for 7%

profile of v6, /device:TPU:0, one launch (start us, length us, event | category | flops | bytes accessed | tf_op | source)
XLA Modules:
  0.0 23.2 jit_solution(12807535764110723511)
XLA Ops:
  0.0 1.0 %shard_map.73 = (f32[544,128]{1,0:T(8,128)S(1)}, f32[288,128]{1,0:T(8,128)S(1)}, f32[288,128]{1,0:T(8,128)S(1)}) custom-call(f32[2,2,128,128]{3,2,1,0:T(8,128)} %inverse_hbm.1, f32[2,2,128]{2,1,0:T(2,128)} %diag_hbm.1, f32[2,2,128]{2,1,0:T(2,128)} %coup_hbm.1, f32[2,2,128]{2,1,0:T(2,128)} %east_hbm.1, f32[2,2,128]{2,1,0:T(2,128)} %north_hbm.1, ...), custom_call_target="tpu_custom_call" | custom-call | tf_op jit(solution)/shard_map/pallas_call | solution.py:533
  1.1 3.0 %collective-permute-start = (f32[288,128]{1,0:T(8,128)S(1)}, f32[288,128]{1,0:T(8,128)S(1)}, u32[]{:S(2)}, u32[]{:S(2)}) collective-permute-start(f32[288,128]{1,0:T(8,128)S(1)} %get-tuple-element.16), channel_id=1, source_target_pairs={{0,4},{4,0},{8,12},{12,8},{16,20},{20,16},{24,28},{28,24},{1,5},{5... | collective-permute-start | bytes 442376 | tf_op jit(solution)/shard_map/ppermute | solution.py:543
  4.1 3.5 %collective-permute-start.1 = (f32[288,128]{1,0:T(8,128)S(1)}, f32[288,128]{1,0:T(8,128)S(1)}, u32[]{:S(2)}, u32[]{:S(2)}) collective-permute-start(f32[288,128]{1,0:T(8,128)S(1)} %get-tuple-element.17), channel_id=1, source_target_pairs={{0,28},{4,8},{8,4},{12,16},{16,12},{20,24},{24,20},{28,0},{1,29},{... | collective-permute-start | bytes 442376 | tf_op jit(solution)/shard_map/ppermute | solution.py:544
  7.6 0.0 collective-permute-start.5
  7.6 1.6 %collective-permute-start.4 = (f32[544,128]{1,0:T(8,128)S(1)}, f32[544,128]{1,0:T(8,128)S(1)}, u32[]{:S(2)}, u32[]{:S(2)}) collective-permute-start(f32[544,128]{1,0:T(8,128)S(1)} %get-tuple-element.15.own.refs_0_), channel_id=1, source_target_pairs={{0,1},{1,0},{2,3},{3,2},{4,5},{5,4},{6,7},{7,6},{8,9},{9,8},{10,11... | collective-permute-start | bytes 835592 | tf_op jit(solution)/shard_map/ppermute | solution.py:545
  9.2 1.1 %collective-permute-done.ring.lon_near.refs_1_ = f32[288,128]{1,0:T(8,128)S(1)} collective-permute-done((f32[288,128]{1,0:T(8,128)S(1)}, f32[288,128]{1,0:T(8,128)S(1)}, u32[]{:S(2)}, u32[]{:S(2)}) %collective-permute-start) | collective-permute-done | bytes 147488 | tf_op jit(solution)/shard_map/ppermute | solution.py:543
  10.4 5.6 %collective-permute-start.3 = (f32[280,128]{1,0:T(8,128)S(1)}, f32[280,128]{1,0:T(8,128)S(1)}, u32[]{:S(2)}, u32[]{:S(2)}) collective-permute-start(f32[280,128]{1,0:T(8,128)S(1)} %shard_map.75), channel_id=1, source_target_pairs={{0,28},{4,8},{8,4},{12,16},{16,12},{20,24},{24,20},{28,0},{1,29},{... | collective-permute-start | bytes 430088 | tf_op jit(solution)/shard_map/ppermute | solution.py:558
  16.0 0.0 collective-permute-done.1.ring.lon_far.refs_2_
  16.0 0.1 collective-permute-start.2
  16.1 0.0 collective-permute-done.5.lat_far.refs_6_
  16.1 0.0 collective-permute-done.4.lat_near.refs_5_
  16.1 1.4 %collective-permute-start.7 = (f32[296,128]{1,0:T(8,128)S(1)}, f32[296,128]{1,0:T(8,128)S(1)}, u32[]{:S(2)}, u32[]{:S(2)}) collective-permute-start(f32[296,128]{1,0:T(8,128)S(1)} %shard_map.77), channel_id=1, source_target_pairs={{0,8},{1,2},{2,1},{3,11},{4,12},{5,6},{6,5},{7,15},{8,0},{9,10},{1... | collective-permute-start | bytes 454664 | tf_op jit(solution)/shard_map/ppermute | solution.py:51
  17.5 1.3 %shard_map.76 = (f32[12,128,128]{2,1,0:T(8,128)S(1)}, f32[4,128,128]{2,1,0:T(8,128)S(1)}, f32[5,128,128]{2,1,0:T(8,128)S(1)}, f32[8,128,128]{2,1,0:T(8,128)S(1)}...) custom-call(f32[544,128]{1,0:T(8,128)S(1)} %get-tuple-element.15.own.refs_0_, ...), custom_call_target="tpu_custom_call" | custom-call | flops 1000000 | bytes 1000 | tf_op jit(solution)/shard_map/pallas_call | solution.py:570
  18.9 0.1 collective-permute-start.6
  18.9 2.2 %collective-permute-done.2.wide_near.refs_3_ = f32[272,128]{1,0:T(8,128)S(1)} collective-permute-done((f32[272,128]{1,0:T(8,128)S(1)}, f32[272,128]{1,0:T(8,128)S(1)}, u32[]{:S(2)}, u32[]{:S(2)}) %collective-permute-start.2) | collective-permute-done | bytes 139296 | tf_op jit(solution)/shard_map/ppermute | solution.py:559
  21.1 0.0 collective-permute-done.3.wide_far.refs_4_
  21.1 0.3 %shard_map.78.refs_15_ = f32[4,128,128]{2,1,0:T(8,128)S(1)} custom-call(f32[544,128]{1,0:T(8,128)S(1)} %get-tuple-element.15.own.refs_0_, f32[288,128]{1,0:T(8,128)S(1)} %collective-permute-done.ring.lon_near.refs_1_, f32[288,128]{1,0:T(8,128)S(1)} %collective-permute-done.1.ring.lon_far.refs_2_, f32[272,128]{1,0:T(8,128)S(1)} %collective-permute-done.2.wide_near.refs_3_, ...), custom_call_target="tpu_custom_call" | custom-call | flops 49999998976 | bytes 50000000 | tf_op jit(solution)/shard_map/pallas_call | solution.py:584
  21.4 0.0 collective-permute-done.7.refs_8_
  21.4 0.0 collective-permute-done.6.refs_7_
  21.4 1.7 %shard_map.79 = f32[13,128,128]{2,1,0:T(8,128)} custom-call(f32[544,128]{1,0:T(8,128)S(1)} %get-tuple-element.15.own.refs_0_, f32[288,128]{1,0:T(8,128)S(1)} %collective-permute-done.ring.lon_near.refs_1_, f32[288,128]{1,0:T(8,128)S(1)} %collective-permute-done.1.ring.lon_far.refs_2_, f32[272,128]{1,0:T(8,128)S(1)} %collective-permute-done.2.wide_near.refs_3_, ...), custom_call_target="tpu_custom_call" | custom-call | tf_op jit(solution)/shard_map/pallas_call | solution.py:592
  (3 shorter events, 0.1 us)
Async XLA Ops:
  1.1 9.3 %collective-permute-start = (f32[288,128]{1,0:T(8,128)S(1)}, f32[288,128]{1,0:T(8,128)S(1)}, u32[]{:S(2)}, u32[]{:S(2)}) collective-permute-start(f32[288,128]{1,0:T(8,128)S(1)} %get-tuple-element.16), channel_id=1, source_target_pairs={{0,4},{4,0},{8,12},{12,8},{16,20},{20,16},{24,28},{28,24},{1,5},{5... | collective-permute-start | bytes 442376 | tf_op jit(solution)/shard_map/ppermute | solution.py:543
  4.1 11.9 %collective-permute-start.1 = (f32[288,128]{1,0:T(8,128)S(1)}, f32[288,128]{1,0:T(8,128)S(1)}, u32[]{:S(2)}, u32[]{:S(2)}) collective-permute-start(f32[288,128]{1,0:T(8,128)S(1)} %get-tuple-element.17), channel_id=1, source_target_pairs={{0,28},{4,8},{8,4},{12,16},{16,12},{20,24},{24,20},{28,0},{1,29},{... | collective-permute-start | bytes 442376 | tf_op jit(solution)/shard_map/ppermute | solution.py:544
  7.6 8.4 %collective-permute-start.5 = (f32[544,128]{1,0:T(8,128)S(1)}, f32[544,128]{1,0:T(8,128)S(1)}, u32[]{:S(2)}, u32[]{:S(2)}) collective-permute-start(f32[544,128]{1,0:T(8,128)S(1)} %get-tuple-element.15.own.refs_0_), channel_id=1, source_target_pairs={{0,8},{1,2},{2,1},{3,11},{4,12},{5,6},{6,5},{7,15},{8,0},{9,10},{1... | collective-permute-start | bytes 835592 | tf_op jit(solution)/shard_map/ppermute | solution.py:51
  7.6 8.5 %collective-permute-start.4 = (f32[544,128]{1,0:T(8,128)S(1)}, f32[544,128]{1,0:T(8,128)S(1)}, u32[]{:S(2)}, u32[]{:S(2)}) collective-permute-start(f32[544,128]{1,0:T(8,128)S(1)} %get-tuple-element.15.own.refs_0_), channel_id=1, source_target_pairs={{0,1},{1,0},{2,3},{3,2},{4,5},{5,4},{6,7},{7,6},{8,9},{9,8},{10,11... | collective-permute-start | bytes 835592 | tf_op jit(solution)/shard_map/ppermute | solution.py:545
  10.4 10.7 %collective-permute-start.3 = (f32[280,128]{1,0:T(8,128)S(1)}, f32[280,128]{1,0:T(8,128)S(1)}, u32[]{:S(2)}, u32[]{:S(2)}) collective-permute-start(f32[280,128]{1,0:T(8,128)S(1)} %shard_map.75), channel_id=1, source_target_pairs={{0,28},{4,8},{8,4},{12,16},{16,12},{20,24},{24,20},{28,0},{1,29},{... | collective-permute-start | bytes 430088 | tf_op jit(solution)/shard_map/ppermute | solution.py:558
  16.0 5.1 %collective-permute-start.2 = (f32[272,128]{1,0:T(8,128)S(1)}, f32[272,128]{1,0:T(8,128)S(1)}, u32[]{:S(2)}, u32[]{:S(2)}) collective-permute-start(f32[272,128]{1,0:T(8,128)S(1)} %shard_map.74), channel_id=1, source_target_pairs={{0,4},{4,0},{8,12},{12,8},{16,20},{20,16},{24,28},{28,24},{1,5},{5... | collective-permute-start | bytes 417800 | tf_op jit(solution)/shard_map/ppermute | solution.py:559
  16.1 5.3 %collective-permute-start.7 = (f32[296,128]{1,0:T(8,128)S(1)}, f32[296,128]{1,0:T(8,128)S(1)}, u32[]{:S(2)}, u32[]{:S(2)}) collective-permute-start(f32[296,128]{1,0:T(8,128)S(1)} %shard_map.77), channel_id=1, source_target_pairs={{0,8},{1,2},{2,1},{3,11},{4,12},{5,6},{6,5},{7,15},{8,0},{9,10},{1... | collective-permute-start | bytes 454664 | tf_op jit(solution)/shard_map/ppermute | solution.py:51
  18.9 2.6 %collective-permute-start.6 = (f32[296,128]{1,0:T(8,128)S(1)}, f32[296,128]{1,0:T(8,128)S(1)}, u32[]{:S(2)}, u32[]{:S(2)}) collective-permute-start(f32[296,128]{1,0:T(8,128)S(1)} %get-tuple-element.18), channel_id=1, source_target_pairs={{0,1},{1,0},{2,3},{3,2},{4,5},{5,4},{6,7},{7,6},{8,9},{9,8},{10,11... | collective-permute-start | bytes 454664 | tf_op jit(solution)/shard_map/ppermute | solution.py:582

commit v7 on v6

--- a/solution.py
+++ b/solution.py
@@ -555,7 +555,7 @@
             compiler_params=params,
         )(both, ring)
 
-    wide_far = lax.ppermute(widened(False, lon_near, 8, 1000), "lon", pair_far_closed("lon"))
+    wide_far = lax.ppermute(widened(False, lon_near, 0, 1000), "lon", pair_far_closed("lon"))
     wide_near = lax.ppermute(widened(True, lon_far, 0, 8000), "lon", pair_near("lon"))
     corner_rows = 2 * levels + CORNER_ROWS
     corner_to_far = pl.pallas_call(

time: 23.3 us -> 23.3 us (level)
  transfers between devices with their start and end apart: 8 -> 8, of which waited for: 2 -> 3; matrix products, arithmetic and copies ran while one was open for 0% -> 0% of each run, Pallas kernels for 7% -> 7%
where the time goes in v7:
time: 23.3 us; the launch traced here: 23.1 us
  starting transfers between devices  15.3 us (66%)
  Pallas kernels  4.45 us (19%)
  waiting for transfers between devices  3.3 us (14%)
    ppermute x1, starting transfers between devices, local(): lax.ppermute(widened(False, lon_near, 0, 1000), 'lon', pair_far_closed('l...  5.58 us
    ppermute x1, starting transfers between devices, local(): lon_far = lax.ppermute(to_far, 'lon', pair_far_closed('lon'))  3.54 us
    ppermute x1, starting transfers between devices, local(): lon_near = lax.ppermute(to_near, 'lon', pair_near('lon'))  3.03 us
    ppermute x1, waiting for transfers between devices, local(): lax.ppermute(widened(True, lon_far, 0, 8000), 'lon', pair_near('lon'))  2.12 us
    pallas_call x1, Pallas kernels, local(): pl.pallas_call(coarse_kernel, out_shape=blocks(len(stencil_offsets)), in_...  1.71 us
    ppermute x1, starting transfers between devices, local(): lat_near = lax.ppermute(both, 'lat', pair_near('lat'))  1.6 us
    ppermute x2, starting transfers between devices, exchange_lat_far(): return lax.ppermute(values, ('lon', 'lat'), pairs)  1.39 us
    pallas_call x1, Pallas kernels, local(): pl.pallas_call(close_kernel, out_shape=(*(blocks(len(cells)) for cells in...  1.33 us
  transfers between devices with their start and end apart: 8, of which 3 were waited for; matrix products, arithmetic and copies ran while one was open for 0% of the time, Pallas kernels for 7%

profile of v7, /device:TPU:0, one launch (start us, length us, event | category | flops | bytes accessed | tf_op | source)
XLA Modules:
  0.0 23.1 jit_solution(6098222742554659290)
XLA Ops:
  0.0 1.0 %shard_map.73 = (f32[544,128]{1,0:T(8,128)S(1)}, f32[288,128]{1,0:T(8,128)S(1)}, f32[288,128]{1,0:T(8,128)S(1)}) custom-call(f32[2,2,128,128]{3,2,1,0:T(8,128)} %inverse_hbm.1, f32[2,2,128]{2,1,0:T(2,128)} %diag_hbm.1, f32[2,2,128]{2,1,0:T(2,128)} %coup_hbm.1, f32[2,2,128]{2,1,0:T(2,128)} %east_hbm.1, f32[2,2,128]{2,1,0:T(2,128)} %north_hbm.1, ...), custom_call_target="tpu_custom_call" | custom-call | tf_op jit(solution)/shard_map/pallas_call | solution.py:533
  1.1 3.0 %collective-permute-start = (f32[288,128]{1,0:T(8,128)S(1)}, f32[288,128]{1,0:T(8,128)S(1)}, u32[]{:S(2)}, u32[]{:S(2)}) collective-permute-start(f32[288,128]{1,0:T(8,128)S(1)} %get-tuple-element.16), channel_id=1, source_target_pairs={{0,4},{4,0},{8,12},{12,8},{16,20},{20,16},{24,28},{28,24},{1,5},{5... | collective-permute-start | bytes 442376 | tf_op jit(solution)/shard_map/ppermute | solution.py:543
  4.1 3.5 %collective-permute-start.1 = (f32[288,128]{1,0:T(8,128)S(1)}, f32[288,128]{1,0:T(8,128)S(1)}, u32[]{:S(2)}, u32[]{:S(2)}) collective-permute-start(f32[288,128]{1,0:T(8,128)S(1)} %get-tuple-element.17), channel_id=1, source_target_pairs={{0,28},{4,8},{8,4},{12,16},{16,12},{20,24},{24,20},{28,0},{1,29},{... | collective-permute-start | bytes 442376 | tf_op jit(solution)/shard_map/ppermute | solution.py:544
  7.6 0.0 collective-permute-start.5
  7.6 1.6 %collective-permute-start.4 = (f32[544,128]{1,0:T(8,128)S(1)}, f32[544,128]{1,0:T(8,128)S(1)}, u32[]{:S(2)}, u32[]{:S(2)}) collective-permute-start(f32[544,128]{1,0:T(8,128)S(1)} %get-tuple-element.15.own.refs_0_), channel_id=1, source_target_pairs={{0,1},{1,0},{2,3},{3,2},{4,5},{5,4},{6,7},{7,6},{8,9},{9,8},{10,11... | collective-permute-start | bytes 835592 | tf_op jit(solution)/shard_map/ppermute | solution.py:545
  9.2 1.1 %collective-permute-done.ring.lon_near.refs_1_ = f32[288,128]{1,0:T(8,128)S(1)} collective-permute-done((f32[288,128]{1,0:T(8,128)S(1)}, f32[288,128]{1,0:T(8,128)S(1)}, u32[]{:S(2)}, u32[]{:S(2)}) %collective-permute-start) | collective-permute-done | bytes 147488 | tf_op jit(solution)/shard_map/ppermute | solution.py:543
  10.4 5.6 %collective-permute-start.3 = (f32[272,128]{1,0:T(8,128)S(1)}, f32[272,128]{1,0:T(8,128)S(1)}, u32[]{:S(2)}, u32[]{:S(2)}) collective-permute-start(f32[272,128]{1,0:T(8,128)S(1)} %shard_map.75), channel_id=1, source_target_pairs={{0,28},{4,8},{8,4},{12,16},{16,12},{20,24},{24,20},{28,0},{1,29},{... | collective-permute-start | bytes 417800 | tf_op jit(solution)/shard_map/ppermute | solution.py:558
  16.0 0.0 collective-permute-done.1.ring.lon_far.refs_2_
  16.0 0.1 collective-permute-start.2
  16.1 0.0 collective-permute-done.5.lat_far.refs_6_
  16.1 0.0 collective-permute-done.4.lat_near.refs_5_
  16.1 1.4 %collective-permute-start.7 = (f32[296,128]{1,0:T(8,128)S(1)}, f32[296,128]{1,0:T(8,128)S(1)}, u32[]{:S(2)}, u32[]{:S(2)}) collective-permute-start(f32[296,128]{1,0:T(8,128)S(1)} %shard_map.77), channel_id=1, source_target_pairs={{0,8},{1,2},{2,1},{3,11},{4,12},{5,6},{6,5},{7,15},{8,0},{9,10},{1... | collective-permute-start | bytes 454664 | tf_op jit(solution)/shard_map/ppermute | solution.py:51
  17.5 1.3 %shard_map.76 = (f32[12,128,128]{2,1,0:T(8,128)S(1)}, f32[4,128,128]{2,1,0:T(8,128)S(1)}, f32[5,128,128]{2,1,0:T(8,128)S(1)}, f32[8,128,128]{2,1,0:T(8,128)S(1)}...) custom-call(f32[544,128]{1,0:T(8,128)S(1)} %get-tuple-element.15.own.refs_0_, ...), custom_call_target="tpu_custom_call" | custom-call | flops 1000000 | bytes 1000 | tf_op jit(solution)/shard_map/pallas_call | solution.py:570
  18.9 0.1 collective-permute-start.6
  18.9 0.1 collective-permute-done.3.wide_far.refs_4_
  19.0 2.1 %collective-permute-done.2.wide_near.refs_3_ = f32[272,128]{1,0:T(8,128)S(1)} collective-permute-done((f32[272,128]{1,0:T(8,128)S(1)}, f32[272,128]{1,0:T(8,128)S(1)}, u32[]{:S(2)}, u32[]{:S(2)}) %collective-permute-start.2) | collective-permute-done | bytes 139296 | tf_op jit(solution)/shard_map/ppermute | solution.py:559
  21.1 0.3 %shard_map.78.refs_15_ = f32[4,128,128]{2,1,0:T(8,128)S(1)} custom-call(f32[544,128]{1,0:T(8,128)S(1)} %get-tuple-element.15.own.refs_0_, f32[288,128]{1,0:T(8,128)S(1)} %collective-permute-done.ring.lon_near.refs_1_, f32[288,128]{1,0:T(8,128)S(1)} %collective-permute-done.1.ring.lon_far.refs_2_, f32[272,128]{1,0:T(8,128)S(1)} %collective-permute-done.2.wide_near.refs_3_, ...), custom_call_target="tpu_custom_call" | custom-call | flops 49999998976 | bytes 50000000 | tf_op jit(solution)/shard_map/pallas_call | solution.py:584
  21.4 0.0 collective-permute-done.7.refs_8_
  21.4 0.0 collective-permute-done.6.refs_7_
  21.4 1.7 %shard_map.79 = f32[13,128,128]{2,1,0:T(8,128)} custom-call(f32[544,128]{1,0:T(8,128)S(1)} %get-tuple-element.15.own.refs_0_, f32[288,128]{1,0:T(8,128)S(1)} %collective-permute-done.ring.lon_near.refs_1_, f32[288,128]{1,0:T(8,128)S(1)} %collective-permute-done.1.ring.lon_far.refs_2_, f32[272,128]{1,0:T(8,128)S(1)} %collective-permute-done.2.wide_near.refs_3_, ...), custom_call_target="tpu_custom_call" | custom-call | tf_op jit(solution)/shard_map/pallas_call | solution.py:592
  (3 shorter events, 0.1 us)
Async XLA Ops:
  1.1 9.3 %collective-permute-start = (f32[288,128]{1,0:T(8,128)S(1)}, f32[288,128]{1,0:T(8,128)S(1)}, u32[]{:S(2)}, u32[]{:S(2)}) collective-permute-start(f32[288,128]{1,0:T(8,128)S(1)} %get-tuple-element.16), channel_id=1, source_target_pairs={{0,4},{4,0},{8,12},{12,8},{16,20},{20,16},{24,28},{28,24},{1,5},{5... | collective-permute-start | bytes 442376 | tf_op jit(solution)/shard_map/ppermute | solution.py:543
  4.1 11.9 %collective-permute-start.1 = (f32[288,128]{1,0:T(8,128)S(1)}, f32[288,128]{1,0:T(8,128)S(1)}, u32[]{:S(2)}, u32[]{:S(2)}) collective-permute-start(f32[288,128]{1,0:T(8,128)S(1)} %get-tuple-element.17), channel_id=1, source_target_pairs={{0,28},{4,8},{8,4},{12,16},{16,12},{20,24},{24,20},{28,0},{1,29},{... | collective-permute-start | bytes 442376 | tf_op jit(solution)/shard_map/ppermute | solution.py:544
  7.6 8.4 %collective-permute-start.5 = (f32[544,128]{1,0:T(8,128)S(1)}, f32[544,128]{1,0:T(8,128)S(1)}, u32[]{:S(2)}, u32[]{:S(2)}) collective-permute-start(f32[544,128]{1,0:T(8,128)S(1)} %get-tuple-element.15.own.refs_0_), channel_id=1, source_target_pairs={{0,8},{1,2},{2,1},{3,11},{4,12},{5,6},{6,5},{7,15},{8,0},{9,10},{1... | collective-permute-start | bytes 835592 | tf_op jit(solution)/shard_map/ppermute | solution.py:51
  7.6 8.5 %collective-permute-start.4 = (f32[544,128]{1,0:T(8,128)S(1)}, f32[544,128]{1,0:T(8,128)S(1)}, u32[]{:S(2)}, u32[]{:S(2)}) collective-permute-start(f32[544,128]{1,0:T(8,128)S(1)} %get-tuple-element.15.own.refs_0_), channel_id=1, source_target_pairs={{0,1},{1,0},{2,3},{3,2},{4,5},{5,4},{6,7},{7,6},{8,9},{9,8},{10,11... | collective-permute-start | bytes 835592 | tf_op jit(solution)/shard_map/ppermute | solution.py:545
  10.4 8.6 %collective-permute-start.3 = (f32[272,128]{1,0:T(8,128)S(1)}, f32[272,128]{1,0:T(8,128)S(1)}, u32[]{:S(2)}, u32[]{:S(2)}) collective-permute-start(f32[272,128]{1,0:T(8,128)S(1)} %shard_map.75), channel_id=1, source_target_pairs={{0,28},{4,8},{8,4},{12,16},{16,12},{20,24},{24,20},{28,0},{1,29},{... | collective-permute-start | bytes 417800 | tf_op jit(solution)/shard_map/ppermute | solution.py:558
  16.0 5.1 %collective-permute-start.2 = (f32[272,128]{1,0:T(8,128)S(1)}, f32[272,128]{1,0:T(8,128)S(1)}, u32[]{:S(2)}, u32[]{:S(2)}) collective-permute-start(f32[272,128]{1,0:T(8,128)S(1)} %shard_map.74), channel_id=1, source_target_pairs={{0,4},{4,0},{8,12},{12,8},{16,20},{20,16},{24,28},{28,24},{1,5},{5... | collective-permute-start | bytes 417800 | tf_op jit(solution)/shard_map/ppermute | solution.py:559
  16.1 5.3 %collective-permute-start.7 = (f32[296,128]{1,0:T(8,128)S(1)}, f32[296,128]{1,0:T(8,128)S(1)}, u32[]{:S(2)}, u32[]{:S(2)}) collective-permute-start(f32[296,128]{1,0:T(8,128)S(1)} %shard_map.77), channel_id=1, source_target_pairs={{0,8},{1,2},{2,1},{3,11},{4,12},{5,6},{6,5},{7,15},{8,0},{9,10},{1... | collective-permute-start | bytes 454664 | tf_op jit(solution)/shard_map/ppermute | solution.py:51
  18.9 2.6 %collective-permute-start.6 = (f32[296,128]{1,0:T(8,128)S(1)}, f32[296,128]{1,0:T(8,128)S(1)}, u32[]{:S(2)}, u32[]{:S(2)}) collective-permute-start(f32[296,128]{1,0:T(8,128)S(1)} %get-tuple-element.18), channel_id=1, source_target_pairs={{0,1},{1,0},{2,3},{3,2},{4,5},{5,4},{6,7},{7,6},{8,9},{9,8},{10,11... | collective-permute-start | bytes 454664 | tf_op jit(solution)/shard_map/ppermute | solution.py:582

commit v8 on v7

--- a/solution.py
+++ b/solution.py
@@ -469,16 +469,6 @@
         smooth_of[cell] = lon_smooth.at[place]
     for place, cell in enumerate(lat_far_cells):
         smooth_of[cell] = lat_smooth.at[place]
-    for place, (x, y) in enumerate(product_cells):
-        if (x, y) in near_cells:
-            known = near_cells.index((x, y))
-            rest = rest_in[known] + rows_t[x, y] * cells.outer_face(x, y)
-            smooths[place] = product_of_parts(rest, high_in[known], low_in[known])
-        else:
-            rest = cells.residual(rows_t, x, y)
-            smooths[place] = product(rest, cells.inverse(x, y))
-        rests[place] = rest
-        rest_of[x, y], smooth_of[x, y] = rests.at[place], smooths.at[place]
     lateral, own = {}, {}
     for device, members in groups.items():
         for x, y in members:
@@ -495,7 +485,18 @@
     slots = {target: place for place, target in enumerate(stencil_offsets)}
     copies = []
     strip = levels // 4
-    for target in target_order:
+    for turn, target in enumerate(target_order):
+        if turn == 4:
+            for place, (x, y) in enumerate(product_cells):
+                if (x, y) in near_cells:
+                    known = near_cells.index((x, y))
+                    rest = rest_in[known] + rows_t[x, y] * cells.outer_face(x, y)
+                    smooths[place] = product_of_parts(rest, high_in[known], low_in[known])
+                else:
+                    rest = cells.residual(rows_t, x, y)
+                    smooths[place] = product(rest, cells.inverse(x, y))
+                rests[place] = rest
+                rest_of[x, y], smooth_of[x, y] = rests.at[place], smooths.at[place]
         for start in range(0, levels, strip):
             rows = slice(start, start + strip)
             total = None

time: 23.3 us -> 23.3 us (level)
  no operation moved by 1% of the time
where the time goes in v8:
time: 23.3 us; the launch traced here: 23.2 us
  starting transfers between devices  15.3 us (66%)
  Pallas kernels  4.46 us (19%)
  waiting for transfers between devices  3.3 us (14%)
    ppermute x1, starting transfers between devices, local(): lax.ppermute(widened(False, lon_near, 0, 1000), 'lon', pair_far_closed('l...  5.58 us
    ppermute x1, starting transfers between devices, local(): lon_far = lax.ppermute(to_far, 'lon', pair_far_closed('lon'))  3.54 us
    ppermute x1, starting transfers between devices, local(): lon_near = lax.ppermute(to_near, 'lon', pair_near('lon'))  3.03 us
    ppermute x1, waiting for transfers between devices, local(): lax.ppermute(widened(True, lon_far, 0, 8000), 'lon', pair_near('lon'))  2.12 us
    pallas_call x1, Pallas kernels, local(): pl.pallas_call(coarse_kernel, out_shape=blocks(len(stencil_offsets)), in_...  1.73 us
    ppermute x1, starting transfers between devices, local(): lat_near = lax.ppermute(both, 'lat', pair_near('lat'))  1.6 us
    ppermute x2, starting transfers between devices, exchange_lat_far(): return lax.ppermute(values, ('lon', 'lat'), pairs)  1.39 us
    pallas_call x1, Pallas kernels, local(): pl.pallas_call(close_kernel, out_shape=(*(blocks(len(cells)) for cells in...  1.33 us
  transfers between devices with their start and end apart: 8, of which 3 were waited for; matrix products, arithmetic and copies ran while one was open for 0% of the time, Pallas kernels for 7%

profile of v8, /device:TPU:0, one launch (start us, length us, event | category | flops | bytes accessed | tf_op | source)
XLA Modules:
  0.0 23.2 jit_solution(15640581241287554675)
XLA Ops:
  0.0 1.0 %shard_map.73 = (f32[544,128]{1,0:T(8,128)S(1)}, f32[288,128]{1,0:T(8,128)S(1)}, f32[288,128]{1,0:T(8,128)S(1)}) custom-call(f32[2,2,128,128]{3,2,1,0:T(8,128)} %inverse_hbm.1, f32[2,2,128]{2,1,0:T(2,128)} %diag_hbm.1, f32[2,2,128]{2,1,0:T(2,128)} %coup_hbm.1, f32[2,2,128]{2,1,0:T(2,128)} %east_hbm.1, f32[2,2,128]{2,1,0:T(2,128)} %north_hbm.1, ...), custom_call_target="tpu_custom_call" | custom-call | tf_op jit(solution)/shard_map/pallas_call | solution.py:534
  1.1 3.0 %collective-permute-start = (f32[288,128]{1,0:T(8,128)S(1)}, f32[288,128]{1,0:T(8,128)S(1)}, u32[]{:S(2)}, u32[]{:S(2)}) collective-permute-start(f32[288,128]{1,0:T(8,128)S(1)} %get-tuple-element.16), channel_id=1, source_target_pairs={{0,4},{4,0},{8,12},{12,8},{16,20},{20,16},{24,28},{28,24},{1,5},{5... | collective-permute-start | bytes 442376 | tf_op jit(solution)/shard_map/ppermute | solution.py:544
  4.1 3.5 %collective-permute-start.1 = (f32[288,128]{1,0:T(8,128)S(1)}, f32[288,128]{1,0:T(8,128)S(1)}, u32[]{:S(2)}, u32[]{:S(2)}) collective-permute-start(f32[288,128]{1,0:T(8,128)S(1)} %get-tuple-element.17), channel_id=1, source_target_pairs={{0,28},{4,8},{8,4},{12,16},{16,12},{20,24},{24,20},{28,0},{1,29},{... | collective-permute-start | bytes 442376 | tf_op jit(solution)/shard_map/ppermute | solution.py:545
  7.6 0.0 collective-permute-start.5
  7.6 1.6 %collective-permute-start.4 = (f32[544,128]{1,0:T(8,128)S(1)}, f32[544,128]{1,0:T(8,128)S(1)}, u32[]{:S(2)}, u32[]{:S(2)}) collective-permute-start(f32[544,128]{1,0:T(8,128)S(1)} %get-tuple-element.15.own.refs_0_), channel_id=1, source_target_pairs={{0,1},{1,0},{2,3},{3,2},{4,5},{5,4},{6,7},{7,6},{8,9},{9,8},{10,11... | collective-permute-start | bytes 835592 | tf_op jit(solution)/shard_map/ppermute | solution.py:546
  9.2 1.1 %collective-permute-done.ring.lon_near.refs_1_ = f32[288,128]{1,0:T(8,128)S(1)} collective-permute-done((f32[288,128]{1,0:T(8,128)S(1)}, f32[288,128]{1,0:T(8,128)S(1)}, u32[]{:S(2)}, u32[]{:S(2)}) %collective-permute-start) | collective-permute-done | bytes 147488 | tf_op jit(solution)/shard_map/ppermute | solution.py:544
  10.4 5.6 %collective-permute-start.3 = (f32[272,128]{1,0:T(8,128)S(1)}, f32[272,128]{1,0:T(8,128)S(1)}, u32[]{:S(2)}, u32[]{:S(2)}) collective-permute-start(f32[272,128]{1,0:T(8,128)S(1)} %shard_map.75), channel_id=1, source_target_pairs={{0,28},{4,8},{8,4},{12,16},{16,12},{20,24},{24,20},{28,0},{1,29},{... | collective-permute-start | bytes 417800 | tf_op jit(solution)/shard_map/ppermute | solution.py:559
  16.0 0.0 collective-permute-done.1.ring.lon_far.refs_2_
  16.0 0.1 collective-permute-start.2
  16.1 0.0 collective-permute-done.5.lat_far.refs_6_
  16.1 0.0 collective-permute-done.4.lat_near.refs_5_
  16.1 1.4 %collective-permute-start.7 = (f32[296,128]{1,0:T(8,128)S(1)}, f32[296,128]{1,0:T(8,128)S(1)}, u32[]{:S(2)}, u32[]{:S(2)}) collective-permute-start(f32[296,128]{1,0:T(8,128)S(1)} %shard_map.77), channel_id=1, source_target_pairs={{0,8},{1,2},{2,1},{3,11},{4,12},{5,6},{6,5},{7,15},{8,0},{9,10},{1... | collective-permute-start | bytes 454664 | tf_op jit(solution)/shard_map/ppermute | solution.py:51
  17.5 1.3 %shard_map.76 = (f32[12,128,128]{2,1,0:T(8,128)S(1)}, f32[4,128,128]{2,1,0:T(8,128)S(1)}, f32[5,128,128]{2,1,0:T(8,128)S(1)}, f32[8,128,128]{2,1,0:T(8,128)S(1)}...) custom-call(f32[544,128]{1,0:T(8,128)S(1)} %get-tuple-element.15.own.refs_0_, ...), custom_call_target="tpu_custom_call" | custom-call | flops 1000000 | bytes 1000 | tf_op jit(solution)/shard_map/pallas_call | solution.py:571
  18.9 0.1 collective-permute-start.6
  18.9 0.1 collective-permute-done.3.wide_far.refs_4_
  19.0 2.1 %collective-permute-done.2.wide_near.refs_3_ = f32[272,128]{1,0:T(8,128)S(1)} collective-permute-done((f32[272,128]{1,0:T(8,128)S(1)}, f32[272,128]{1,0:T(8,128)S(1)}, u32[]{:S(2)}, u32[]{:S(2)}) %collective-permute-start.2) | collective-permute-done | bytes 139296 | tf_op jit(solution)/shard_map/ppermute | solution.py:560
  21.1 0.3 %shard_map.78.refs_15_ = f32[4,128,128]{2,1,0:T(8,128)S(1)} custom-call(f32[544,128]{1,0:T(8,128)S(1)} %get-tuple-element.15.own.refs_0_, f32[288,128]{1,0:T(8,128)S(1)} %collective-permute-done.ring.lon_near.refs_1_, f32[288,128]{1,0:T(8,128)S(1)} %collective-permute-done.1.ring.lon_far.refs_2_, f32[272,128]{1,0:T(8,128)S(1)} %collective-permute-done.2.wide_near.refs_3_, ...), custom_call_target="tpu_custom_call" | custom-call | flops 49999998976 | bytes 50000000 | tf_op jit(solution)/shard_map/pallas_call | solution.py:585
  21.4 0.0 collective-permute-done.7.refs_8_
  21.4 0.0 collective-permute-done.6.refs_7_
  21.4 1.7 %shard_map.79 = f32[13,128,128]{2,1,0:T(8,128)} custom-call(f32[544,128]{1,0:T(8,128)S(1)} %get-tuple-element.15.own.refs_0_, f32[288,128]{1,0:T(8,128)S(1)} %collective-permute-done.ring.lon_near.refs_1_, f32[288,128]{1,0:T(8,128)S(1)} %collective-permute-done.1.ring.lon_far.refs_2_, f32[272,128]{1,0:T(8,128)S(1)} %collective-permute-done.2.wide_near.refs_3_, ...), custom_call_target="tpu_custom_call" | custom-call | tf_op jit(solution)/shard_map/pallas_call | solution.py:593
  (3 shorter events, 0.1 us)
Async XLA Ops:
  1.1 9.3 %collective-permute-start = (f32[288,128]{1,0:T(8,128)S(1)}, f32[288,128]{1,0:T(8,128)S(1)}, u32[]{:S(2)}, u32[]{:S(2)}) collective-permute-start(f32[288,128]{1,0:T(8,128)S(1)} %get-tuple-element.16), channel_id=1, source_target_pairs={{0,4},{4,0},{8,12},{12,8},{16,20},{20,16},{24,28},{28,24},{1,5},{5... | collective-permute-start | bytes 442376 | tf_op jit(solution)/shard_map/ppermute | solution.py:544
  4.1 11.9 %collective-permute-start.1 = (f32[288,128]{1,0:T(8,128)S(1)}, f32[288,128]{1,0:T(8,128)S(1)}, u32[]{:S(2)}, u32[]{:S(2)}) collective-permute-start(f32[288,128]{1,0:T(8,128)S(1)} %get-tuple-element.17), channel_id=1, source_target_pairs={{0,28},{4,8},{8,4},{12,16},{16,12},{20,24},{24,20},{28,0},{1,29},{... | collective-permute-start | bytes 442376 | tf_op jit(solution)/shard_map/ppermute | solution.py:545
  7.6 8.4 %collective-permute-start.5 = (f32[544,128]{1,0:T(8,128)S(1)}, f32[544,128]{1,0:T(8,128)S(1)}, u32[]{:S(2)}, u32[]{:S(2)}) collective-permute-start(f32[544,128]{1,0:T(8,128)S(1)} %get-tuple-element.15.own.refs_0_), channel_id=1, source_target_pairs={{0,8},{1,2},{2,1},{3,11},{4,12},{5,6},{6,5},{7,15},{8,0},{9,10},{1... | collective-permute-start | bytes 835592 | tf_op jit(solution)/shard_map/ppermute | solution.py:51
  7.6 8.5 %collective-permute-start.4 = (f32[544,128]{1,0:T(8,128)S(1)}, f32[544,128]{1,0:T(8,128)S(1)}, u32[]{:S(2)}, u32[]{:S(2)}) collective-permute-start(f32[544,128]{1,0:T(8,128)S(1)} %get-tuple-element.15.own.refs_0_), channel_id=1, source_target_pairs={{0,1},{1,0},{2,3},{3,2},{4,5},{5,4},{6,7},{7,6},{8,9},{9,8},{10,11... | collective-permute-start | bytes 835592 | tf_op jit(solution)/shard_map/ppermute | solution.py:546
  10.4 8.6 %collective-permute-start.3 = (f32[272,128]{1,0:T(8,128)S(1)}, f32[272,128]{1,0:T(8,128)S(1)}, u32[]{:S(2)}, u32[]{:S(2)}) collective-permute-start(f32[272,128]{1,0:T(8,128)S(1)} %shard_map.75), channel_id=1, source_target_pairs={{0,28},{4,8},{8,4},{12,16},{16,12},{20,24},{24,20},{28,0},{1,29},{... | collective-permute-start | bytes 417800 | tf_op jit(solution)/shard_map/ppermute | solution.py:559
  16.0 5.1 %collective-permute-start.2 = (f32[272,128]{1,0:T(8,128)S(1)}, f32[272,128]{1,0:T(8,128)S(1)}, u32[]{:S(2)}, u32[]{:S(2)}) collective-permute-start(f32[272,128]{1,0:T(8,128)S(1)} %shard_map.74), channel_id=1, source_target_pairs={{0,4},{4,0},{8,12},{12,8},{16,20},{20,16},{24,28},{28,24},{1,5},{5... | collective-permute-start | bytes 417800 | tf_op jit(solution)/shard_map/ppermute | solution.py:560
  16.1 5.3 %collective-permute-start.7 = (f32[296,128]{1,0:T(8,128)S(1)}, f32[296,128]{1,0:T(8,128)S(1)}, u32[]{:S(2)}, u32[]{:S(2)}) collective-permute-start(f32[296,128]{1,0:T(8,128)S(1)} %shard_map.77), channel_id=1, source_target_pairs={{0,8},{1,2},{2,1},{3,11},{4,12},{5,6},{6,5},{7,15},{8,0},{9,10},{1... | collective-permute-start | bytes 454664 | tf_op jit(solution)/shard_map/ppermute | solution.py:51
  18.9 2.6 %collective-permute-start.6 = (f32[296,128]{1,0:T(8,128)S(1)}, f32[296,128]{1,0:T(8,128)S(1)}, u32[]{:S(2)}, u32[]{:S(2)}) collective-permute-start(f32[296,128]{1,0:T(8,128)S(1)} %get-tuple-element.18), channel_id=1, source_target_pairs={{0,1},{1,0},{2,3},{3,2},{4,5},{5,4},{6,7},{7,6},{8,9},{9,8},{10,11... | collective-permute-start | bytes 454664 | tf_op jit(solution)/shard_map/ppermute | solution.py:583
